TPU v7x, 256 devices: a whole 4x4x8 slice. The times are simulated.
256 devices in a mesh: gz: 32 (over z, x_lo, core), gy: 8 (over y, x_hi).
Axes of the slice: x: 4 (x_hi: 2, x_lo: 2; x = x_hi * 2 + x_lo), y: 4, z: 8, core: 2. Of those that a mesh axis runs over, the one named last changes fastest.
Arguments:
- vorticity: float32 [512, 512, 512], P('gz', 'gy'), may hold values from -12 to 12
- keep_one: int32 [7, 256, 256, 256], P(None, 'gz', 'gy'), may hold values 0 or 1
- keep_two: int32 [7, 128, 128, 128], P(None, 'gz', 'gy'), may hold values 0 or 1
- keep_three: int32 [7, 64, 64, 64], P(None, 'gz', 'gy'), may hold values 0 or 1
- keep_four: int32 [7, 32, 32, 32], P(None, 'gz', 'gy'), may hold values 0 or 1
- keep_coarse: int32 [32, 32, 32], P('gz', 'gy'), may hold values 0 or 1
Outputs:
- coherent: float32 [512, 512, 512], P('gz', 'gy')
All inputs are finite; a program needn't handle non-finite values. No bound on the sum of `keep_one` or of `keep_two` or of `keep_three` or of `keep_four` or of `keep_coarse` on one device may be relied on, other than what follows from the above.
Results may differ from a plain program's by a relative error of at most 0.00017.
Values sent between devices are 32-bit elements; how exact they have to be, the bound alone decides.
No kernel may reach another device: no remote copies, remote signals or barrier semaphores. Data moves between devices by JAX's collectives and lax.ppermute only.
A program may use at most 128 MiB of HBM per device.

v0:
```python
import functools

import jax
import jax.numpy as jnp
import ml_dtypes
import numpy as np
from jax import lax
from jax.experimental import pallas as pl
from jax.experimental.pallas import tpu as pltpu
from jax.sharding import PartitionSpec as P

low_taps = (
    0.11154074335008017,
    0.4946238903983854,
    0.7511339080215775,
    0.3152503517092432,
    -0.22626469396516913,
    -0.12976686756709563,
    0.09750160558707936,
    0.02752286553001629,
    -0.031582039318031156,
    0.0005538422009938016,
    0.004777257511010651,
    -0.00107730108499558,
)
high_taps = tuple(((-1.0) ** k * low_taps[11 - k] for k in range(12)))

GZ, GY = 32, 8
MEMBERS = 4
F32, BF16 = jnp.float32, jnp.bfloat16


def tail_of(s):
    return (s + 11) // 2


def band(taps, n, s):
    t = tail_of(s)
    out = np.zeros((t + n // 2, s + n))
    for row in range(t + n // 2):
        for col in range(s + n):
            k = (col - s) - 2 * (row - t)
            if 0 <= k < 12:
                out[row, col] = taps[k]
    return out


def periodic(taps, n):
    out = np.zeros((n // 2, n))
    for i in range(n // 2):
        for k in range(12):
            out[i, (2 * i + k) % n] += taps[k]
    return out


def rank_five():
    block = np.concatenate([band(low_taps, 10, 0)[:5], band(high_taps, 10, 0)[:5]])
    u, sing, vt = np.linalg.svd(block)
    return u[:, :5] * sing[:5], vt[:5]


def pair(matrix):
    high = matrix.astype(ml_dtypes.bfloat16)
    low = (matrix - high.astype(np.float64)).astype(ml_dtypes.bfloat16)
    return np.stack([high, low])


def padded(matrix, rows, cols):
    out = np.zeros((rows, cols))
    out[: matrix.shape[0], : matrix.shape[1]] = matrix
    return out


@functools.lru_cache(None)
def tables():
    spread, basis = rank_five()
    mats = {}
    x1 = np.concatenate([periodic(low_taps, 512), periodic(high_taps, 512)])
    mats["x1f"], mats["x1i"], mats["x1l"] = x1.T, x1, x1[:256]
    lo2 = periodic(low_taps, 256)
    lo3 = periodic(low_taps, 128) @ lo2
    xm = np.concatenate(
        [
            lo2,
            periodic(high_taps, 256),
            lo3,
            periodic(high_taps, 128) @ lo2,
            periodic(low_taps, 64) @ lo3,
            periodic(high_taps, 64) @ lo3,
            np.zeros((64, 256)),
        ]
    )
    mats["xmf"], mats["xmi"] = xm.T, xm
    y1 = np.concatenate([band(low_taps, 64, 0)[5:], band(high_taps, 64, 0)[5:]])
    mats["y1f"] = np.kron(np.eye(4), y1)
    mats["y1i"] = mats["y1f"].T
    pick = padded(basis, 5, 64)
    mats["y1q"] = padded(np.kron(np.eye(8), pick), 48, 512)
    mats["y1qt"] = mats["y1q"].T
    put = np.zeros((64, 5))
    put[27:32], put[59:64] = spread[:5], spread[5:]
    mats["y1u"] = padded(np.kron(np.eye(8), put), 512, 48)
    mats["y1ut"] = mats["y1u"].T
    mats["y1l"] = np.kron(np.eye(4), y1[:32])
    mats["y1lt"] = mats["y1l"].T
    mats["y1ul"] = padded(np.kron(np.eye(8), put[:32]), 256, 48)
    mats["y1ult"] = mats["y1ul"].T
    corner = np.kron(np.eye(5), padded(pick, 8, 64))
    lows, highs = np.kron(np.eye(5), y1[:32]), np.kron(np.eye(5), y1[32:])
    mats["r5f"] = np.concatenate([lows, corner, highs])
    mats["r5i"] = np.kron(np.eye(5), y1.T)
    mats["r5u"] = np.kron(np.eye(5), padded(put, 64, 8))
    mats["r5ut"] = mats["r5u"].T
    mats["r5ul"] = np.kron(np.eye(5), padded(put[:32], 32, 8))
    mats["r5ult"] = mats["r5ul"].T
    far = np.zeros((2, 48, 40))
    for z in range(10):
        for k in range(5):
            far[z // 8, (z % 8) * 5 + k, k::8] = basis[:, z]
    mats["r5z"] = far.reshape(96, 40)
    z1 = np.concatenate([band(low_taps, 16, 0)[5:], band(high_taps, 16, 0)[5:]])
    mats["z1f"] = np.kron(z1, np.eye(16))
    mats["z1i"] = mats["z1f"].T
    zput = np.zeros((16, 5))
    zput[3:8], zput[11:16] = spread[:5], spread[5:]
    mats["z1u"] = np.kron(zput, np.eye(16))
    zpick = padded(basis, 5, 16)
    mats["z1qt"] = np.kron(zpick.T, np.eye(16))
    lo_a = band(low_taps, 32, 0)
    lo_b = band(low_taps, 16, 5) @ lo_a
    lev2 = [lo_a, band(high_taps, 32, 0)]
    lev3 = [lo_b, band(high_taps, 16, 5) @ lo_a]
    lev4 = [band(low_taps, 8, 8) @ lo_b, band(high_taps, 8, 8) @ lo_b]

    def row2(b, i):
        return lev2[b][i + 5]

    def row3(b, i):
        return lev3[b][i + 8]

    def row4(b, i):
        return lev4[b][i + 9]

    pick32 = padded(basis, 5, 32)
    put2 = np.zeros((2, 16, 5))
    put2[0, 11:], put2[1, 11:] = spread[:5], spread[5:]

    y2 = np.zeros((256, 256))
    y2u = np.zeros((256, 64))
    y34 = np.zeros((592, 512))
    y2q = np.kron(np.eye(8), padded(pick32, 8, 32))
    for m in range(4):
        for z in range(8):
            cells = slice(z * 32, z * 32 + 32)
            cells4 = slice(256 + z * 32, 256 + z * 32 + 32)
            for r in range(8):
                row = (m * 8 + z) * 8 + r
                y2[row, cells] = row2(r // 4, 4 * m + r % 4)
                y2u[row, z * 8 : z * 8 + 5] = put2[r // 4, 4 * m + r % 4]
                if r < 4:
                    y34[row, cells] = row3(r // 2, 2 * m + r % 2)
                    y34[256 + row, cells] = row3(r // 2, 2 * m + r % 2 - 8)
                elif r < 6:
                    y34[row, cells4] = row4(r - 4, m)
                    y34[256 + row, cells4] = row4(r - 4, m - 4)
    y34p = np.zeros((256, 80))
    for z in range(8):
        cells4 = slice(256 + z * 32, 256 + z * 32 + 32)
        for by in range(2):
            for i in range(4):
                y34[512 + z * 8 + by * 4 + i, cells4] = row4(by, i - 8)
                y34p[(i * 8 + z) * 8 + 4 + by, z * 8 + by * 4 + i] = 1.0
            y34[576 + z * 2 + by, cells4] = row4(by, -9)
            y34p[(3 * 8 + z) * 8 + 4 + by, 64 + z * 2 + by] = 1.0
    mats["y2"], mats["y2t"] = y2, y2.T
    mats["y2u"], mats["y2ut"] = y2u, y2u.T
    mats["y2q"], mats["y2qt"] = y2q, y2q.T
    mats["y34"], mats["y34t"] = y34, y34.T
    mats["y34p"], mats["y34pt"] = y34p, y34p.T

    eye8 = np.eye(8)
    z2 = np.kron(np.array([row2(b, i) for b in range(2) for i in range(16)]), eye8)
    z2q = padded(np.kron(pick32, eye8), 48, 256)
    z2u = padded(np.kron(put2.reshape(32, 5), eye8), 256, 48)
    z34 = np.zeros((288, 32, 8))
    z34p = np.zeros((128, 32))
    for b in range(2):
        for i in range(8):
            for r in range(4):
                z34[(b * 8 + i) * 8 + r, :, r] = row3(b, i)
                z34[128 + (b * 8 + i) * 8 + r, :, r] = row3(b, i - 8)
        for by in range(2):
            for i in range(4):
                slot = b * 4 + i
                z34[slot * 8 + 4 + by, :, 4 + by] = row4(b, i)
                z34[128 + slot * 8 + 4 + by, :, 4 + by] = row4(b, i - 4)
                z34[256 + slot * 2 + by, :, 4 + by] = row4(b, i - 8)
                z34p[slot * 8 + 4 + by, slot * 2 + by] = 1.0
            z34[272 + b * 2 + by, :, 4 + by] = row4(b, -9)
            z34p[(b * 4 + 3) * 8 + 4 + by, 16 + b * 2 + by] = 1.0
    z34 = z34.reshape(288, 256)
    mats["z2"], mats["z2t"] = z2, z2.T
    mats["z2q"], mats["z2qt"] = z2q, z2q.T
    mats["z2u"], mats["z2ut"] = z2u, z2u.T
    mats["z34"], mats["z34t"] = z34, z34.T
    mats["z34p"], mats["z34pt"] = z34p, z34p.T
    return mats


SPREAD, BASIS = rank_five()
Z1LO = band(low_taps, 16, 0)[5:]


def packed(shelves):
    mats = tables()
    places, rows, width = {}, 0, 0
    for shelf in shelves:
        col = tall = 0
        for name in shelf:
            height, wide = mats[name].shape
            places[name] = (rows, height, col, wide)
            col += -(-wide // 128) * 128
            tall = max(tall, -(-height // 16) * 16)
        rows, width = rows + tall, max(width, col)
    out = np.zeros((rows, width))
    for name, (row, height, col, wide) in places.items():
        out[row : row + height, col : col + wide] = mats[name]
    return pair(out), places


class Tables:
    def __init__(self, ref, places):
        self.ref, self.places = ref, places

    def __call__(self, name):
        row, height, col, wide = self.places[name]
        return [self.ref[k, row : row + height, col : col + wide] for k in range(2)]


SPREAD, BASIS = rank_five()
Z1LO = band(low_taps, 16, 0)[5:]


def halves(value):
    high = value.astype(BF16)
    return high, (value - high.astype(F32)).astype(BF16)


def dot(a, b):
    return lax.dot_general(a, b, (((1,), (0,)), ((), ())), preferred_element_type=F32)


def left(table, value):
    vh, vl = halves(value)
    return dot(table[0], vh) + dot(table[0], vl) + dot(table[1], vh)


def right(value, table):
    vh, vl = halves(value)
    return dot(vh, table[0]) + dot(vl, table[0]) + dot(vh, table[1])


def combine(weights, planes):
    total = None
    for weight, plane in zip(weights, planes):
        if weight == 0.0:
            continue
        term = float(weight) * plane()
        total = term if total is None else total + term
    return total


def taller(value, rows):
    return jnp.concatenate([value, jnp.zeros((rows, value.shape[1]), F32)], axis=0)


def call(kernel, micros, outs, *operands, shelves=None, index=None, scratch=(), streamed=None):
    spec, anywhere = pl.BlockSpec(memory_space=pltpu.VMEM), pl.BlockSpec(memory_space=pltpu.HBM)
    specs = [spec] * len(operands)
    out_specs = [spec] * len(outs)
    operands = list(operands)
    places = None
    scratch = [pltpu.VMEM(shape, F32) for shape in scratch]
    if index is not None:
        operands.append(index)
        specs.append(pl.BlockSpec(memory_space=pltpu.SMEM))
    if shelves is not None:
        table, places = packed(shelves)
        operands.append(jnp.asarray(table))
        specs.append(spec)
    if streamed == "in":
        specs[0] = specs[-1] = anywhere
        for at in (0, -1):
            operands[at] = pltpu.with_memory_space_constraint(operands[at], pltpu.HBM)
        scratch += [
            pltpu.VMEM(operands[0].shape, F32),
            pltpu.VMEM(operands[-1].shape, BF16),
            pltpu.SemaphoreType.DMA((6,)),
        ]
    if streamed == "out":
        out_specs = [anywhere] * len(outs)
        scratch += [pltpu.VMEM(outs[0], F32), pltpu.SemaphoreType.DMA((4,))]

    def body(*refs):
        refs = list(refs)
        count = len(operands)
        if streamed == "in":
            held, table_held, sems = refs[-3:]
            table_copies = []
            for k, (low, high) in enumerate(((0, 512), (512, table_held.shape[1]))):
                rows = pl.ds(low, high - low)
                table_copies.append(
                    pltpu.make_async_copy(
                        refs[count - 1].at[:, rows], table_held.at[:, rows], sems.at[4 + k]
                    )
                )
            chunks = []
            for c in range(4):
                rows = pl.ds(4 * c, 4)
                chunks.append(pltpu.make_async_copy(refs[0].at[rows], held.at[rows], sems.at[c]))
            chunks[0].start()
            table_copies[0].start()
            for copy in chunks[1:]:
                copy.start()
            table_copies[1].start()
            table_copies[0].wait()
            refs[0], refs[count - 1] = held, table_held
            refs = refs[:-3] + [chunks + table_copies[1:]]
        if streamed == "out":
            held, sems = refs[-2:]
            target = refs[count]
            chunks = []
            for c in range(4):
                rows = pl.ds(4 * c, 4)
                chunks.append(pltpu.make_async_copy(held.at[rows], target.at[rows], sems.at[c]))
            refs[count] = held
            refs = refs[:-2] + [chunks]
        if places is not None:
            refs[count - 1] = Tables(refs[count - 1], places)
        kernel(*refs)

    return pl.pallas_call(
        body,
        name=kernel.__name__,
        out_shape=[jax.ShapeDtypeStruct(shape, F32) for shape in outs],
        in_specs=specs,
        out_specs=out_specs,
        scratch_shapes=scratch,
        cost_estimate=pl.CostEstimate(
            flops=int(micros * 1.1e9), transcendentals=0, bytes_accessed=int(micros * 3.6e6)
        ),
        compiler_params=pltpu.CompilerParams(vmem_limit_bytes=24 * 2**20),
    )(*operands)


def member(index, by):
    return lax.rem(index[0] + by + MEMBERS, MEMBERS)


def block(index, by, rows=64):
    return pl.ds(pl.multiple_of(member(index, by) * rows, rows), rows)


def x_split(v, t, f, q, qz, qc, b, chunks):
    for c in range(4):
        chunks[c].wait()
        part = v[4 * c : 4 * c + 4].reshape(256, 512)
        f[4 * c : 4 * c + 4] = right(part, t("x1f")).reshape(4, 64, 512)
    for n in range(5):
        b[n] = combine(BASIS[n], [lambda j=j: f[j] for j in range(10)])
    chunks[4].wait()
    rim = left(t("r5f"), b[...].reshape(320, 512))
    qz[:, :32] = rim[:160].reshape(5, 32, 512)
    qc[...] = rim[160:200]
    qz[:, 32:] = rim[200:].reshape(5, 32, 512)
    for half in range(2):
        part = f[8 * half : 8 * half + 8].reshape(512, 512)
        q[half] = left(t("y1q"), part)[:40]


def deep_split(f, q, qz, qc, t, own, m1, m2, m3, g, low):
    for half in range(2):
        extra = left(t("y1ul"), taller(q[half, :, :256], 8))
        for c in range(2):
            z = 8 * half + 4 * c
            part = left(t("y1l"), f[z : z + 4, :, :256].reshape(256, 256))
            g[z : z + 4] = (part + extra[128 * c : 128 * c + 128]).reshape(4, 32, 256)
    rim = qz[:, :32, :256].reshape(160, 256) + left(t("r5ul"), qc[:, :256])
    rim = rim.reshape(5, 32, 256)
    for i in range(8):
        plane = combine(Z1LO[i], [lambda j=j: g[j] for j in range(16)])
        if i >= 3:
            plane = plane + combine(SPREAD[i - 3], [lambda n=n: rim[n] for n in range(5)])
        low[i] = plane
    wide = right(low[...].reshape(256, 256), t("xmf"))
    rim = left(t("y2q"), wide[:, :256])
    m1[256:320] = rim[:, :128]
    m1[320:384] = rim[:, 128:]
    rest = left(t("y34"), jnp.concatenate([wide[:, 256:384], wide[:, 384:]], axis=0))
    own[:, 256:] = rest[:256]
    m1[:256] = rest[256:512]
    m2[...] = rest[512:576]
    m3[...] = rest[576:592]
    own[:, :256] = left(t("y2"), wide[:, :256])


def y_gather(own, m1, m2, m3, index, t, p0, p1, p2, p3, w):
    rim = jnp.concatenate([m1[256:320], m1[320:384]], axis=1)
    w[:, :256] = own[:, :256] + left(t("y2u"), rim)
    far = jnp.concatenate([m2[...], m3[...]], axis=0)
    w[:, 256:] = own[:, 256:] + m1[:256] + left(t("y34p"), far)
    for s, piece in enumerate((p0, p1, p2, p3)):
        piece[...] = w[block(index, s)]


def z_split(p0, p1, p2, p3, index, t, own2, own34, n1, n2, n3, w):
    for s, piece in enumerate((p0, p1, p2, p3)):
        w[block(index, -s)] = piece[...]
    rim = left(t("z2q"), w[:, :256])
    n1[128:168] = rim[:40, :128]
    n1[168:208] = rim[:40, 128:]
    rest = left(t("z34"), w[:, 256:])
    own34[...] = rest[:128]
    n1[:128] = rest[128:256]
    n2[...] = rest[256:272]
    n3[...] = rest[272:280]
    own2[...] = left(t("z2"), w[:, :256])


def mask_pack(two, three, four, coarse, index, k0, k2, near, full):
    def plain(ref, b, z):
        if b == 0:
            return jnp.zeros(ref.shape[2:], F32)
        return ref[b - 1, z].astype(F32)

    for bz in range(2):
        for z in range(4):
            for bx in range(2):
                rows = [plain(two, 4 * bz + 2 * by + bx, z) for by in range(2)]
                at = bx * 64 + (bz * 4 + z) * 8
                for m in range(4):
                    full[m, at : at + 8] = jnp.concatenate(
                        [part[4 * m : 4 * m + 4] for part in rows], axis=0
                    )
        for z in range(2):
            rows = [
                jnp.concatenate([plain(three, 4 * bz + 2 * by + bx, z) for bx in range(2)], axis=1)
                for by in range(2)
            ]
            at = 128 + (bz * 2 + z) * 8
            for m in range(4):
                parts = [part[2 * m : 2 * m + 2] for part in rows]
                full[m, at : at + 8] = jnp.concatenate(parts + [jnp.zeros((4, 128), F32)], axis=0)
        rows = []
        for by in range(2):
            parts = [
                coarse[0].astype(F32) if bz + by + bx == 0 else plain(four, 4 * bz + 2 * by + bx, 0)
                for bx in range(2)
            ]
            rows.append(jnp.concatenate(parts + [jnp.zeros((4, 64), F32)], axis=1))
        at = 160 + bz * 8
        for m in range(4):
            parts = [jnp.zeros((4, 128), F32)] + [part[m : m + 1] for part in rows]
            full[m, at : at + 8] = jnp.concatenate(parts + [jnp.zeros((2, 128), F32)], axis=0)
    k0[...] = full[index[0]]
    k2[...] = full[lax.bitwise_xor(index[0], 2)]
    for n in range(2):
        near[n] = full[lax.bitwise_xor(index[0], 2 * n + 1)]


def z_mask(own2, own34, n1, n2, n3, k0, near, away, index, t, c2, c34, s1, s2, s3, full, keep2):
    full[index[0]] = k0[...]
    full[lax.bitwise_xor(index[0], 1)] = near[0]
    for n in range(2):
        full[lax.bitwise_xor(index[0], 2 + n)] = away[n]
    for a in range(4):
        for bz in range(2):
            for bx in range(2):
                at = bz * 128 + a * 32
                rows = full[a, bx * 64 + bz * 32 : bx * 64 + bz * 32 + 32]
                keep2[at : at + 32, bx * 128 : bx * 128 + 128] = rows
    tiles = []
    for slot in range(16):
        bz, a, z = slot // 8, slot // 2 % 4, slot % 2
        tile = full[a, 128 + (bz * 2 + z) * 8 : 136 + (bz * 2 + z) * 8]
        if slot < 8:
            bz, a = slot // 4, slot % 4
            tile = tile + full[a, 160 + bz * 8 : 168 + bz * 8]
        tiles.append(tile)
    keep34 = jnp.concatenate(tiles, axis=0)

    far = taller(jnp.concatenate([n2[...], n3[...]], axis=0), 8)
    part34 = (own34[...] + n1[:128] + left(t("z34p"), far)) * keep34
    c34[...] = part34
    s1[:128] = part34
    back = left(t("z34pt"), part34)
    s2[...] = back[:16]
    s3[...] = back[16:24]
    rim = taller(jnp.concatenate([n1[128:168], n1[168:208]], axis=1), 8)
    part2 = (own2[...] + left(t("z2u"), rim)) * keep2[...]
    c2[...] = part2
    back = left(t("z2ut"), part2)
    s1[128:168] = back[:40, :128]
    s1[168:208] = back[:40, 128:]


def z_join(c2, c34, s1, s2, s3, index, t, p0, p1, p2, p3, w):
    rim = taller(jnp.concatenate([s1[128:168], s1[168:208]], axis=1), 8)
    w[:, :256] = left(t("z2t"), c2[...]) + left(t("z2qt"), rim)
    rows = jnp.concatenate([c34[...], s1[:128], s2[...], s3[...]], axis=0)
    w[:, 256:] = left(t("z34t"), taller(rows, 8))
    for s, piece in enumerate((p0, p1, p2, p3)):
        piece[...] = w[block(index, s)]


def y_send(p0, p1, p2, p3, index, t, w, m1, m2, m3):
    for s, piece in enumerate((p0, p1, p2, p3)):
        w[block(index, -s)] = piece[...]
    m1[:256] = w[:, 256:]
    rim = left(t("y2ut"), w[:, :256])
    m1[256:320] = rim[:, :128]
    m1[320:384] = rim[:, 128:]
    far = left(t("y34pt"), w[:, 256:])
    m2[...] = far[:64]
    m3[...] = far[64:]


def deep_join(w, m1, m2, m3, dz, dy, dc, t, g, pz, py, pc, low):
    rim = jnp.concatenate([m1[256:320], m1[320:384]], axis=1)
    first = left(t("y2t"), w[:, :256]) + left(t("y2qt"), rim)
    rows = [w[:, 256:], m1[:256], m2[...], m3[...]]
    rest = left(t("y34t"), jnp.concatenate(rows, axis=0))
    wide = jnp.concatenate([first, rest[:256], rest[256:]], axis=1)
    low[...] = right(wide, t("xmi")).reshape(8, 32, 256)
    planes = [
        combine(SPREAD[:5, n], [lambda i=i: low[i + 3] for i in range(5)]) for n in range(5)
    ]
    pz[...] = dz[...]
    for n in range(5):
        pz[n, :32, :256] = dz[n, :32, :256] + planes[n]
    corner = left(t("r5ult"), jnp.concatenate(planes, axis=0))
    pc[:, :256] = dc[:, :256] + corner
    pc[:, 256:] = dc[:, 256:]
    for z in range(16):
        g[z] = combine(Z1LO[:, z], [lambda i=i: low[i] for i in range(8)])
    for half in range(2):
        part = g[8 * half : 8 * half + 8].reshape(256, 256)
        py[half, :, :256] = dy[half, :, :256] + left(t("y1ult"), part)[:40]
        py[half, :, 256:] = dy[half, :, 256:]


def own_join(g, low, t, out):
    for c in range(4):
        planes = []
        for z in range(4 * c, 4 * c + 4):
            corner = g[z, :32, :256] + low[z]
            top = jnp.concatenate([corner, g[z, :32, 256:]], axis=1)
            planes += [top, g[z, 32:]]
        part = left(t("y1i"), jnp.concatenate(planes, axis=0))
        out[4 * c : 4 * c + 4] = right(part, t("x1i")).reshape(4, 64, 512)


def finish(base, pz, py, pc, t, out, rz, chunks):
    far = left(t("r5z"), pc[...])
    rims = [taller(py[half], 8) + far[48 * half : 48 * half + 48] for half in range(2)]
    rims = [left(t("r5i"), pz[...].reshape(320, 512))] + rims
    rims = right(jnp.concatenate(rims, axis=0), t("x1i"))
    rz[...] = rims[:320].reshape(5, 64, 512)
    for half in range(2):
        extra = left(t("y1qt"), rims[320 + 48 * half : 368 + 48 * half]).reshape(8, 64, 512)
        for k in range(8):
            z = 8 * half + k
            plane = base[z] + extra[k]
            if z < 10:
                plane = plane + combine(BASIS[:, z], [lambda n=n: rz[n] for n in range(5)])
            out[z] = plane
            if z % 4 == 3:
                chunks[z // 4].start()
    for copy in chunks:
        copy.wait()


def details(f, q, qz, qc, keep, t, g, pz, kept):
    for half in range(2):
        extra = left(t("y1u"), taller(q[half], 8))
        for c in range(2):
            z = 8 * half + 4 * c
            part = left(t("y1f"), f[z : z + 4].reshape(256, 512))
            g[z : z + 4] = (part + extra[256 * c : 256 * c + 256]).reshape(4, 64, 512)
    corner = left(t("r5u"), qc[...]).reshape(5, 64, 512)
    for c in range(4):
        rows = slice(16 * c, 16 * c + 16)
        rim = (qz[:, rows] + corner[:, rows]).reshape(80, 512)
        out = left(t("z1f"), g[:, rows].reshape(256, 512)) + left(t("z1u"), rim)
        out = out.reshape(16, 16, 512)
        by = c // 2
        at = slice(16 * (c % 2), 16 * (c % 2) + 16)
        for bz in range(2):
            for bx in range(2):
                cols = slice(256 * bx, 256 * bx + 256)
                number = 4 * bz + 2 * by + bx
                if number:
                    mask = keep[number - 1, :, at].astype(F32)
                    part = out[8 * bz : 8 * bz + 8, :, cols] * mask
                else:
                    part = jnp.zeros((8, 16, 256), F32)
                kept[8 * bz : 8 * bz + 8, rows, cols] = part
    for n in range(5):
        plane = combine(SPREAD[:5, n], [lambda i=i: kept[i + 3] for i in range(5)])
        pz[n] = plane + combine(SPREAD[5:, n], [lambda i=i: kept[i + 11] for i in range(5)])
    for c in range(4):
        rows = slice(16 * c, 16 * c + 16)
        out = left(t("z1i"), kept[:, rows].reshape(256, 512))
        g[:, rows] = out.reshape(16, 16, 512)


def details_rim(g, pz, t, py, pc):
    for half in range(2):
        part = g[8 * half : 8 * half + 8].reshape(512, 512)
        py[half] = left(t("y1ut"), part)[:40]
    pc[...] = left(t("r5ut"), pz[...].reshape(320, 512))


def moved(value, by_z, by_y):
    pairs = [
        (z * GY + y, (z + by_z) % GZ * GY + (y + by_y) % GY) for z in range(GZ) for y in range(GY)
    ]
    return lax.ppermute(value, ("gz", "gy"), pairs)


def across(value, flip):
    return lax.ppermute(value, "gz", [(z, z ^ flip) for z in range(GZ)])


def exchanged(pieces):
    out = [pieces[0]]
    for s in range(1, MEMBERS):
        pairs = [(z, z // MEMBERS * MEMBERS + (z + s) % MEMBERS) for z in range(GZ)]
        out.append(lax.ppermute(pieces[s], "gz", pairs))
    return out


def on_device(vorticity, keep_one, keep_two, keep_three, keep_four, keep_coarse):
    index = lax.rem(lax.axis_index("gz"), MEMBERS).astype(jnp.int32).reshape(1)
    piece, half = (64, 384), (40, 512)

    f, q, qz, qc = call(
        x_split,
        3.0,
        [(16, 64, 512), (2, 40, 512), (5, 64, 512), half],
        vorticity,
        shelves=[["x1f"], ["y1q"], ["r5f"]],
        scratch=[(5, 64, 512)],
        streamed="in",
    )
    q, qz, qc = moved(q, 0, -1), moved(qz, -1, 0), moved(qc, -1, -1)
    own, m1, m2, m3 = call(
        deep_split,
        3.0,
        [(256, 384), (384, 128), (64, 128), (16, 128)],
        f,
        q,
        qz,
        qc,
        shelves=[["y34"], ["xmf"], ["y2", "y1l"], ["y1ul", "r5ul", "y2q"]],
        scratch=[(16, 32, 256), (8, 32, 256)],
    )
    f, late, m1, m2, m3 = lax.optimization_barrier((f, index, m1, m2, m3))
    m1, m2, m3 = moved(m1, 0, -1), moved(m2, 0, -2), moved(m3, 0, -3)
    g, dz = call(
        details,
        0.5,
        [(16, 64, 512), (5, 64, 512)],
        f,
        q,
        qz,
        qc,
        keep_one,
        shelves=[["y1f", "z1f", "z1i", "z1u"], ["y1u", "r5u"]],
        scratch=[(16, 64, 512)],
    )
    k0, k2, near = call(
        mask_pack,
        0.1,
        [(176, 128), (176, 128), (2, 176, 128)],
        keep_two,
        keep_three,
        keep_four,
        keep_coarse,
        index=late,
        scratch=[(4, 176, 128)],
    )
    near = across(near, 1)
    own, g, near = lax.optimization_barrier((own, g, near))
    away = jnp.stack([k2, near[1]])

    pieces = call(
        y_gather,
        0.7,
        [piece] * 4,
        own,
        m1,
        m2,
        m3,
        index=index,
        shelves=[["y2u", "y34p"]],
        scratch=[(256, 384)],
    )
    pieces = exchanged(pieces)
    own2, own34, n1, n2, n3 = call(
        z_split,
        0.5,
        [(256, 256), (128, 128), (208, 128), (16, 128), (8, 128)],
        *pieces,
        index=index,
        shelves=[["z2", "z34"], ["z2q"]],
        scratch=[(256, 384)],
    )
    away, n1, n2, n3 = lax.optimization_barrier((away, n1, n2, n3))
    n1, n2, n3 = moved(n1, -4, 0), moved(n2, -8, 0), moved(n3, -12, 0)
    away = across(away, 2)

    c2, c34, s1, s2, s3 = call(
        z_mask,
        0.7,
        [(256, 256), (128, 128), (208, 128), (16, 128), (8, 128)],
        own2,
        own34,
        n1,
        n2,
        n3,
        k0,
        near,
        away,
        index=index,
        shelves=[["z2u"], ["z34p", "z34pt", "z2ut"]],
        scratch=[(4, 176, 128), (256, 256)],
    )
    g, s1, s2, s3 = lax.optimization_barrier((g, s1, s2, s3))
    s1, s2, s3 = moved(s1, 4, 0), moved(s2, 8, 0), moved(s3, 12, 0)
    dy, dc = call(
        details_rim, 0.3, [(2, 40, 512), half], g, dz, shelves=[["y1ut"], ["r5ut"]]
    )
    c2, dy = lax.optimization_barrier((c2, dy))
    pieces = call(
        z_join,
        0.8,
        [piece] * 4,
        c2,
        c34,
        s1,
        s2,
        s3,
        index=index,
        shelves=[["z2t", "z34t", "z2qt"]],
        scratch=[(256, 384)],
    )
    pieces = exchanged(pieces)
    w, m1, m2, m3 = call(
        y_send,
        0.4,
        [(256, 384), (384, 128), (64, 128), (16, 128)],
        *pieces,
        index=index,
        shelves=[["y2ut"], ["y34pt"]],
    )
    m1, m2, m3 = moved(m1, 0, 1), moved(m2, 0, 2), moved(m3, 0, 3)
    low, pz, py, pc = call(
        deep_join,
        2.5,
        [(16, 32, 256), (5, 64, 512), (2, 40, 512), half],
        w,
        m1,
        m2,
        m3,
        dz,
        dy,
        dc,
        shelves=[["y34t"], ["xmi", "y2t"], ["y2qt", "y1ult", "r5ult"]],
        scratch=[(8, 32, 256)],
    )
    pz, py, pc = moved(pz, 1, 0), moved(py, 0, 1), moved(pc, 1, 1)
    (base,) = call(
        own_join, 0.5, [(16, 64, 512)], g, low, shelves=[["x1i"], ["y1i"]]
    )
    (out,) = call(
        finish,
        3.0,
        [(16, 64, 512)],
        base,
        pz,
        py,
        pc,
        shelves=[["x1i"], ["y1qt", "r5i"], ["r5z"]],
        scratch=[(5, 64, 512)],
        streamed="out",
    )
    return out


def solution(mesh):
    in_specs = (
        P("gz", "gy", None),
        P(None, "gz", "gy", None),
        P(None, "gz", "gy", None),
        P(None, "gz", "gy", None),
        P(None, "gz", "gy", None),
        P("gz", "gy", None),
    )
    out_specs = P("gz", "gy", None)
    return jax.shard_map(
        on_device, mesh=mesh, in_specs=in_specs, out_specs=out_specs, check_vma=False
    )
```

profile of v0, /device:TPU:1, one launch (start us, length us, event | category | flops | bytes accessed | tf_op | source)
XLA Modules:
  0.0 108.9 jit_solution(1110618286037273013)
XLA Ops:
  0.0 5.9 %x_split.1 = (f32[16,64,512]{2,1,0:T(8,128)S(1)}, f32[2,40,512]{2,1,0:T(8,128)S(1)}, f32[5,64,512]{2,1,0:T(8,128)}, f32[40,512]{1,0:T(8,128)S(1)}) custom-call(f32[16,64,512]{2,1,0:T(8,128)} %refs_0_.2, bf16[2,928,512]{2,1,0:T(8,128)(2,1)} %constant.35.clone.refs_1_), custom_call_target="tpu_custom_call" | custom-call | flops 3300000000 | bytes 10800000 | tf_op jit(solution)/shard_map/x_split/pallas_call | solution.py:342
  5.9 3.3 %collective-permute-start.1 = (f32[5,64,512]{2,1,0:T(8,128)}, f32[5,64,512]{2,1,0:T(8,128)S(1)}, u32[]{:S(2)}, u32[]{:S(2)}) collective-permute-start(f32[5,64,512]{2,1,0:T(8,128)} %get-tuple-element.66), channel_id=1, source_target_pairs={{0,248},{1,249},{2,250},{3,251},{4,252},{5,253},{6,254},{7,255},{8... | collective-permute-start | bytes 1966088 | tf_op jit(solution)/shard_map/ppermute | solution.py:628
  9.2 3.5 %collective-permute-start = (f32[2,40,512]{2,1,0:T(8,128)S(1)}, f32[2,40,512]{2,1,0:T(8,128)S(1)}, u32[]{:S(2)}, u32[]{:S(2)}) collective-permute-start(f32[2,40,512]{2,1,0:T(8,128)S(1)} %get-tuple-element.65), channel_id=1, source_target_pairs={{0,7},{1,0},{2,1},{3,2},{4,3},{5,4},{6,5},{7,6},{8,15},{9,8},{10,9... | collective-permute-start | bytes 491528 | tf_op jit(solution)/shard_map/ppermute | solution.py:628
  12.7 6.6 %collective-permute-start.2 = (f32[40,512]{1,0:T(8,128)S(1)}, f32[40,512]{1,0:T(8,128)S(1)}, u32[]{:S(2)}, u32[]{:S(2)}) collective-permute-start(f32[40,512]{1,0:T(8,128)S(1)} %get-tuple-element.67), channel_id=1, source_target_pairs={{0,255},{1,248},{2,249},{3,250},{4,251},{5,252},{6,253},{7,254},{8... | collective-permute-start | bytes 245768 | tf_op jit(solution)/shard_map/ppermute | solution.py:628
  19.3 2.3 %collective-permute-done.2.refs_3_ = f32[40,512]{1,0:T(8,128)S(1)} collective-permute-done((f32[40,512]{1,0:T(8,128)S(1)}, f32[40,512]{1,0:T(8,128)S(1)}, u32[]{:S(2)}, u32[]{:S(2)}) %collective-permute-start.2) | collective-permute-done | bytes 81952 | tf_op jit(solution)/shard_map/ppermute | solution.py:628
  21.6 2.3 %collective-permute-done.refs_1_ = f32[2,40,512]{2,1,0:T(8,128)S(1)} collective-permute-done((f32[2,40,512]{2,1,0:T(8,128)S(1)}, f32[2,40,512]{2,1,0:T(8,128)S(1)}, u32[]{:S(2)}, u32[]{:S(2)}) %collective-permute-start) | collective-permute-done | bytes 163872 | tf_op jit(solution)/shard_map/ppermute | solution.py:628
  23.9 1.8 %copy-done.9 = bf16[2,1360,512]{2,1,0:T(8,128)(2,1)S(1)} copy-done((bf16[2,1360,512]{2,1,0:T(8,128)(2,1)S(1)}, bf16[2,1360,512]{2,1,0:T(8,128)(2,1)}, u32[]{:S(2)}) %copy-start.9) | copy-done | bytes 2785304
  25.7 2.0 %deep_split.1 = (f32[256,384]{1,0:T(8,128)S(1)}, f32[384,128]{1,0:T(8,128)S(1)}, f32[64,128]{1,0:T(8,128)S(1)}, f32[16,128]{1,0:T(8,128)S(1)}) custom-call(f32[16,64,512]{2,1,0:T(8,128)S(1)} %get-tuple-element.72.refs_0_, f32[2,40,512]{2,1,0:T(8,128)S(1)} %collective-permute-done.refs_1_, f32[5,64,512]{2,1,0:T(8,128)S(1)} %collective-permute-done.1.refs_2_, ...), custom_call_target="tpu_custom_call" | custom-call | flops 3300000000 | bytes 10800000 | tf_op jit(solution)/shard_map/deep_split/pallas_call | solution.py:342
  27.7 1.1 %collective-permute-start.4 = (f32[384,128]{1,0:T(8,128)S(1)}, f32[384,128]{1,0:T(8,128)S(1)}, u32[]{:S(2)}, u32[]{:S(2)}) collective-permute-start(f32[384,128]{1,0:T(8,128)S(1)} %get-tuple-element.78), channel_id=1, source_target_pairs={{0,7},{1,0},{2,1},{3,2},{4,3},{5,4},{6,5},{7,6},{8,15},{9,8},{10,9... | collective-permute-start | bytes 589832 | tf_op jit(solution)/shard_map/ppermute | solution.py:628
  29.0 3.9 %collective-permute-start.3 = (f32[2,176,128]{2,1,0:T(8,128)S(1)}, f32[2,176,128]{2,1,0:T(8,128)S(1)}, u32[]{:S(2)}, u32[]{:S(2)}) collective-permute-start(f32[2,176,128]{2,1,0:T(8,128)S(1)} %get-tuple-element.75), channel_id=1, source_target_pairs={{0,8},{8,0},{16,24},{24,16},{32,40},{40,32},{48,56},{56,48},{64,72... | collective-permute-start | bytes 540680 | tf_op jit(solution)/shard_map/ppermute | solution.py:632
  34.4 4.6 %details.1 = (f32[16,64,512]{2,1,0:T(8,128)S(1)}, f32[5,64,512]{2,1,0:T(8,128)S(1)}) custom-call(f32[16,64,512]{2,1,0:T(8,128)S(1)} %get-tuple-element.72.refs_0_, f32[2,40,512]{2,1,0:T(8,128)S(1)} %collective-permute-done.refs_1_, f32[5,64,512]{2,1,0:T(8,128)S(1)} %collective-permute-done.1.refs_2_, f32[40,512]{1,0:T(8,128)S(1)} %collective-permute-done.2.refs_3_, ...), custom_call_target="tpu_custom_call" | custom-call | flops 550000000 | bytes 1800000 | tf_op jit(solution)/shard_map/details/pallas_call | solution.py:342
  39.5 1.3 %collective-permute-start.7 = (f32[64,384]{1,0:T(8,128)S(1)}, f32[64,384]{1,0:T(8,128)S(1)}, u32[]{:S(2)}, u32[]{:S(2)}) collective-permute-start(f32[64,384]{1,0:T(8,128)S(1)} %get-tuple-element.82), channel_id=1, source_target_pairs={{0,8},{8,16},{16,24},{24,0},{32,40},{40,48},{48,56},{56,32},{64,72... | collective-permute-start | bytes 294920 | tf_op jit(solution)/shard_map/ppermute | solution.py:639
  41.6 1.2 %collective-permute-done.7.refs_1_ = f32[64,384]{1,0:T(8,128)S(1)} collective-permute-done((f32[64,384]{1,0:T(8,128)S(1)}, f32[64,384]{1,0:T(8,128)S(1)}, u32[]{:S(2)}, u32[]{:S(2)}) %collective-permute-start.7) | collective-permute-done | bytes 98336 | tf_op jit(solution)/shard_map/ppermute | solution.py:639
  42.8 3.3 %collective-permute-done.8.refs_2_ = f32[64,384]{1,0:T(8,128)S(1)} collective-permute-done((f32[64,384]{1,0:T(8,128)S(1)}, f32[64,384]{1,0:T(8,128)S(1)}, u32[]{:S(2)}, u32[]{:S(2)}) %collective-permute-start.8) | collective-permute-done | bytes 98336 | tf_op jit(solution)/shard_map/ppermute | solution.py:639
  48.0 5.7 %collective-permute-start.10 = (f32[208,128]{1,0:T(8,128)S(1)}, f32[208,128]{1,0:T(8,128)S(1)}, u32[]{:S(2)}, u32[]{:S(2)}) collective-permute-start(f32[208,128]{1,0:T(8,128)S(1)} %get-tuple-element.92), channel_id=1, source_target_pairs={{0,224},{1,225},{2,226},{3,227},{4,228},{5,229},{6,230},{7,231},{8... | collective-permute-start | bytes 319496 | tf_op jit(solution)/shard_map/ppermute | solution.py:628
  55.2 3.8 %collective-permute-done.12.refs_4_ = f32[8,128]{1,0:T(8,128)S(1)} collective-permute-done((f32[8,128]{1,0:T(8,128)S(1)}, f32[8,128]{1,0:T(8,128)S(1)}, u32[]{:S(2)}, u32[]{:S(2)}) %collective-permute-start.12) | collective-permute-done | bytes 4128 | tf_op jit(solution)/shard_map/ppermute | solution.py:628
  59.6 2.0 %collective-permute-start.14 = (f32[208,128]{1,0:T(8,128)S(1)}, f32[208,128]{1,0:T(8,128)S(1)}, u32[]{:S(2)}, u32[]{:S(2)}) collective-permute-start(f32[208,128]{1,0:T(8,128)S(1)} %get-tuple-element.106), channel_id=1, source_target_pairs={{0,32},{1,33},{2,34},{3,35},{4,36},{5,37},{6,38},{7,39},{8,40},{9,... | collective-permute-start | bytes 319496 | tf_op jit(solution)/shard_map/ppermute | solution.py:628
  62.0 1.7 %collective-permute-start.15 = (f32[16,128]{1,0:T(8,128)S(1)}, f32[16,128]{1,0:T(8,128)S(1)}, u32[]{:S(2)}, u32[]{:S(2)}) collective-permute-start(f32[16,128]{1,0:T(8,128)S(1)} %get-tuple-element.107), channel_id=1, source_target_pairs={{0,64},{1,65},{2,66},{3,67},{4,68},{5,69},{6,70},{7,71},{8,72},{9,... | collective-permute-start | bytes 24584 | tf_op jit(solution)/shard_map/ppermute | solution.py:628
  64.6 2.5 %collective-permute-done.16.refs_4_ = f32[8,128]{1,0:T(8,128)S(1)} collective-permute-done((f32[8,128]{1,0:T(8,128)S(1)}, f32[8,128]{1,0:T(8,128)S(1)}, u32[]{:S(2)}, u32[]{:S(2)}) %collective-permute-start.16) | collective-permute-done | bytes 4128 | tf_op jit(solution)/shard_map/ppermute | solution.py:628
  67.7 3.4 %collective-permute-start.17 = (f32[64,384]{1,0:T(8,128)S(1)}, f32[64,384]{1,0:T(8,128)S(1)}, u32[]{:S(2)}, u32[]{:S(2)}) collective-permute-start(f32[64,384]{1,0:T(8,128)S(1)} %get-tuple-element.110), channel_id=1, source_target_pairs={{0,8},{8,16},{16,24},{24,0},{32,40},{40,48},{48,56},{56,32},{64,72... | collective-permute-start | bytes 294920 | tf_op jit(solution)/shard_map/ppermute | solution.py:639
  71.9 1.2 %collective-permute-done.17.refs_1_ = f32[64,384]{1,0:T(8,128)S(1)} collective-permute-done((f32[64,384]{1,0:T(8,128)S(1)}, f32[64,384]{1,0:T(8,128)S(1)}, u32[]{:S(2)}, u32[]{:S(2)}) %collective-permute-start.17) | collective-permute-done | bytes 98336 | tf_op jit(solution)/shard_map/ppermute | solution.py:639
  73.1 3.3 %collective-permute-done.18.refs_2_ = f32[64,384]{1,0:T(8,128)S(1)} collective-permute-done((f32[64,384]{1,0:T(8,128)S(1)}, f32[64,384]{1,0:T(8,128)S(1)}, u32[]{:S(2)}, u32[]{:S(2)}) %collective-permute-start.18) | collective-permute-done | bytes 98336 | tf_op jit(solution)/shard_map/ppermute | solution.py:639
  77.3 2.7 %collective-permute-start.20 = (f32[384,128]{1,0:T(8,128)S(1)}, f32[384,128]{1,0:T(8,128)S(1)}, u32[]{:S(2)}, u32[]{:S(2)}) collective-permute-start(f32[384,128]{1,0:T(8,128)S(1)} %get-tuple-element.114), channel_id=1, source_target_pairs={{0,1},{1,2},{2,3},{3,4},{4,5},{5,6},{6,7},{7,0},{8,9},{9,10},{10,1... | collective-permute-start | bytes 589832 | tf_op jit(solution)/shard_map/ppermute | solution.py:628
  80.0 1.2 %collective-permute-start.21 = (f32[64,128]{1,0:T(8,128)S(1)}, f32[64,128]{1,0:T(8,128)S(1)}, u32[]{:S(2)}, u32[]{:S(2)}) collective-permute-start(f32[64,128]{1,0:T(8,128)S(1)} %get-tuple-element.115), channel_id=1, source_target_pairs={{0,2},{1,3},{2,4},{3,5},{4,6},{5,7},{6,0},{7,1},{8,10},{9,11},{10,... | collective-permute-start | bytes 98312 | tf_op jit(solution)/shard_map/ppermute | solution.py:628
  81.3 1.1 collective-permute-start.22
  82.3 5.4 %collective-permute-done.22.refs_3_ = f32[16,128]{1,0:T(8,128)S(1)} collective-permute-done((f32[16,128]{1,0:T(8,128)S(1)}, f32[16,128]{1,0:T(8,128)S(1)}, u32[]{:S(2)}, u32[]{:S(2)}) %collective-permute-start.22) | collective-permute-done | bytes 8224 | tf_op jit(solution)/shard_map/ppermute | solution.py:628
  88.5 1.9 %deep_join.1 = (f32[16,32,256]{2,1,0:T(8,128)S(1)}, f32[5,64,512]{2,1,0:T(8,128)S(1)}, f32[2,40,512]{2,1,0:T(8,128)S(1)}, f32[40,512]{1,0:T(8,128)S(1)}) custom-call(f32[256,384]{1,0:T(8,128)S(1)} %get-tuple-element.113.refs_0_, f32[384,128]{1,0:T(8,128)S(1)} %collective-permute-done.20.refs_1_, f32[64,128]{1,0:T(8,128)S(1)} %collective-permute-done.21.refs_2_, ...), custom_call_target="tpu_custom_call" | custom-call | flops 2750000128 | bytes 9000000 | tf_op jit(solution)/shard_map/deep_join/pallas_call | solution.py:342
  91.6 2.1 %collective-permute-start.25 = (f32[40,512]{1,0:T(8,128)S(1)}, f32[40,512]{1,0:T(8,128)S(1)}, u32[]{:S(2)}, u32[]{:S(2)}) collective-permute-start(f32[40,512]{1,0:T(8,128)S(1)} %get-tuple-element.122), channel_id=1, source_target_pairs={{0,9},{1,10},{2,11},{3,12},{4,13},{5,14},{6,15},{7,8},{8,17},{9,18... | collective-permute-start | bytes 245768 | tf_op jit(solution)/shard_map/ppermute | solution.py:628
  93.8 3.0 %own_join.1.refs_0_ = f32[16,64,512]{2,1,0:T(8,128)S(1)} custom-call(f32[16,64,512]{2,1,0:T(8,128)S(1)} %get-tuple-element.100.refs_0_, f32[16,32,256]{2,1,0:T(8,128)S(1)} %get-tuple-element.119.refs_1_, bf16[2,768,512]{2,1,0:T(8,128)(2,1)S(1)} %copy-done.2), custom_call_target="tpu_custom_call" | custom-call | flops 550000000 | bytes 1800000 | tf_op jit(solution)/shard_map/own_join/pallas_call | solution.py:342
  96.7 6.4 %collective-permute-done.25.refs_3_ = f32[40,512]{1,0:T(8,128)S(1)} collective-permute-done((f32[40,512]{1,0:T(8,128)S(1)}, f32[40,512]{1,0:T(8,128)S(1)}, u32[]{:S(2)}, u32[]{:S(2)}) %collective-permute-start.25) | collective-permute-done | bytes 81952 | tf_op jit(solution)/shard_map/ppermute | solution.py:628
  103.1 2.1 %collective-permute-done.24.refs_2_ = f32[2,40,512]{2,1,0:T(8,128)S(1)} collective-permute-done((f32[2,40,512]{2,1,0:T(8,128)S(1)}, f32[2,40,512]{2,1,0:T(8,128)S(1)}, u32[]{:S(2)}, u32[]{:S(2)}) %collective-permute-start.24) | collective-permute-done | bytes 163872 | tf_op jit(solution)/shard_map/ppermute | solution.py:628
  105.2 3.4 %finish.1 = f32[16,64,512]{2,1,0:T(8,128)} custom-call(f32[16,64,512]{2,1,0:T(8,128)S(1)} %own_join.1.refs_0_, f32[5,64,512]{2,1,0:T(8,128)S(1)} %collective-permute-done.23.refs_1_, f32[2,40,512]{2,1,0:T(8,128)S(1)} %collective-permute-done.24.refs_2_, f32[40,512]{1,0:T(8,128)S(1)} %collective-permute-done.25.refs_3_, bf16[2,1120,512]{2,1,0:T(8,128)(2,1)S(1)} %copy-done.10), custom_call_target="tpu_custom_call" | custom-call | flops 3300000000 | bytes 10800000 | tf_op jit(solution)/shard_map/finish/pallas_call | solution.py:342
  (67 shorter events, 12.3 us)
Async XLA Ops:
  5.9 17.9 %collective-permute-start.1 = (f32[5,64,512]{2,1,0:T(8,128)}, f32[5,64,512]{2,1,0:T(8,128)S(1)}, u32[]{:S(2)}, u32[]{:S(2)}) collective-permute-start(f32[5,64,512]{2,1,0:T(8,128)} %get-tuple-element.66), channel_id=1, source_target_pairs={{0,248},{1,249},{2,250},{3,251},{4,252},{5,253},{6,254},{7,255},{8... | collective-permute-start | bytes 1966088 | tf_op jit(solution)/shard_map/ppermute | solution.py:628
  9.2 14.6 %collective-permute-start = (f32[2,40,512]{2,1,0:T(8,128)S(1)}, f32[2,40,512]{2,1,0:T(8,128)S(1)}, u32[]{:S(2)}, u32[]{:S(2)}) collective-permute-start(f32[2,40,512]{2,1,0:T(8,128)S(1)} %get-tuple-element.65), channel_id=1, source_target_pairs={{0,7},{1,0},{2,1},{3,2},{4,3},{5,4},{6,5},{7,6},{8,15},{9,8},{10,9... | collective-permute-start | bytes 491528 | tf_op jit(solution)/shard_map/ppermute | solution.py:628
  12.7 8.9 %collective-permute-start.2 = (f32[40,512]{1,0:T(8,128)S(1)}, f32[40,512]{1,0:T(8,128)S(1)}, u32[]{:S(2)}, u32[]{:S(2)}) collective-permute-start(f32[40,512]{1,0:T(8,128)S(1)} %get-tuple-element.67), channel_id=1, source_target_pairs={{0,255},{1,248},{2,249},{3,250},{4,251},{5,252},{6,253},{7,254},{8... | collective-permute-start | bytes 245768 | tf_op jit(solution)/shard_map/ppermute | solution.py:628
  27.7 11.4 %collective-permute-start.4 = (f32[384,128]{1,0:T(8,128)S(1)}, f32[384,128]{1,0:T(8,128)S(1)}, u32[]{:S(2)}, u32[]{:S(2)}) collective-permute-start(f32[384,128]{1,0:T(8,128)S(1)} %get-tuple-element.78), channel_id=1, source_target_pairs={{0,7},{1,0},{2,1},{3,2},{4,3},{5,4},{6,5},{7,6},{8,15},{9,8},{10,9... | collective-permute-start | bytes 589832 | tf_op jit(solution)/shard_map/ppermute | solution.py:628
  28.9 10.2 %copy-start.14 = (bf16[2,256,256]{2,1,0:T(8,128)(2,1)S(1)}, bf16[2,256,256]{2,1,0:T(8,128)(2,1)}, u32[]{:S(2)}) copy-start(bf16[2,256,256]{2,1,0:T(8,128)(2,1)} %constant.38.clone.refs_5_) | copy-start | bytes 786436
  29.0 10.1 %collective-permute-start.3 = (f32[2,176,128]{2,1,0:T(8,128)S(1)}, f32[2,176,128]{2,1,0:T(8,128)S(1)}, u32[]{:S(2)}, u32[]{:S(2)}) collective-permute-start(f32[2,176,128]{2,1,0:T(8,128)S(1)} %get-tuple-element.75), channel_id=1, source_target_pairs={{0,8},{8,0},{16,24},{24,16},{32,40},{40,32},{48,56},{56,48},{64,72... | collective-permute-start | bytes 540680 | tf_op jit(solution)/shard_map/ppermute | solution.py:632
  32.9 6.2 %collective-permute-start.6 = (f32[16,128]{1,0:T(8,128)S(1)}, f32[16,128]{1,0:T(8,128)S(1)}, u32[]{:S(2)}, u32[]{:S(2)}) collective-permute-start(f32[16,128]{1,0:T(8,128)S(1)} %get-tuple-element.80), channel_id=1, source_target_pairs={{0,5},{1,6},{2,7},{3,0},{4,1},{5,2},{6,3},{7,4},{8,13},{9,14},{10,... | collective-permute-start | bytes 24584 | tf_op jit(solution)/shard_map/ppermute | solution.py:628
  33.6 5.5 %collective-permute-start.5 = (f32[64,128]{1,0:T(8,128)S(1)}, f32[64,128]{1,0:T(8,128)S(1)}, u32[]{:S(2)}, u32[]{:S(2)}) collective-permute-start(f32[64,128]{1,0:T(8,128)S(1)} %get-tuple-element.79), channel_id=1, source_target_pairs={{0,6},{1,7},{2,0},{3,1},{4,2},{5,3},{6,4},{7,5},{8,14},{9,15},{10,... | collective-permute-start | bytes 98312 | tf_op jit(solution)/shard_map/ppermute | solution.py:628
  39.1 19.9 %copy-start.12 = (bf16[2,384,512]{2,1,0:T(8,128)(2,1)S(1)}, bf16[2,384,512]{2,1,0:T(8,128)(2,1)}, u32[]{:S(2)}) copy-start(bf16[2,384,512]{2,1,0:T(8,128)(2,1)} %constant.40.clone.refs_9_) | copy-start | bytes 2359300
  39.5 3.3 %collective-permute-start.7 = (f32[64,384]{1,0:T(8,128)S(1)}, f32[64,384]{1,0:T(8,128)S(1)}, u32[]{:S(2)}, u32[]{:S(2)}) collective-permute-start(f32[64,384]{1,0:T(8,128)S(1)} %get-tuple-element.82), channel_id=1, source_target_pairs={{0,8},{8,16},{16,24},{24,0},{32,40},{40,48},{48,56},{56,32},{64,72... | collective-permute-start | bytes 294920 | tf_op jit(solution)/shard_map/ppermute | solution.py:639
  40.8 5.3 %collective-permute-start.8 = (f32[64,384]{1,0:T(8,128)S(1)}, f32[64,384]{1,0:T(8,128)S(1)}, u32[]{:S(2)}, u32[]{:S(2)}) collective-permute-start(f32[64,384]{1,0:T(8,128)S(1)} %get-tuple-element.83), channel_id=1, source_target_pairs={{0,16},{8,24},{16,0},{24,8},{32,48},{40,56},{48,32},{56,40},{64,80... | collective-permute-start | bytes 294920 | tf_op jit(solution)/shard_map/ppermute | solution.py:639
  41.6 5.2 %collective-permute-start.9 = (f32[64,384]{1,0:T(8,128)S(1)}, f32[64,384]{1,0:T(8,128)S(1)}, u32[]{:S(2)}, u32[]{:S(2)}) collective-permute-start(f32[64,384]{1,0:T(8,128)S(1)} %get-tuple-element.84), channel_id=1, source_target_pairs={{0,24},{8,0},{16,8},{24,16},{32,56},{40,32},{48,40},{56,48},{64,88... | collective-permute-start | bytes 294920 | tf_op jit(solution)/shard_map/ppermute | solution.py:639
  46.7 17.0 %copy-start.3 = (bf16[2,96,512]{2,1,0:T(8,128)(2,1)S(1)}, bf16[2,96,512]{2,1,0:T(8,128)(2,1)}, u32[]{:S(2)}) copy-start(bf16[2,96,512]{2,1,0:T(8,128)(2,1)} %constant.41.clone.refs_2_) | copy-start | bytes 589828
  47.2 11.8 %collective-permute-start.13 = (f32[2,176,128]{2,1,0:T(8,128)S(1)}, f32[2,176,128]{2,1,0:T(8,128)S(1)}, u32[]{:S(2)}, u32[]{:S(2)}) collective-permute-start(f32[2,176,128]{2,1,0:T(8,128)S(1)} %pad_maximum_fusion), channel_id=1, source_target_pairs={{0,16},{8,24},{16,0},{24,8},{32,48},{40,56},{48,32},{56,40},{64,80... | collective-permute-start | bytes 540680 | tf_op jit(solution)/shard_map/ppermute | solution.py:632
  48.0 11.0 %collective-permute-start.10 = (f32[208,128]{1,0:T(8,128)S(1)}, f32[208,128]{1,0:T(8,128)S(1)}, u32[]{:S(2)}, u32[]{:S(2)}) collective-permute-start(f32[208,128]{1,0:T(8,128)S(1)} %get-tuple-element.92), channel_id=1, source_target_pairs={{0,224},{1,225},{2,226},{3,227},{4,228},{5,229},{6,230},{7,231},{8... | collective-permute-start | bytes 319496 | tf_op jit(solution)/shard_map/ppermute | solution.py:628
  53.7 5.3 %collective-permute-start.11 = (f32[16,128]{1,0:T(8,128)S(1)}, f32[16,128]{1,0:T(8,128)S(1)}, u32[]{:S(2)}, u32[]{:S(2)}) collective-permute-start(f32[16,128]{1,0:T(8,128)S(1)} %get-tuple-element.93), channel_id=1, source_target_pairs={{0,192},{1,193},{2,194},{3,195},{4,196},{5,197},{6,198},{7,199},{8... | collective-permute-start | bytes 24584 | tf_op jit(solution)/shard_map/ppermute | solution.py:628
  54.8 4.3 %collective-permute-start.12 = (f32[8,128]{1,0:T(8,128)S(1)}, f32[8,128]{1,0:T(8,128)S(1)}, u32[]{:S(2)}, u32[]{:S(2)}) collective-permute-start(f32[8,128]{1,0:T(8,128)S(1)} %get-tuple-element.94), channel_id=1, source_target_pairs={{0,160},{1,161},{2,162},{3,163},{4,164},{5,165},{6,166},{7,167},{8... | collective-permute-start | bytes 12296 | tf_op jit(solution)/shard_map/ppermute | solution.py:628
  59.6 7.5 %collective-permute-start.14 = (f32[208,128]{1,0:T(8,128)S(1)}, f32[208,128]{1,0:T(8,128)S(1)}, u32[]{:S(2)}, u32[]{:S(2)}) collective-permute-start(f32[208,128]{1,0:T(8,128)S(1)} %get-tuple-element.106), channel_id=1, source_target_pairs={{0,32},{1,33},{2,34},{3,35},{4,36},{5,37},{6,38},{7,39},{8,40},{9,... | collective-permute-start | bytes 319496 | tf_op jit(solution)/shard_map/ppermute | solution.py:628
  61.7 5.5 %collective-permute-start.16 = (f32[8,128]{1,0:T(8,128)S(1)}, f32[8,128]{1,0:T(8,128)S(1)}, u32[]{:S(2)}, u32[]{:S(2)}) collective-permute-start(f32[8,128]{1,0:T(8,128)S(1)} %get-tuple-element.108), channel_id=1, source_target_pairs={{0,96},{1,97},{2,98},{3,99},{4,100},{5,101},{6,102},{7,103},{8,104... | collective-permute-start | bytes 12296 | tf_op jit(solution)/shard_map/ppermute | solution.py:628
  62.0 5.1 %collective-permute-start.15 = (f32[16,128]{1,0:T(8,128)S(1)}, f32[16,128]{1,0:T(8,128)S(1)}, u32[]{:S(2)}, u32[]{:S(2)}) collective-permute-start(f32[16,128]{1,0:T(8,128)S(1)} %get-tuple-element.107), channel_id=1, source_target_pairs={{0,64},{1,65},{2,66},{3,67},{4,68},{5,69},{6,70},{7,71},{8,72},{9,... | collective-permute-start | bytes 24584 | tf_op jit(solution)/shard_map/ppermute | solution.py:628
  64.6 12.4 %copy-start.15 = (bf16[2,144,256]{2,1,0:T(8,128)(2,1)S(1)}, bf16[2,144,256]{2,1,0:T(8,128)(2,1)}, u32[]{:S(2)}) copy-start(bf16[2,144,256]{2,1,0:T(8,128)(2,1)} %constant.43.clone.refs_5_) | copy-start | bytes 442372
  67.1 21.4 %copy-start.8 = (bf16[2,1280,640]{2,1,0:T(8,128)(2,1)S(1)}, bf16[2,1280,640]{2,1,0:T(8,128)(2,1)}, u32[]{:S(2)}) copy-start(bf16[2,1280,640]{2,1,0:T(8,128)(2,1)} %constant.44.clone.refs_7_) | copy-start | bytes 9830404
  67.7 5.4 %collective-permute-start.17 = (f32[64,384]{1,0:T(8,128)S(1)}, f32[64,384]{1,0:T(8,128)S(1)}, u32[]{:S(2)}, u32[]{:S(2)}) collective-permute-start(f32[64,384]{1,0:T(8,128)S(1)} %get-tuple-element.110), channel_id=1, source_target_pairs={{0,8},{8,16},{16,24},{24,0},{32,40},{40,48},{48,56},{56,32},{64,72... | collective-permute-start | bytes 294920 | tf_op jit(solution)/shard_map/ppermute | solution.py:639
  71.2 5.3 %collective-permute-start.18 = (f32[64,384]{1,0:T(8,128)S(1)}, f32[64,384]{1,0:T(8,128)S(1)}, u32[]{:S(2)}, u32[]{:S(2)}) collective-permute-start(f32[64,384]{1,0:T(8,128)S(1)} %get-tuple-element.111), channel_id=1, source_target_pairs={{0,16},{8,24},{16,0},{24,8},{32,48},{40,56},{48,32},{56,40},{64,80... | collective-permute-start | bytes 294920 | tf_op jit(solution)/shard_map/ppermute | solution.py:639
  71.9 5.2 %collective-permute-start.19 = (f32[64,384]{1,0:T(8,128)S(1)}, f32[64,384]{1,0:T(8,128)S(1)}, u32[]{:S(2)}, u32[]{:S(2)}) collective-permute-start(f32[64,384]{1,0:T(8,128)S(1)} %get-tuple-element.112), channel_id=1, source_target_pairs={{0,24},{8,0},{16,8},{24,16},{32,56},{40,32},{48,40},{56,48},{64,88... | collective-permute-start | bytes 294920 | tf_op jit(solution)/shard_map/ppermute | solution.py:639
  77.3 11.2 %collective-permute-start.20 = (f32[384,128]{1,0:T(8,128)S(1)}, f32[384,128]{1,0:T(8,128)S(1)}, u32[]{:S(2)}, u32[]{:S(2)}) collective-permute-start(f32[384,128]{1,0:T(8,128)S(1)} %get-tuple-element.114), channel_id=1, source_target_pairs={{0,1},{1,2},{2,3},{3,4},{4,5},{5,6},{6,7},{7,0},{8,9},{9,10},{10,1... | collective-permute-start | bytes 589832 | tf_op jit(solution)/shard_map/ppermute | solution.py:628
  80.0 8.5 %collective-permute-start.21 = (f32[64,128]{1,0:T(8,128)S(1)}, f32[64,128]{1,0:T(8,128)S(1)}, u32[]{:S(2)}, u32[]{:S(2)}) collective-permute-start(f32[64,128]{1,0:T(8,128)S(1)} %get-tuple-element.115), channel_id=1, source_target_pairs={{0,2},{1,3},{2,4},{3,5},{4,6},{5,7},{6,0},{7,1},{8,10},{9,11},{10,... | collective-permute-start | bytes 98312 | tf_op jit(solution)/shard_map/ppermute | solution.py:628
  81.3 6.4 %collective-permute-start.22 = (f32[16,128]{1,0:T(8,128)S(1)}, f32[16,128]{1,0:T(8,128)S(1)}, u32[]{:S(2)}, u32[]{:S(2)}) collective-permute-start(f32[16,128]{1,0:T(8,128)S(1)} %get-tuple-element.116), channel_id=1, source_target_pairs={{0,3},{1,4},{2,5},{3,6},{4,7},{5,0},{6,1},{7,2},{8,11},{9,12},{10,... | collective-permute-start | bytes 24584 | tf_op jit(solution)/shard_map/ppermute | solution.py:628
  90.4 14.8 %collective-permute-start.23 = (f32[5,64,512]{2,1,0:T(8,128)S(1)}, f32[5,64,512]{2,1,0:T(8,128)S(1)}, u32[]{:S(2)}, u32[]{:S(2)}) collective-permute-start(f32[5,64,512]{2,1,0:T(8,128)S(1)} %get-tuple-element.120), channel_id=1, source_target_pairs={{0,8},{1,9},{2,10},{3,11},{4,12},{5,13},{6,14},{7,15},{8,16},{9,17... | collective-permute-start | bytes 1966088 | tf_op jit(solution)/shard_map/ppermute | solution.py:628
  91.4 13.9 %collective-permute-start.24 = (f32[2,40,512]{2,1,0:T(8,128)S(1)}, f32[2,40,512]{2,1,0:T(8,128)S(1)}, u32[]{:S(2)}, u32[]{:S(2)}) collective-permute-start(f32[2,40,512]{2,1,0:T(8,128)S(1)} %get-tuple-element.121), channel_id=1, source_target_pairs={{0,1},{1,2},{2,3},{3,4},{4,5},{5,6},{6,7},{7,0},{8,9},{9,10},{10,1... | collective-permute-start | bytes 491528 | tf_op jit(solution)/shard_map/ppermute | solution.py:628
  91.6 11.5 %collective-permute-start.25 = (f32[40,512]{1,0:T(8,128)S(1)}, f32[40,512]{1,0:T(8,128)S(1)}, u32[]{:S(2)}, u32[]{:S(2)}) collective-permute-start(f32[40,512]{1,0:T(8,128)S(1)} %get-tuple-element.122), channel_id=1, source_target_pairs={{0,9},{1,10},{2,11},{3,12},{4,13},{5,14},{6,15},{7,8},{8,17},{9,18... | collective-permute-start | bytes 245768 | tf_op jit(solution)/shard_map/ppermute | solution.py:628
  93.8 11.5 %copy-start.10 = (bf16[2,1120,512]{2,1,0:T(8,128)(2,1)S(1)}, bf16[2,1120,512]{2,1,0:T(8,128)(2,1)}, u32[]{:S(2)}) copy-start(bf16[2,1120,512]{2,1,0:T(8,128)(2,1)} %constant.46.clone.refs_4_) | copy-start | bytes 6881284
  (10 other events, 52.4 us)
where the time goes:
time: 109 us
  starting transfers between devices  46.6 us (43%)
  waiting for transfers between devices  35.8 us (33%)
  Pallas kernels  24.1 us (22%)
  local copies, waits for them, and re-layouts  1.88 us (2%)
    ppermute x18, starting transfers between devices, moved(): return lax.ppermute(value, ('gz', 'gy'), pairs)  35.6 us
    ppermute x18, waiting for transfers between devices, moved(): return lax.ppermute(value, ('gz', 'gy'), pairs)  25.5 us
    pallas_call x13, Pallas kernels, call(): pl.pallas_call(body, name=kernel.__name__, out_shape=[jax.ShapeDtypeStruc...  24.1 us
    ppermute x6, waiting for transfers between devices, exchanged(): out.append(lax.ppermute(pieces[s], 'gz', pairs))  10.3 us
    ppermute x6, starting transfers between devices, exchanged(): out.append(lax.ppermute(pieces[s], 'gz', pairs))  6.25 us
    ppermute x2, starting transfers between devices, across(): return lax.ppermute(value, 'gz', [(z, z ^ flip) for z in range(GZ)])  4.74 us
  transfers between devices with their start and end apart: 26, of which 14 were waited for; matrix products, arithmetic and copies ran while one was open for 0% of the time, Pallas kernels for 8%

commit v1 on v0

--- a/solution.py
+++ b/solution.py
@@ -109,6 +109,8 @@
     lows, highs = np.kron(np.eye(5), y1[:32]), np.kron(np.eye(5), y1[32:])
     mats["r5f"] = np.concatenate([lows, corner, highs])
     mats["r5i"] = np.kron(np.eye(5), y1.T)
+    mats["r5il"] = np.kron(np.eye(5), y1[:32].T)
+    mats["y1r"] = np.kron(np.eye(16), padded(basis, 5, 16))
     mats["r5u"] = np.kron(np.eye(5), padded(put, 64, 8))
     mats["r5ut"] = mats["r5u"].T
     mats["r5ul"] = np.kron(np.eye(5), padded(put[:32], 32, 8))
@@ -274,8 +276,8 @@
     return jnp.concatenate([value, jnp.zeros((rows, value.shape[1]), F32)], axis=0)
 
 
-def call(kernel, micros, outs, *operands, shelves=None, index=None, scratch=(), streamed=None):
-    spec, anywhere = pl.BlockSpec(memory_space=pltpu.VMEM), pl.BlockSpec(memory_space=pltpu.HBM)
+def call(kernel, micros, outs, *operands, shelves=None, index=None, scratch=(), table=None, streamed=False):
+    spec, far = pl.BlockSpec(memory_space=pltpu.VMEM), pl.BlockSpec(memory_space=pltpu.HBM)
     specs = [spec] * len(operands)
     out_specs = [spec] * len(outs)
     operands = list(operands)
@@ -285,48 +287,17 @@
         operands.append(index)
         specs.append(pl.BlockSpec(memory_space=pltpu.SMEM))
     if shelves is not None:
-        table, places = packed(shelves)
-        operands.append(jnp.asarray(table))
+        packed_table, places = packed(shelves)
+        operands.append(jnp.asarray(packed_table) if table is None else table)
         specs.append(spec)
-    if streamed == "in":
-        specs[0] = specs[-1] = anywhere
-        for at in (0, -1):
-            operands[at] = pltpu.with_memory_space_constraint(operands[at], pltpu.HBM)
-        scratch += [
-            pltpu.VMEM(operands[0].shape, F32),
-            pltpu.VMEM(operands[-1].shape, BF16),
-            pltpu.SemaphoreType.DMA((6,)),
-        ]
-    if streamed == "out":
-        out_specs = [anywhere] * len(outs)
+    if streamed:
+        out_specs = [far] * len(outs)
         scratch += [pltpu.VMEM(outs[0], F32), pltpu.SemaphoreType.DMA((4,))]
 
     def body(*refs):
         refs = list(refs)
         count = len(operands)
-        if streamed == "in":
-            held, table_held, sems = refs[-3:]
-            table_copies = []
-            for k, (low, high) in enumerate(((0, 512), (512, table_held.shape[1]))):
-                rows = pl.ds(low, high - low)
-                table_copies.append(
-                    pltpu.make_async_copy(
-                        refs[count - 1].at[:, rows], table_held.at[:, rows], sems.at[4 + k]
-                    )
-                )
-            chunks = []
-            for c in range(4):
-                rows = pl.ds(4 * c, 4)
-                chunks.append(pltpu.make_async_copy(refs[0].at[rows], held.at[rows], sems.at[c]))
-            chunks[0].start()
-            table_copies[0].start()
-            for copy in chunks[1:]:
-                copy.start()
-            table_copies[1].start()
-            table_copies[0].wait()
-            refs[0], refs[count - 1] = held, table_held
-            refs = refs[:-3] + [chunks + table_copies[1:]]
-        if streamed == "out":
+        if streamed:
             held, sems = refs[-2:]
             target = refs[count]
             chunks = []
@@ -361,31 +332,75 @@
     return pl.ds(pl.multiple_of(member(index, by) * rows, rows), rows)
 
 
-def x_split(v, t, f, q, qz, qc, b, chunks):
+DEEP = [["y34"], ["xmf"], ["y2", "y1l"], ["y1ul", "r5ul", "y2q"]]
+
+
+def x_rims(vorticity):
+    table, places = packed([["x1f"], ["r5f"], ["y1r"]])
+    deep_table, _ = packed(DEEP)
+    operands = [vorticity, jnp.asarray(table), jnp.asarray(deep_table)]
+    operands = [pltpu.with_memory_space_constraint(part, pltpu.HBM) for part in operands]
+    outs = [(2, 40, 512), (5, 32, 256), (5, 32, 768), (40, 512), (16, 64, 512)]
+
+    def kernel(v, small, large, q, qa, qb, qc, held, deep, small_held, b, sems):
+        chunks = []
+        for c in range(4):
+            rows = pl.ds(4 * c, 4)
+            chunks.append(pltpu.make_async_copy(v.at[rows], held.at[rows], sems.at[c]))
+        small_copy = pltpu.make_async_copy(small, small_held, sems.at[4])
+        deep_copy = pltpu.make_async_copy(large, deep, sems.at[5])
+        for copy in chunks[:3] + [small_copy, chunks[3], deep_copy]:
+            copy.start()
+        for copy in chunks[:3]:
+            copy.wait()
+        t = Tables(small_held, places)
+        for n in range(5):
+            b[n] = combine(BASIS[n], [lambda j=j: held[j] for j in range(10)])
+        small_copy.wait()
+        chunks[3].wait()
+        rim = left(t("r5f"), b[...].reshape(320, 512))
+        rows = left(t("y1r"), held[:, :16].reshape(256, 512))
+        rim = right(jnp.concatenate([rim, rows], axis=0), t("x1f"))
+        q[...] = rim[360:].reshape(2, 40, 512)
+        qc[...] = rim[160:200]
+        qa[...] = rim[:160, :256].reshape(5, 32, 256)
+        qb[:, :, :256] = rim[:160, 256:].reshape(5, 32, 256)
+        qb[:, :, 256:] = rim[200:360].reshape(5, 32, 512)
+        deep_copy.wait()
+
+    spec, far = pl.BlockSpec(memory_space=pltpu.VMEM), pl.BlockSpec(memory_space=pltpu.HBM)
+    shapes = [jax.ShapeDtypeStruct(shape, F32) for shape in outs]
+    shapes.append(jax.ShapeDtypeStruct(deep_table.shape, BF16))
+    return pl.pallas_call(
+        kernel,
+        name="x_rims",
+        out_shape=shapes,
+        in_specs=[far] * 3,
+        out_specs=[spec] * 6,
+        scratch_shapes=[
+            pltpu.VMEM(table.shape, BF16),
+            pltpu.VMEM((5, 64, 512), F32),
+            pltpu.SemaphoreType.DMA((6,)),
+        ],
+        cost_estimate=pl.CostEstimate(flops=3 * 10**9, transcendentals=0, bytes_accessed=10**7),
+        compiler_params=pltpu.CompilerParams(vmem_limit_bytes=24 * 2**20),
+    )(*operands)
+
+
+def x_split(v, t, f):
     for c in range(4):
-        chunks[c].wait()
         part = v[4 * c : 4 * c + 4].reshape(256, 512)
         f[4 * c : 4 * c + 4] = right(part, t("x1f")).reshape(4, 64, 512)
-    for n in range(5):
-        b[n] = combine(BASIS[n], [lambda j=j: f[j] for j in range(10)])
-    chunks[4].wait()
-    rim = left(t("r5f"), b[...].reshape(320, 512))
-    qz[:, :32] = rim[:160].reshape(5, 32, 512)
-    qc[...] = rim[160:200]
-    qz[:, 32:] = rim[200:].reshape(5, 32, 512)
-    for half in range(2):
-        part = f[8 * half : 8 * half + 8].reshape(512, 512)
-        q[half] = left(t("y1q"), part)[:40]
-
-
-def deep_split(f, q, qz, qc, t, own, m1, m2, m3, g, low):
+
+
+def deep_split(f, q, qa, qc, t, own, m1, m2, m3, g, low):
     for half in range(2):
         extra = left(t("y1ul"), taller(q[half, :, :256], 8))
         for c in range(2):
             z = 8 * half + 4 * c
             part = left(t("y1l"), f[z : z + 4, :, :256].reshape(256, 256))
             g[z : z + 4] = (part + extra[128 * c : 128 * c + 128]).reshape(4, 32, 256)
-    rim = qz[:, :32, :256].reshape(160, 256) + left(t("r5ul"), qc[:, :256])
+    rim = qa[...].reshape(160, 256) + left(t("r5ul"), qc[:, :256])
     rim = rim.reshape(5, 32, 256)
     for i in range(8):
         plane = combine(Z1LO[i], [lambda j=j: g[j] for j in range(16)])
@@ -535,18 +550,18 @@
     planes = [
         combine(SPREAD[:5, n], [lambda i=i: low[i + 3] for i in range(5)]) for n in range(5)
     ]
-    pz[...] = dz[...]
-    for n in range(5):
-        pz[n, :32, :256] = dz[n, :32, :256] + planes[n]
-    corner = left(t("r5ult"), jnp.concatenate(planes, axis=0))
-    pc[:, :256] = dc[:, :256] + corner
-    pc[:, 256:] = dc[:, 256:]
     for z in range(16):
         g[z] = combine(Z1LO[:, z], [lambda i=i: low[i] for i in range(8)])
+    planes = jnp.concatenate(planes, axis=0)
+    rims = [left(t("r5il"), planes)]
     for half in range(2):
         part = g[8 * half : 8 * half + 8].reshape(256, 256)
-        py[half, :, :256] = dy[half, :, :256] + left(t("y1ult"), part)[:40]
-        py[half, :, 256:] = dy[half, :, 256:]
+        rims.append(left(t("y1ult"), part)[:40])
+    rims.append(left(t("r5ult"), planes))
+    rims = right(jnp.concatenate(rims, axis=0), t("x1l"))
+    pz[...] = dz[...] + rims[:320].reshape(5, 64, 512)
+    py[...] = dy[...] + rims[320:400].reshape(2, 40, 512)
+    pc[...] = dc[...] + rims[400:]
 
 
 def own_join(g, low, t, out):
@@ -560,19 +575,16 @@
         out[4 * c : 4 * c + 4] = right(part, t("x1i")).reshape(4, 64, 512)
 
 
-def finish(base, pz, py, pc, t, out, rz, chunks):
+def finish(base, pz, py, pc, t, out, chunks):
     far = left(t("r5z"), pc[...])
-    rims = [taller(py[half], 8) + far[48 * half : 48 * half + 48] for half in range(2)]
-    rims = [left(t("r5i"), pz[...].reshape(320, 512))] + rims
-    rims = right(jnp.concatenate(rims, axis=0), t("x1i"))
-    rz[...] = rims[:320].reshape(5, 64, 512)
     for half in range(2):
-        extra = left(t("y1qt"), rims[320 + 48 * half : 368 + 48 * half]).reshape(8, 64, 512)
+        rim = taller(py[half], 8) + far[48 * half : 48 * half + 48]
+        extra = left(t("y1qt"), rim).reshape(8, 64, 512)
         for k in range(8):
             z = 8 * half + k
             plane = base[z] + extra[k]
             if z < 10:
-                plane = plane + combine(BASIS[:, z], [lambda n=n: rz[n] for n in range(5)])
+                plane = plane + combine(BASIS[:, z], [lambda n=n: pz[n] for n in range(5)])
             out[z] = plane
             if z % 4 == 3:
                 chunks[z // 4].start()
@@ -580,17 +592,19 @@
         copy.wait()
 
 
-def details(f, q, qz, qc, keep, t, g, pz, kept):
+def details(f, q, qa, qb, qc, keep, t, g, pz, kept):
     for half in range(2):
         extra = left(t("y1u"), taller(q[half], 8))
         for c in range(2):
             z = 8 * half + 4 * c
             part = left(t("y1f"), f[z : z + 4].reshape(256, 512))
             g[z : z + 4] = (part + extra[256 * c : 256 * c + 256]).reshape(4, 64, 512)
-    corner = left(t("r5u"), qc[...]).reshape(5, 64, 512)
+    top = jnp.concatenate([qa[...], qb[:, :, :256]], axis=2)
+    planes = jnp.concatenate([top, qb[:, :, 256:]], axis=1)
+    planes = planes + left(t("r5u"), qc[...]).reshape(5, 64, 512)
     for c in range(4):
         rows = slice(16 * c, 16 * c + 16)
-        rim = (qz[:, rows] + corner[:, rows]).reshape(80, 512)
+        rim = planes[:, rows].reshape(80, 512)
         out = left(t("z1f"), g[:, rows].reshape(256, 512)) + left(t("z1u"), rim)
         out = out.reshape(16, 16, 512)
         by = c // 2
@@ -614,11 +628,17 @@
         g[:, rows] = out.reshape(16, 16, 512)
 
 
-def details_rim(g, pz, t, py, pc):
+def details_rim(g, dz, t, pz, py, pc):
+    planes = dz[...].reshape(320, 512)
+    rims = [left(t("r5i"), planes)]
     for half in range(2):
         part = g[8 * half : 8 * half + 8].reshape(512, 512)
-        py[half] = left(t("y1ut"), part)[:40]
-    pc[...] = left(t("r5ut"), pz[...].reshape(320, 512))
+        rims.append(left(t("y1ut"), part)[:40])
+    rims.append(left(t("r5ut"), planes))
+    rims = right(jnp.concatenate(rims, axis=0), t("x1i"))
+    pz[...] = rims[:320].reshape(5, 64, 512)
+    py[...] = rims[320:400].reshape(2, 40, 512)
+    pc[...] = rims[400:]
 
 
 def moved(value, by_z, by_y):
@@ -644,41 +664,24 @@
     index = lax.rem(lax.axis_index("gz"), MEMBERS).astype(jnp.int32).reshape(1)
     piece, half = (64, 384), (40, 512)
 
-    f, q, qz, qc = call(
-        x_split,
-        3.0,
-        [(16, 64, 512), (2, 40, 512), (5, 64, 512), half],
-        vorticity,
-        shelves=[["x1f"], ["y1q"], ["r5f"]],
-        scratch=[(5, 64, 512)],
-        streamed="in",
-    )
-    q, qz, qc = moved(q, 0, -1), moved(qz, -1, 0), moved(qc, -1, -1)
+    q, qa, qb, qc, held, deep = x_rims(vorticity)
+    held, q, qa, qc = lax.optimization_barrier((held, q, qa, qc))
+    q, qa, qc = moved(q, 0, -1), moved(qa, -1, 0), moved(qc, -1, -1)
+    (f,) = call(x_split, 0.5, [(16, 64, 512)], held, shelves=[["x1f"]])
     own, m1, m2, m3 = call(
         deep_split,
         3.0,
         [(256, 384), (384, 128), (64, 128), (16, 128)],
         f,
         q,
-        qz,
+        qa,
         qc,
-        shelves=[["y34"], ["xmf"], ["y2", "y1l"], ["y1ul", "r5ul", "y2q"]],
+        shelves=DEEP,
+        table=deep,
         scratch=[(16, 32, 256), (8, 32, 256)],
     )
-    f, late, m1, m2, m3 = lax.optimization_barrier((f, index, m1, m2, m3))
+    late, m1, m2, m3 = lax.optimization_barrier((index, m1, m2, m3))
     m1, m2, m3 = moved(m1, 0, -1), moved(m2, 0, -2), moved(m3, 0, -3)
-    g, dz = call(
-        details,
-        0.5,
-        [(16, 64, 512), (5, 64, 512)],
-        f,
-        q,
-        qz,
-        qc,
-        keep_one,
-        shelves=[["y1f", "z1f", "z1i", "z1u"], ["y1u", "r5u"]],
-        scratch=[(16, 64, 512)],
-    )
     k0, k2, near = call(
         mask_pack,
         0.1,
@@ -691,7 +694,7 @@
         scratch=[(4, 176, 128)],
     )
     near = across(near, 1)
-    own, g, near = lax.optimization_barrier((own, g, near))
+    own, near = lax.optimization_barrier((own, near))
     away = jnp.stack([k2, near[1]])
 
     pieces = call(
@@ -716,9 +719,10 @@
         shelves=[["z2", "z34"], ["z2q"]],
         scratch=[(256, 384)],
     )
-    away, n1, n2, n3 = lax.optimization_barrier((away, n1, n2, n3))
+    away, qb, n1, n2, n3 = lax.optimization_barrier((away, qb, n1, n2, n3))
     n1, n2, n3 = moved(n1, -4, 0), moved(n2, -8, 0), moved(n3, -12, 0)
     away = across(away, 2)
+    qb = moved(qb, -1, 0)
 
     c2, c34, s1, s2, s3 = call(
         z_mask,
@@ -736,12 +740,22 @@
         shelves=[["z2u"], ["z34p", "z34pt", "z2ut"]],
         scratch=[(4, 176, 128), (256, 256)],
     )
-    g, s1, s2, s3 = lax.optimization_barrier((g, s1, s2, s3))
+    f, s1, s2, s3 = lax.optimization_barrier((f, s1, s2, s3))
     s1, s2, s3 = moved(s1, 4, 0), moved(s2, 8, 0), moved(s3, 12, 0)
-    dy, dc = call(
-        details_rim, 0.3, [(2, 40, 512), half], g, dz, shelves=[["y1ut"], ["r5ut"]]
-    )
-    c2, dy = lax.optimization_barrier((c2, dy))
+    g, dz = call(
+        details,
+        0.5,
+        [(16, 64, 512), (5, 64, 512)],
+        f,
+        q,
+        qa,
+        qb,
+        qc,
+        keep_one,
+        shelves=[["y1f", "z1f", "z1i", "z1u"], ["y1u", "r5u"]],
+        scratch=[(16, 64, 512)],
+    )
+    c2, g = lax.optimization_barrier((c2, g))
     pieces = call(
         z_join,
         0.8,
@@ -764,7 +778,16 @@
         index=index,
         shelves=[["y2ut"], ["y34pt"]],
     )
+    g, m1, m2, m3 = lax.optimization_barrier((g, m1, m2, m3))
     m1, m2, m3 = moved(m1, 0, 1), moved(m2, 0, 2), moved(m3, 0, 3)
+    dz, dy, dc = call(
+        details_rim,
+        0.5,
+        [(5, 64, 512), (2, 40, 512), half],
+        g,
+        dz,
+        shelves=[["x1i"], ["r5i"], ["y1ut"], ["r5ut"]],
+    )
     low, pz, py, pc = call(
         deep_join,
         2.5,
@@ -776,7 +799,7 @@
         dz,
         dy,
         dc,
-        shelves=[["y34t"], ["xmi", "y2t"], ["y2qt", "y1ult", "r5ult"]],
+        shelves=[["y34t"], ["xmi", "y2t"], ["x1l", "y2qt"], ["y1ult", "r5ult"], ["r5il"]],
         scratch=[(8, 32, 256)],
     )
     pz, py, pc = moved(pz, 1, 0), moved(py, 0, 1), moved(pc, 1, 1)
@@ -785,15 +808,14 @@
     )
     (out,) = call(
         finish,
-        3.0,
+        2.0,
         [(16, 64, 512)],
         base,
         pz,
         py,
         pc,
-        shelves=[["x1i"], ["y1qt", "r5i"], ["r5z"]],
-        scratch=[(5, 64, 512)],
-        streamed="out",
+        shelves=[["y1qt", "r5z"]],
+        streamed=True,
     )
     return out
 

time: 109 us -> 109 us (level)
  waiting for transfers between devices: 35.8 us -> 32.4 us
  Pallas kernels: 24.1 us -> 25.3 us
  starting transfers between devices: 46.6 us -> 47.8 us
    pallas_call x0 -> x1, Pallas kernels: none -> 4.64 us  [x_rims(): pl.pallas_call(kernel, name='x_rims', out_shape=shapes, in_specs=[far] *...]
    ppermute x18 -> x19, waiting for transfers between devices: 25.5 us -> 21.1 us  [moved(): return lax.ppermute(value, ('gz', 'gy'), pairs)]
    ppermute x6, starting transfers between devices: 6.25 us -> 10.6 us  [exchanged(): out.append(lax.ppermute(pieces[s], 'gz', pairs))]
    pallas_call x13, Pallas kernels: 24.1 us -> 20.7 us  [call(): pl.pallas_call(body, name=kernel.__name__, out_shape=[jax.ShapeDtypeStruc...]
    ppermute x18 -> x19, starting transfers between devices: 35.6 us -> 32.2 us  [moved(): return lax.ppermute(value, ('gz', 'gy'), pairs)]
    unnamed x32 -> x42, local copies, waits for them, and re-layouts: 1.87 us -> 2.4 us
  transfers between devices with their start and end apart: 26 -> 27, of which waited for: 14 -> 12; matrix products, arithmetic and copies ran while one was open for 0% -> 0% of each run, Pallas kernels for 8% -> 11%
where the time goes in v1:
time: 109 us
  starting transfers between devices  47.8 us (44%)
  waiting for transfers between devices  32.4 us (30%)
  Pallas kernels  25.3 us (23%)
  local copies, waits for them, and re-layouts  2.4 us (2%)
    ppermute x19, starting transfers between devices, moved(): return lax.ppermute(value, ('gz', 'gy'), pairs)  32.2 us
    ppermute x19, waiting for transfers between devices, moved(): return lax.ppermute(value, ('gz', 'gy'), pairs)  21.1 us
    pallas_call x13, Pallas kernels, call(): pl.pallas_call(body, name=kernel.__name__, out_shape=[jax.ShapeDtypeStruc...  20.7 us
    ppermute x6, starting transfers between devices, exchanged(): out.append(lax.ppermute(pieces[s], 'gz', pairs))  10.6 us
    ppermute x6, waiting for transfers between devices, exchanged(): out.append(lax.ppermute(pieces[s], 'gz', pairs))  10.3 us
    ppermute x2, starting transfers between devices, across(): return lax.ppermute(value, 'gz', [(z, z ^ flip) for z in range(GZ)])  5.01 us
    pallas_call x1, Pallas kernels, x_rims(): pl.pallas_call(kernel, name='x_rims', out_shape=shapes, in_specs=[far] *...  4.64 us
    unnamed x42, local copies, waits for them, and re-layouts  2.4 us
  transfers between devices with their start and end apart: 27, of which 12 were waited for; matrix products, arithmetic and copies ran while one was open for 0% of the time, Pallas kernels for 11%

profile of v1, /device:TPU:1, one launch (start us, length us, event | category | flops | bytes accessed | tf_op | source)
XLA Modules:
  0.0 108.5 jit_solution(4885344646976610114)
XLA Ops:
  0.0 4.6 %x_rims.1 = (f32[2,40,512]{2,1,0:T(8,128)}, f32[5,32,256]{2,1,0:T(8,128)}, f32[5,32,768]{2,1,0:T(8,128)S(1)}, f32[40,512]{1,0:T(8,128)}, f32[16,64,512]{2,1,0:T(8,128)S(1)}, /*index=5*/bf16[2,1360,512]{2,1,0:T(8,128)(2,1)S(1)}) custom-call(f32[16,64,512]{2,1,0:T(8,128)} %v.1, bf16[2,960,512]{2,1,0:T(8,128)(2,1)} %constant.37.clone.small, ...), custom_call_target="tpu_custom_call" | custom-call | flops 3000000000 | bytes 10000000 | tf_op jit(solution)/shard_map/x_rims/pallas_call | solution.py:374
  5.4 1.5 %copy-done.17 = bf16[2,1360,512]{2,1,0:T(8,128)(2,1)} copy-done((bf16[2,1360,512]{2,1,0:T(8,128)(2,1)}, bf16[2,1360,512]{2,1,0:T(8,128)(2,1)S(1)}, u32[]{:S(2)}) %copy-start.17) | copy-done | bytes 2785304
  7.0 6.0 %collective-permute-start = (f32[2,40,512]{2,1,0:T(8,128)}, f32[2,40,512]{2,1,0:T(8,128)S(1)}, u32[]{:S(2)}, u32[]{:S(2)}) collective-permute-start(f32[2,40,512]{2,1,0:T(8,128)} %get-tuple-element.79), channel_id=1, source_target_pairs={{0,7},{1,0},{2,1},{3,2},{4,3},{5,4},{6,5},{7,6},{8,15},{9,8},{10,9... | collective-permute-start | bytes 491528 | tf_op jit(solution)/shard_map/ppermute | solution.py:648
  13.9 6.7 %collective-permute-start.2 = (f32[40,512]{1,0:T(8,128)}, f32[40,512]{1,0:T(8,128)S(1)}, u32[]{:S(2)}, u32[]{:S(2)}) collective-permute-start(f32[40,512]{1,0:T(8,128)} %get-tuple-element.81), channel_id=1, source_target_pairs={{0,255},{1,248},{2,249},{3,250},{4,251},{5,252},{6,253},{7,254},{8... | collective-permute-start | bytes 245768 | tf_op jit(solution)/shard_map/ppermute | solution.py:648
  20.6 1.8 %x_split.1.refs_0_ = f32[16,64,512]{2,1,0:T(8,128)S(1)} custom-call(f32[16,64,512]{2,1,0:T(8,128)S(1)} %get-tuple-element.78.refs_0_, bf16[2,512,512]{2,1,0:T(8,128)(2,1)S(1)} %copy-done.4), custom_call_target="tpu_custom_call" | custom-call | flops 550000000 | bytes 1800000 | tf_op jit(solution)/shard_map/x_split/pallas_call | solution.py:313
  22.5 2.0 %deep_split.1 = (f32[256,384]{1,0:T(8,128)S(1)}, f32[384,128]{1,0:T(8,128)S(1)}, f32[64,128]{1,0:T(8,128)S(1)}, f32[16,128]{1,0:T(8,128)S(1)}) custom-call(f32[16,64,512]{2,1,0:T(8,128)S(1)} %x_split.1.refs_0_, f32[2,40,512]{2,1,0:T(8,128)S(1)} %collective-permute-done.refs_1_, f32[5,32,256]{2,1,0:T(8,128)S(1)} %collective-permute-done.1.refs_2_, ...), custom_call_target="tpu_custom_call" | custom-call | flops 3300000000 | bytes 10800000 | tf_op jit(solution)/shard_map/deep_split/pallas_call | solution.py:313
  24.5 1.5 %collective-permute-start.4 = (f32[384,128]{1,0:T(8,128)S(1)}, f32[384,128]{1,0:T(8,128)S(1)}, u32[]{:S(2)}, u32[]{:S(2)}) collective-permute-start(f32[384,128]{1,0:T(8,128)S(1)} %get-tuple-element.90), channel_id=1, source_target_pairs={{0,7},{1,0},{2,1},{3,2},{4,3},{5,4},{6,5},{7,6},{8,15},{9,8},{10,9... | collective-permute-start | bytes 589832 | tf_op jit(solution)/shard_map/ppermute | solution.py:648
  26.2 4.9 %collective-permute-start.3 = (f32[2,176,128]{2,1,0:T(8,128)S(1)}, f32[2,176,128]{2,1,0:T(8,128)S(1)}, u32[]{:S(2)}, u32[]{:S(2)}) collective-permute-start(f32[2,176,128]{2,1,0:T(8,128)S(1)} %get-tuple-element.88), channel_id=1, source_target_pairs={{0,8},{8,0},{16,24},{24,16},{32,40},{40,32},{48,56},{56,48},{64,72... | collective-permute-start | bytes 540680 | tf_op jit(solution)/shard_map/ppermute | solution.py:652
  32.2 3.8 %collective-permute-done.6.refs_3_ = f32[16,128]{1,0:T(8,128)S(1)} collective-permute-done((f32[16,128]{1,0:T(8,128)S(1)}, f32[16,128]{1,0:T(8,128)S(1)}, u32[]{:S(2)}, u32[]{:S(2)}) %collective-permute-start.6) | collective-permute-done | bytes 8224 | tf_op jit(solution)/shard_map/ppermute | solution.py:648
  36.5 2.7 %collective-permute-start.8 = (f32[64,384]{1,0:T(8,128)S(1)}, f32[64,384]{1,0:T(8,128)S(1)}, u32[]{:S(2)}, u32[]{:S(2)}) collective-permute-start(f32[64,384]{1,0:T(8,128)S(1)} %get-tuple-element.95), channel_id=1, source_target_pairs={{0,16},{8,24},{16,0},{24,8},{32,48},{40,56},{48,32},{56,40},{64,80... | collective-permute-start | bytes 294920 | tf_op jit(solution)/shard_map/ppermute | solution.py:659
  39.2 4.5 %collective-permute-done.8.refs_2_ = f32[64,384]{1,0:T(8,128)S(1)} collective-permute-done((f32[64,384]{1,0:T(8,128)S(1)}, f32[64,384]{1,0:T(8,128)S(1)}, u32[]{:S(2)}, u32[]{:S(2)}) %collective-permute-start.8) | collective-permute-done | bytes 98336 | tf_op jit(solution)/shard_map/ppermute | solution.py:659
  45.0 3.3 %collective-permute-start.10 = (f32[208,128]{1,0:T(8,128)S(1)}, f32[208,128]{1,0:T(8,128)S(1)}, u32[]{:S(2)}, u32[]{:S(2)}) collective-permute-start(f32[208,128]{1,0:T(8,128)S(1)} %get-tuple-element.105), channel_id=1, source_target_pairs={{0,224},{1,225},{2,226},{3,227},{4,228},{5,229},{6,230},{7,231},{8... | collective-permute-start | bytes 319496 | tf_op jit(solution)/shard_map/ppermute | solution.py:648
  48.3 1.1 %collective-permute-start.11 = (f32[16,128]{1,0:T(8,128)S(1)}, f32[16,128]{1,0:T(8,128)S(1)}, u32[]{:S(2)}, u32[]{:S(2)}) collective-permute-start(f32[16,128]{1,0:T(8,128)S(1)} %get-tuple-element.106), channel_id=1, source_target_pairs={{0,192},{1,193},{2,194},{3,195},{4,196},{5,197},{6,198},{7,199},{8... | collective-permute-start | bytes 24584 | tf_op jit(solution)/shard_map/ppermute | solution.py:648
  49.9 3.9 %collective-permute-done.12.refs_4_ = f32[8,128]{1,0:T(8,128)S(1)} collective-permute-done((f32[8,128]{1,0:T(8,128)S(1)}, f32[8,128]{1,0:T(8,128)S(1)}, u32[]{:S(2)}, u32[]{:S(2)}) %collective-permute-start.12) | collective-permute-done | bytes 4128 | tf_op jit(solution)/shard_map/ppermute | solution.py:648
  54.4 2.0 %collective-permute-start.15 = (f32[208,128]{1,0:T(8,128)S(1)}, f32[208,128]{1,0:T(8,128)S(1)}, u32[]{:S(2)}, u32[]{:S(2)}) collective-permute-start(f32[208,128]{1,0:T(8,128)S(1)} %get-tuple-element.120), channel_id=1, source_target_pairs={{0,32},{1,33},{2,34},{3,35},{4,36},{5,37},{6,38},{7,39},{8,40},{9,... | collective-permute-start | bytes 319496 | tf_op jit(solution)/shard_map/ppermute | solution.py:648
  57.0 1.6 %collective-permute-start.17 = (f32[8,128]{1,0:T(8,128)S(1)}, f32[8,128]{1,0:T(8,128)S(1)}, u32[]{:S(2)}, u32[]{:S(2)}) collective-permute-start(f32[8,128]{1,0:T(8,128)S(1)} %get-tuple-element.122), channel_id=1, source_target_pairs={{0,96},{1,97},{2,98},{3,99},{4,100},{5,101},{6,102},{7,103},{8,104... | collective-permute-start | bytes 12296 | tf_op jit(solution)/shard_map/ppermute | solution.py:648
  58.6 4.6 %details.1 = (f32[16,64,512]{2,1,0:T(8,128)S(1)}, f32[5,64,512]{2,1,0:T(8,128)S(1)}) custom-call(f32[16,64,512]{2,1,0:T(8,128)S(1)} %x_split.1.refs_0_, f32[2,40,512]{2,1,0:T(8,128)S(1)} %collective-permute-done.refs_1_, f32[5,32,256]{2,1,0:T(8,128)S(1)} %collective-permute-done.1.refs_2_, f32[5,32,768]{2,1,0:T(8,128)S(1)} %collective-permute-done.14.refs_3_, ...), custom_call_target="tpu_custom_call" | custom-call | flops 550000000 | bytes 1800000 | tf_op jit(solution)/shard_map/details/pallas_call | solution.py:313
  63.9 6.1 %collective-permute-start.18 = (f32[64,384]{1,0:T(8,128)S(1)}, f32[64,384]{1,0:T(8,128)S(1)}, u32[]{:S(2)}, u32[]{:S(2)}) collective-permute-start(f32[64,384]{1,0:T(8,128)S(1)} %get-tuple-element.124), channel_id=1, source_target_pairs={{0,8},{8,16},{16,24},{24,0},{32,40},{40,48},{48,56},{56,32},{64,72... | collective-permute-start | bytes 294920 | tf_op jit(solution)/shard_map/ppermute | solution.py:659
  70.0 1.7 %collective-permute-start.19 = (f32[64,384]{1,0:T(8,128)S(1)}, f32[64,384]{1,0:T(8,128)S(1)}, u32[]{:S(2)}, u32[]{:S(2)}) collective-permute-start(f32[64,384]{1,0:T(8,128)S(1)} %get-tuple-element.125), channel_id=1, source_target_pairs={{0,16},{8,24},{16,0},{24,8},{32,48},{40,56},{48,32},{56,40},{64,80... | collective-permute-start | bytes 294920 | tf_op jit(solution)/shard_map/ppermute | solution.py:659
  72.0 4.3 %collective-permute-done.19.refs_2_ = f32[64,384]{1,0:T(8,128)S(1)} collective-permute-done((f32[64,384]{1,0:T(8,128)S(1)}, f32[64,384]{1,0:T(8,128)S(1)}, u32[]{:S(2)}, u32[]{:S(2)}) %collective-permute-start.19) | collective-permute-done | bytes 98336 | tf_op jit(solution)/shard_map/ppermute | solution.py:659
  77.2 2.4 %collective-permute-start.21 = (f32[384,128]{1,0:T(8,128)S(1)}, f32[384,128]{1,0:T(8,128)S(1)}, u32[]{:S(2)}, u32[]{:S(2)}) collective-permute-start(f32[384,128]{1,0:T(8,128)S(1)} %get-tuple-element.132), channel_id=1, source_target_pairs={{0,1},{1,2},{2,3},{3,4},{4,5},{5,6},{6,7},{7,0},{8,9},{9,10},{10,1... | collective-permute-start | bytes 589832 | tf_op jit(solution)/shard_map/ppermute | solution.py:648
  79.5 2.1 %collective-permute-start.23 = (f32[16,128]{1,0:T(8,128)S(1)}, f32[16,128]{1,0:T(8,128)S(1)}, u32[]{:S(2)}, u32[]{:S(2)}) collective-permute-start(f32[16,128]{1,0:T(8,128)S(1)} %get-tuple-element.134), channel_id=1, source_target_pairs={{0,3},{1,4},{2,5},{3,6},{4,7},{5,0},{6,1},{7,2},{8,11},{9,12},{10,... | collective-permute-start | bytes 24584 | tf_op jit(solution)/shard_map/ppermute | solution.py:648
  81.7 2.1 %details_rim.1 = (f32[5,64,512]{2,1,0:T(8,128)S(1)}, f32[2,40,512]{2,1,0:T(8,128)S(1)}, f32[40,512]{1,0:T(8,128)S(1)}) custom-call(f32[16,64,512]{2,1,0:T(8,128)S(1)} %get-tuple-element.130.refs_0_, f32[5,64,512]{2,1,0:T(8,128)S(1)} %get-tuple-element.135.refs_1_, bf16[2,928,512]{2,1,0:T(8,128)(2,1)S(1)} %copy-done.1), custom_call_target="tpu_custom_call" | custom-call | flops 550000000 | bytes 1800000 | tf_op jit(solution)/shard_map/details_rim/pallas_call | solution.py:313
  83.8 3.2 %collective-permute-done.23.refs_3_ = f32[16,128]{1,0:T(8,128)S(1)} collective-permute-done((f32[16,128]{1,0:T(8,128)S(1)}, f32[16,128]{1,0:T(8,128)S(1)}, u32[]{:S(2)}, u32[]{:S(2)}) %collective-permute-start.23) | collective-permute-done | bytes 8224 | tf_op jit(solution)/shard_map/ppermute | solution.py:648
  87.0 1.3 %collective-permute-done.22.refs_2_ = f32[64,128]{1,0:T(8,128)S(1)} collective-permute-done((f32[64,128]{1,0:T(8,128)S(1)}, f32[64,128]{1,0:T(8,128)S(1)}, u32[]{:S(2)}, u32[]{:S(2)}) %collective-permute-start.22) | collective-permute-done | bytes 32800 | tf_op jit(solution)/shard_map/ppermute | solution.py:648
  88.4 2.4 %deep_join.1 = (f32[16,32,256]{2,1,0:T(8,128)S(1)}, f32[5,64,512]{2,1,0:T(8,128)S(1)}, f32[2,40,512]{2,1,0:T(8,128)S(1)}, f32[40,512]{1,0:T(8,128)S(1)}) custom-call(f32[256,384]{1,0:T(8,128)S(1)} %get-tuple-element.131.refs_0_, f32[384,128]{1,0:T(8,128)S(1)} %collective-permute-done.21.refs_1_, f32[64,128]{1,0:T(8,128)S(1)} %collective-permute-done.22.refs_2_, ...), custom_call_target="tpu_custom_call" | custom-call | flops 2750000128 | bytes 9000000 | tf_op jit(solution)/shard_map/deep_join/pallas_call | solution.py:313
  90.9 1.4 %collective-permute-start.25 = (f32[2,40,512]{2,1,0:T(8,128)S(1)}, f32[2,40,512]{2,1,0:T(8,128)S(1)}, u32[]{:S(2)}, u32[]{:S(2)}) collective-permute-start(f32[2,40,512]{2,1,0:T(8,128)S(1)} %get-tuple-element.141), channel_id=1, source_target_pairs={{0,1},{1,2},{2,3},{3,4},{4,5},{5,6},{6,7},{7,0},{8,9},{9,10},{10,1... | collective-permute-start | bytes 491528 | tf_op jit(solution)/shard_map/ppermute | solution.py:648
  92.3 1.9 %collective-permute-start.26 = (f32[40,512]{1,0:T(8,128)S(1)}, f32[40,512]{1,0:T(8,128)S(1)}, u32[]{:S(2)}, u32[]{:S(2)}) collective-permute-start(f32[40,512]{1,0:T(8,128)S(1)} %get-tuple-element.142), channel_id=1, source_target_pairs={{0,9},{1,10},{2,11},{3,12},{4,13},{5,14},{6,15},{7,8},{8,17},{9,18... | collective-permute-start | bytes 245768 | tf_op jit(solution)/shard_map/ppermute | solution.py:648
  94.2 3.0 %own_join.1.refs_0_ = f32[16,64,512]{2,1,0:T(8,128)S(1)} custom-call(f32[16,64,512]{2,1,0:T(8,128)S(1)} %get-tuple-element.130.refs_0_, f32[16,32,256]{2,1,0:T(8,128)S(1)} %get-tuple-element.139.refs_1_, bf16[2,768,512]{2,1,0:T(8,128)(2,1)S(1)} %copy-done.3), custom_call_target="tpu_custom_call" | custom-call | flops 550000000 | bytes 1800000 | tf_op jit(solution)/shard_map/own_join/pallas_call | solution.py:313
  97.2 6.3 %collective-permute-done.26.refs_3_ = f32[40,512]{1,0:T(8,128)S(1)} collective-permute-done((f32[40,512]{1,0:T(8,128)S(1)}, f32[40,512]{1,0:T(8,128)S(1)}, u32[]{:S(2)}, u32[]{:S(2)}) %collective-permute-start.26) | collective-permute-done | bytes 81952 | tf_op jit(solution)/shard_map/ppermute | solution.py:648
  103.5 2.5 %collective-permute-done.25.refs_2_ = f32[2,40,512]{2,1,0:T(8,128)S(1)} collective-permute-done((f32[2,40,512]{2,1,0:T(8,128)S(1)}, f32[2,40,512]{2,1,0:T(8,128)S(1)}, u32[]{:S(2)}, u32[]{:S(2)}) %collective-permute-start.25) | collective-permute-done | bytes 163872 | tf_op jit(solution)/shard_map/ppermute | solution.py:648
  106.0 2.4 %finish.1 = f32[16,64,512]{2,1,0:T(8,128)} custom-call(f32[16,64,512]{2,1,0:T(8,128)S(1)} %own_join.1.refs_0_, f32[5,64,512]{2,1,0:T(8,128)S(1)} %collective-permute-done.24.refs_1_, f32[2,40,512]{2,1,0:T(8,128)S(1)} %collective-permute-done.25.refs_2_, f32[40,512]{1,0:T(8,128)S(1)} %collective-permute-done.26.refs_3_, bf16[2,512,256]{2,1,0:T(8,128)(2,1)S(1)} %copy-done.14), custom_call_target="tpu_custom_call" | custom-call | flops 2200000000 | bytes 7200000 | tf_op jit(solution)/shard_map/finish/pallas_call | solution.py:313
  (81 shorter events, 8.2 us)
Async XLA Ops:
  0.0 20.6 %copy-start.4 = (bf16[2,512,512]{2,1,0:T(8,128)(2,1)S(1)}, bf16[2,512,512]{2,1,0:T(8,128)(2,1)}, u32[]{:S(2)}) copy-start(bf16[2,512,512]{2,1,0:T(8,128)(2,1)} %constant.39.clone.refs_1_) | copy-start | bytes 3145732
  7.0 15.5 %collective-permute-start = (f32[2,40,512]{2,1,0:T(8,128)}, f32[2,40,512]{2,1,0:T(8,128)S(1)}, u32[]{:S(2)}, u32[]{:S(2)}) collective-permute-start(f32[2,40,512]{2,1,0:T(8,128)} %get-tuple-element.79), channel_id=1, source_target_pairs={{0,7},{1,0},{2,1},{3,2},{4,3},{5,4},{6,5},{7,6},{8,15},{9,8},{10,9... | collective-permute-start | bytes 491528 | tf_op jit(solution)/shard_map/ppermute | solution.py:648
  13.0 9.4 %collective-permute-start.1 = (f32[5,32,256]{2,1,0:T(8,128)}, f32[5,32,256]{2,1,0:T(8,128)S(1)}, u32[]{:S(2)}, u32[]{:S(2)}) collective-permute-start(f32[5,32,256]{2,1,0:T(8,128)} %get-tuple-element.80), channel_id=1, source_target_pairs={{0,248},{1,249},{2,250},{3,251},{4,252},{5,253},{6,254},{7,255},{8... | collective-permute-start | bytes 491528 | tf_op jit(solution)/shard_map/ppermute | solution.py:648
  13.9 8.5 %collective-permute-start.2 = (f32[40,512]{1,0:T(8,128)}, f32[40,512]{1,0:T(8,128)S(1)}, u32[]{:S(2)}, u32[]{:S(2)}) collective-permute-start(f32[40,512]{1,0:T(8,128)} %get-tuple-element.81), channel_id=1, source_target_pairs={{0,255},{1,248},{2,249},{3,250},{4,251},{5,252},{6,253},{7,254},{8... | collective-permute-start | bytes 245768 | tf_op jit(solution)/shard_map/ppermute | solution.py:648
  24.5 19.8 %copy-start.13 = (bf16[2,336,512]{2,1,0:T(8,128)(2,1)S(1)}, bf16[2,336,512]{2,1,0:T(8,128)(2,1)}, u32[]{:S(2)}) copy-start(bf16[2,336,512]{2,1,0:T(8,128)(2,1)} %constant.41.clone.refs_5_) | copy-start | bytes 2064388
  24.5 11.5 %collective-permute-start.4 = (f32[384,128]{1,0:T(8,128)S(1)}, f32[384,128]{1,0:T(8,128)S(1)}, u32[]{:S(2)}, u32[]{:S(2)}) collective-permute-start(f32[384,128]{1,0:T(8,128)S(1)} %get-tuple-element.90), channel_id=1, source_target_pairs={{0,7},{1,0},{2,1},{3,2},{4,3},{5,4},{6,5},{7,6},{8,15},{9,8},{10,9... | collective-permute-start | bytes 589832 | tf_op jit(solution)/shard_map/ppermute | solution.py:648
  26.2 6.0 %collective-permute-start.3 = (f32[2,176,128]{2,1,0:T(8,128)S(1)}, f32[2,176,128]{2,1,0:T(8,128)S(1)}, u32[]{:S(2)}, u32[]{:S(2)}) collective-permute-start(f32[2,176,128]{2,1,0:T(8,128)S(1)} %get-tuple-element.88), channel_id=1, source_target_pairs={{0,8},{8,0},{16,24},{24,16},{32,40},{40,32},{48,56},{56,48},{64,72... | collective-permute-start | bytes 540680 | tf_op jit(solution)/shard_map/ppermute | solution.py:652
  31.1 4.9 %collective-permute-start.5 = (f32[64,128]{1,0:T(8,128)S(1)}, f32[64,128]{1,0:T(8,128)S(1)}, u32[]{:S(2)}, u32[]{:S(2)}) collective-permute-start(f32[64,128]{1,0:T(8,128)S(1)} %get-tuple-element.91), channel_id=1, source_target_pairs={{0,6},{1,7},{2,0},{3,1},{4,2},{5,3},{6,4},{7,5},{8,14},{9,15},{10,... | collective-permute-start | bytes 98312 | tf_op jit(solution)/shard_map/ppermute | solution.py:648
  31.1 4.9 %collective-permute-start.6 = (f32[16,128]{1,0:T(8,128)S(1)}, f32[16,128]{1,0:T(8,128)S(1)}, u32[]{:S(2)}, u32[]{:S(2)}) collective-permute-start(f32[16,128]{1,0:T(8,128)S(1)} %get-tuple-element.92), channel_id=1, source_target_pairs={{0,5},{1,6},{2,7},{3,0},{4,1},{5,2},{6,3},{7,4},{8,13},{9,14},{10,... | collective-permute-start | bytes 24584 | tf_op jit(solution)/shard_map/ppermute | solution.py:648
  32.2 21.7 %copy-start.12 = (bf16[2,384,512]{2,1,0:T(8,128)(2,1)S(1)}, bf16[2,384,512]{2,1,0:T(8,128)(2,1)}, u32[]{:S(2)}) copy-start(bf16[2,384,512]{2,1,0:T(8,128)(2,1)} %constant.42.clone.refs_9_) | copy-start | bytes 2359300
  36.4 2.8 %collective-permute-start.7 = (f32[64,384]{1,0:T(8,128)S(1)}, f32[64,384]{1,0:T(8,128)S(1)}, u32[]{:S(2)}, u32[]{:S(2)}) collective-permute-start(f32[64,384]{1,0:T(8,128)S(1)} %get-tuple-element.94), channel_id=1, source_target_pairs={{0,8},{8,16},{16,24},{24,0},{32,40},{40,48},{48,56},{56,32},{64,72... | collective-permute-start | bytes 294920 | tf_op jit(solution)/shard_map/ppermute | solution.py:659
  36.5 7.2 %collective-permute-start.8 = (f32[64,384]{1,0:T(8,128)S(1)}, f32[64,384]{1,0:T(8,128)S(1)}, u32[]{:S(2)}, u32[]{:S(2)}) collective-permute-start(f32[64,384]{1,0:T(8,128)S(1)} %get-tuple-element.95), channel_id=1, source_target_pairs={{0,16},{8,24},{16,0},{24,8},{32,48},{40,56},{48,32},{56,40},{64,80... | collective-permute-start | bytes 294920 | tf_op jit(solution)/shard_map/ppermute | solution.py:659
  39.1 5.2 %collective-permute-start.9 = (f32[64,384]{1,0:T(8,128)S(1)}, f32[64,384]{1,0:T(8,128)S(1)}, u32[]{:S(2)}, u32[]{:S(2)}) collective-permute-start(f32[64,384]{1,0:T(8,128)S(1)} %get-tuple-element.96), channel_id=1, source_target_pairs={{0,24},{8,0},{16,8},{24,16},{32,56},{40,32},{48,40},{56,48},{64,88... | collective-permute-start | bytes 294920 | tf_op jit(solution)/shard_map/ppermute | solution.py:659
  44.8 13.8 %collective-permute-start.14 = (f32[5,32,768]{2,1,0:T(8,128)S(1)}, f32[5,32,768]{2,1,0:T(8,128)S(1)}, u32[]{:S(2)}, u32[]{:S(2)}) collective-permute-start(f32[5,32,768]{2,1,0:T(8,128)S(1)} %copy-done.6), channel_id=1, source_target_pairs={{0,248},{1,249},{2,250},{3,251},{4,252},{5,253},{6,254},{7,255},{8... | collective-permute-start | bytes 1474568 | tf_op jit(solution)/shard_map/ppermute | solution.py:648
  44.9 8.9 %collective-permute-start.13 = (f32[2,176,128]{2,1,0:T(8,128)S(1)}, f32[2,176,128]{2,1,0:T(8,128)S(1)}, u32[]{:S(2)}, u32[]{:S(2)}) collective-permute-start(f32[2,176,128]{2,1,0:T(8,128)S(1)} %pad_maximum_fusion), channel_id=1, source_target_pairs={{0,16},{8,24},{16,0},{24,8},{32,48},{40,56},{48,32},{56,40},{64,80... | collective-permute-start | bytes 540680 | tf_op jit(solution)/shard_map/ppermute | solution.py:652
  45.0 8.8 %collective-permute-start.10 = (f32[208,128]{1,0:T(8,128)S(1)}, f32[208,128]{1,0:T(8,128)S(1)}, u32[]{:S(2)}, u32[]{:S(2)}) collective-permute-start(f32[208,128]{1,0:T(8,128)S(1)} %get-tuple-element.105), channel_id=1, source_target_pairs={{0,224},{1,225},{2,226},{3,227},{4,228},{5,229},{6,230},{7,231},{8... | collective-permute-start | bytes 319496 | tf_op jit(solution)/shard_map/ppermute | solution.py:648
  48.3 5.5 %collective-permute-start.11 = (f32[16,128]{1,0:T(8,128)S(1)}, f32[16,128]{1,0:T(8,128)S(1)}, u32[]{:S(2)}, u32[]{:S(2)}) collective-permute-start(f32[16,128]{1,0:T(8,128)S(1)} %get-tuple-element.106), channel_id=1, source_target_pairs={{0,192},{1,193},{2,194},{3,195},{4,196},{5,197},{6,198},{7,199},{8... | collective-permute-start | bytes 24584 | tf_op jit(solution)/shard_map/ppermute | solution.py:648
  49.4 4.4 %collective-permute-start.12 = (f32[8,128]{1,0:T(8,128)S(1)}, f32[8,128]{1,0:T(8,128)S(1)}, u32[]{:S(2)}, u32[]{:S(2)}) collective-permute-start(f32[8,128]{1,0:T(8,128)S(1)} %get-tuple-element.107), channel_id=1, source_target_pairs={{0,160},{1,161},{2,162},{3,163},{4,164},{5,165},{6,166},{7,167},{8... | collective-permute-start | bytes 12296 | tf_op jit(solution)/shard_map/ppermute | solution.py:648
  54.4 8.9 %collective-permute-start.15 = (f32[208,128]{1,0:T(8,128)S(1)}, f32[208,128]{1,0:T(8,128)S(1)}, u32[]{:S(2)}, u32[]{:S(2)}) collective-permute-start(f32[208,128]{1,0:T(8,128)S(1)} %get-tuple-element.120), channel_id=1, source_target_pairs={{0,32},{1,33},{2,34},{3,35},{4,36},{5,37},{6,38},{7,39},{8,40},{9,... | collective-permute-start | bytes 319496 | tf_op jit(solution)/shard_map/ppermute | solution.py:648
  56.4 6.9 %collective-permute-start.16 = (f32[16,128]{1,0:T(8,128)S(1)}, f32[16,128]{1,0:T(8,128)S(1)}, u32[]{:S(2)}, u32[]{:S(2)}) collective-permute-start(f32[16,128]{1,0:T(8,128)S(1)} %get-tuple-element.121), channel_id=1, source_target_pairs={{0,64},{1,65},{2,66},{3,67},{4,68},{5,69},{6,70},{7,71},{8,72},{9,... | collective-permute-start | bytes 24584 | tf_op jit(solution)/shard_map/ppermute | solution.py:648
  57.0 6.3 %collective-permute-start.17 = (f32[8,128]{1,0:T(8,128)S(1)}, f32[8,128]{1,0:T(8,128)S(1)}, u32[]{:S(2)}, u32[]{:S(2)}) collective-permute-start(f32[8,128]{1,0:T(8,128)S(1)} %get-tuple-element.122), channel_id=1, source_target_pairs={{0,96},{1,97},{2,98},{3,99},{4,100},{5,101},{6,102},{7,103},{8,104... | collective-permute-start | bytes 12296 | tf_op jit(solution)/shard_map/ppermute | solution.py:648
  58.6 29.7 %slice-start = ((s8[4218880]{0:T(1024)(128)(4,1)}), s8[24576]{0:T(1024)(128)(4,1)S(1)}, s32[]{:S(2)}) async-start(s8[4218880]{0:T(1024)(128)(4,1)} %bitcast.3), calls=%async_computation | async-start | bytes 49152
  63.4 25.0 %slice-start.1 = ((s8[4218880]{0:T(1024)(128)(4,1)}), s8[4194304]{0:T(1024)(128)(4,1)S(1)}, s32[]{:S(2)}) async-start(s8[4218880]{0:T(1024)(128)(4,1)} %bitcast.3), calls=%async_computation.1 | async-start | bytes 8388608
  63.9 8.1 %collective-permute-start.18 = (f32[64,384]{1,0:T(8,128)S(1)}, f32[64,384]{1,0:T(8,128)S(1)}, u32[]{:S(2)}, u32[]{:S(2)}) collective-permute-start(f32[64,384]{1,0:T(8,128)S(1)} %get-tuple-element.124), channel_id=1, source_target_pairs={{0,8},{8,16},{16,24},{24,0},{32,40},{40,48},{48,56},{56,32},{64,72... | collective-permute-start | bytes 294920 | tf_op jit(solution)/shard_map/ppermute | solution.py:659
  70.0 6.3 %collective-permute-start.19 = (f32[64,384]{1,0:T(8,128)S(1)}, f32[64,384]{1,0:T(8,128)S(1)}, u32[]{:S(2)}, u32[]{:S(2)}) collective-permute-start(f32[64,384]{1,0:T(8,128)S(1)} %get-tuple-element.125), channel_id=1, source_target_pairs={{0,16},{8,24},{16,0},{24,8},{32,48},{40,56},{48,32},{56,40},{64,80... | collective-permute-start | bytes 294920 | tf_op jit(solution)/shard_map/ppermute | solution.py:659
  71.7 5.2 %collective-permute-start.20 = (f32[64,384]{1,0:T(8,128)S(1)}, f32[64,384]{1,0:T(8,128)S(1)}, u32[]{:S(2)}, u32[]{:S(2)}) collective-permute-start(f32[64,384]{1,0:T(8,128)S(1)} %get-tuple-element.126), channel_id=1, source_target_pairs={{0,24},{8,0},{16,8},{24,16},{32,56},{40,32},{48,40},{56,48},{64,88... | collective-permute-start | bytes 294920 | tf_op jit(solution)/shard_map/ppermute | solution.py:659
  77.2 11.2 %collective-permute-start.21 = (f32[384,128]{1,0:T(8,128)S(1)}, f32[384,128]{1,0:T(8,128)S(1)}, u32[]{:S(2)}, u32[]{:S(2)}) collective-permute-start(f32[384,128]{1,0:T(8,128)S(1)} %get-tuple-element.132), channel_id=1, source_target_pairs={{0,1},{1,2},{2,3},{3,4},{4,5},{5,6},{6,7},{7,0},{8,9},{9,10},{10,1... | collective-permute-start | bytes 589832 | tf_op jit(solution)/shard_map/ppermute | solution.py:648
  79.5 8.8 %collective-permute-start.22 = (f32[64,128]{1,0:T(8,128)S(1)}, f32[64,128]{1,0:T(8,128)S(1)}, u32[]{:S(2)}, u32[]{:S(2)}) collective-permute-start(f32[64,128]{1,0:T(8,128)S(1)} %get-tuple-element.133), channel_id=1, source_target_pairs={{0,2},{1,3},{2,4},{3,5},{4,6},{5,7},{6,0},{7,1},{8,10},{9,11},{10,... | collective-permute-start | bytes 98312 | tf_op jit(solution)/shard_map/ppermute | solution.py:648
  79.5 7.5 %collective-permute-start.23 = (f32[16,128]{1,0:T(8,128)S(1)}, f32[16,128]{1,0:T(8,128)S(1)}, u32[]{:S(2)}, u32[]{:S(2)}) collective-permute-start(f32[16,128]{1,0:T(8,128)S(1)} %get-tuple-element.134), channel_id=1, source_target_pairs={{0,3},{1,4},{2,5},{3,6},{4,7},{5,0},{6,1},{7,2},{8,11},{9,12},{10,... | collective-permute-start | bytes 24584 | tf_op jit(solution)/shard_map/ppermute | solution.py:648
  90.8 15.2 %collective-permute-start.24 = (f32[5,64,512]{2,1,0:T(8,128)S(1)}, f32[5,64,512]{2,1,0:T(8,128)S(1)}, u32[]{:S(2)}, u32[]{:S(2)}) collective-permute-start(f32[5,64,512]{2,1,0:T(8,128)S(1)} %get-tuple-element.140), channel_id=1, source_target_pairs={{0,8},{1,9},{2,10},{3,11},{4,12},{5,13},{6,14},{7,15},{8,16},{9,17... | collective-permute-start | bytes 1966088 | tf_op jit(solution)/shard_map/ppermute | solution.py:648
  90.9 15.1 %collective-permute-start.25 = (f32[2,40,512]{2,1,0:T(8,128)S(1)}, f32[2,40,512]{2,1,0:T(8,128)S(1)}, u32[]{:S(2)}, u32[]{:S(2)}) collective-permute-start(f32[2,40,512]{2,1,0:T(8,128)S(1)} %get-tuple-element.141), channel_id=1, source_target_pairs={{0,1},{1,2},{2,3},{3,4},{4,5},{5,6},{6,7},{7,0},{8,9},{9,10},{10,1... | collective-permute-start | bytes 491528 | tf_op jit(solution)/shard_map/ppermute | solution.py:648
  92.3 11.2 %collective-permute-start.26 = (f32[40,512]{1,0:T(8,128)S(1)}, f32[40,512]{1,0:T(8,128)S(1)}, u32[]{:S(2)}, u32[]{:S(2)}) collective-permute-start(f32[40,512]{1,0:T(8,128)S(1)} %get-tuple-element.142), channel_id=1, source_target_pairs={{0,9},{1,10},{2,11},{3,12},{4,13},{5,14},{6,15},{7,8},{8,17},{9,18... | collective-permute-start | bytes 245768 | tf_op jit(solution)/shard_map/ppermute | solution.py:648
  (16 other events, 131.8 us)

commit v2 on v1

--- a/solution.py
+++ b/solution.py
@@ -335,21 +335,39 @@
 DEEP = [["y34"], ["xmf"], ["y2", "y1l"], ["y1ul", "r5ul", "y2q"]]
 
 
+def from_far(kernel, name, micros, outs, operands, scratch):
+    spec, far = pl.BlockSpec(memory_space=pltpu.VMEM), pl.BlockSpec(memory_space=pltpu.HBM)
+    operands = [pltpu.with_memory_space_constraint(part, pltpu.HBM) for part in operands]
+    return pl.pallas_call(
+        kernel,
+        name=name,
+        out_shape=outs,
+        in_specs=[far] * len(operands),
+        out_specs=[spec] * len(outs),
+        scratch_shapes=scratch,
+        cost_estimate=pl.CostEstimate(
+            flops=int(micros * 1.1e9), transcendentals=0, bytes_accessed=int(micros * 3.6e6)
+        ),
+        compiler_params=pltpu.CompilerParams(vmem_limit_bytes=24 * 2**20),
+    )(*operands)
+
+
+def planes_in(v, held, sems):
+    chunks = []
+    for c in range(4):
+        rows = pl.ds(4 * c, 4)
+        chunks.append(pltpu.make_async_copy(v.at[rows], held.at[rows], sems.at[c]))
+    return chunks
+
+
 def x_rims(vorticity):
     table, places = packed([["x1f"], ["r5f"], ["y1r"]])
-    deep_table, _ = packed(DEEP)
-    operands = [vorticity, jnp.asarray(table), jnp.asarray(deep_table)]
-    operands = [pltpu.with_memory_space_constraint(part, pltpu.HBM) for part in operands]
-    outs = [(2, 40, 512), (5, 32, 256), (5, 32, 768), (40, 512), (16, 64, 512)]
-
-    def kernel(v, small, large, q, qa, qb, qc, held, deep, small_held, b, sems):
-        chunks = []
-        for c in range(4):
-            rows = pl.ds(4 * c, 4)
-            chunks.append(pltpu.make_async_copy(v.at[rows], held.at[rows], sems.at[c]))
+    outs = [(2, 40, 512), (5, 32, 256), (5, 32, 768), (40, 512)]
+
+    def kernel(v, small, q, qa, qb, qc, held, small_held, b, sems):
+        chunks = planes_in(v, held, sems)
         small_copy = pltpu.make_async_copy(small, small_held, sems.at[4])
-        deep_copy = pltpu.make_async_copy(large, deep, sems.at[5])
-        for copy in chunks[:3] + [small_copy, chunks[3], deep_copy]:
+        for copy in chunks[:3] + [small_copy, chunks[3]]:
             copy.start()
         for copy in chunks[:3]:
             copy.wait()
@@ -366,31 +384,55 @@
         qa[...] = rim[:160, :256].reshape(5, 32, 256)
         qb[:, :, :256] = rim[:160, 256:].reshape(5, 32, 256)
         qb[:, :, 256:] = rim[200:360].reshape(5, 32, 512)
-        deep_copy.wait()
-
-    spec, far = pl.BlockSpec(memory_space=pltpu.VMEM), pl.BlockSpec(memory_space=pltpu.HBM)
-    shapes = [jax.ShapeDtypeStruct(shape, F32) for shape in outs]
-    shapes.append(jax.ShapeDtypeStruct(deep_table.shape, BF16))
-    return pl.pallas_call(
+
+    return from_far(
         kernel,
-        name="x_rims",
-        out_shape=shapes,
-        in_specs=[far] * 3,
-        out_specs=[spec] * 6,
-        scratch_shapes=[
+        "x_rims",
+        3.0,
+        [jax.ShapeDtypeStruct(shape, F32) for shape in outs],
+        [vorticity, jnp.asarray(table)],
+        [
+            pltpu.VMEM(vorticity.shape, F32),
             pltpu.VMEM(table.shape, BF16),
             pltpu.VMEM((5, 64, 512), F32),
+            pltpu.SemaphoreType.DMA((5,)),
+        ],
+    )
+
+
+def x_split(vorticity):
+    table, places = packed([["x1f"]])
+    deep_table, _ = packed(DEEP)
+
+    def kernel(v, small, large, f, deep, held, small_held, sems):
+        chunks = planes_in(v, held, sems)
+        small_copy = pltpu.make_async_copy(small, small_held, sems.at[4])
+        deep_copy = pltpu.make_async_copy(large, deep, sems.at[5])
+        for copy in [small_copy] + chunks + [deep_copy]:
+            copy.start()
+        small_copy.wait()
+        t = Tables(small_held, places)
+        for c in range(4):
+            chunks[c].wait()
+            part = held[4 * c : 4 * c + 4].reshape(256, 512)
+            f[4 * c : 4 * c + 4] = right(part, t("x1f")).reshape(4, 64, 512)
+        deep_copy.wait()
+
+    return from_far(
+        kernel,
+        "x_split",
+        0.5,
+        [
+            jax.ShapeDtypeStruct(vorticity.shape, F32),
+            jax.ShapeDtypeStruct(deep_table.shape, BF16),
+        ],
+        [vorticity, jnp.asarray(table), jnp.asarray(deep_table)],
+        [
+            pltpu.VMEM(vorticity.shape, F32),
+            pltpu.VMEM(table.shape, BF16),
             pltpu.SemaphoreType.DMA((6,)),
         ],
-        cost_estimate=pl.CostEstimate(flops=3 * 10**9, transcendentals=0, bytes_accessed=10**7),
-        compiler_params=pltpu.CompilerParams(vmem_limit_bytes=24 * 2**20),
-    )(*operands)
-
-
-def x_split(v, t, f):
-    for c in range(4):
-        part = v[4 * c : 4 * c + 4].reshape(256, 512)
-        f[4 * c : 4 * c + 4] = right(part, t("x1f")).reshape(4, 64, 512)
+    )
 
 
 def deep_split(f, q, qa, qc, t, own, m1, m2, m3, g, low):
@@ -540,7 +582,7 @@
     m3[...] = far[64:]
 
 
-def deep_join(w, m1, m2, m3, dz, dy, dc, t, g, pz, py, pc, low):
+def deep_join(w, m1, m2, m3, da, dy, dc, t, g, pa, py, pc, low):
     rim = jnp.concatenate([m1[256:320], m1[320:384]], axis=1)
     first = left(t("y2t"), w[:, :256]) + left(t("y2qt"), rim)
     rows = [w[:, 256:], m1[:256], m2[...], m3[...]]
@@ -552,39 +594,44 @@
     ]
     for z in range(16):
         g[z] = combine(Z1LO[:, z], [lambda i=i: low[i] for i in range(8)])
-    planes = jnp.concatenate(planes, axis=0)
-    rims = [left(t("r5il"), planes)]
+    for n in range(5):
+        pa[n] = da[n] + planes[n]
+    corner = left(t("r5ult"), jnp.concatenate(planes, axis=0))
+    pc[:, :256] = dc[:, :256] + corner
+    pc[:, 256:] = dc[:, 256:]
     for half in range(2):
         part = g[8 * half : 8 * half + 8].reshape(256, 256)
-        rims.append(left(t("y1ult"), part)[:40])
-    rims.append(left(t("r5ult"), planes))
-    rims = right(jnp.concatenate(rims, axis=0), t("x1l"))
-    pz[...] = dz[...] + rims[:320].reshape(5, 64, 512)
-    py[...] = dy[...] + rims[320:400].reshape(2, 40, 512)
-    pc[...] = dc[...] + rims[400:]
-
-
-def own_join(g, low, t, out):
+        py[half, :, :256] = dy[half, :, :256] + left(t("y1ult"), part)[:40]
+        py[half, :, 256:] = dy[half, :, 256:]
+
+
+def own_join(g, low, pb, t, out):
     for c in range(4):
         planes = []
         for z in range(4 * c, 4 * c + 4):
+            rest = [g[z, :32, 256:], g[z, 32:]]
+            if z < 10:
+                rim = combine(BASIS[:, z], [lambda n=n: pb[n] for n in range(5)])
+                rest = [rest[0] + rim[:, :256], rest[1] + rim[:, 256:]]
             corner = g[z, :32, :256] + low[z]
-            top = jnp.concatenate([corner, g[z, :32, 256:]], axis=1)
-            planes += [top, g[z, 32:]]
+            planes += [jnp.concatenate([corner, rest[0]], axis=1), rest[1]]
         part = left(t("y1i"), jnp.concatenate(planes, axis=0))
         out[4 * c : 4 * c + 4] = right(part, t("x1i")).reshape(4, 64, 512)
 
 
-def finish(base, pz, py, pc, t, out, chunks):
+def finish(base, pa, py, pc, t, out, rz, chunks):
+    x1l = [part[:256] for part in t("x1i")]
+    rz[...] = right(left(t("r5il"), pa[...].reshape(160, 256)), x1l).reshape(5, 64, 512)
     far = left(t("r5z"), pc[...])
+    rims = [taller(py[half], 8) + far[48 * half : 48 * half + 48] for half in range(2)]
+    rims = right(jnp.concatenate(rims, axis=0), t("x1i"))
     for half in range(2):
-        rim = taller(py[half], 8) + far[48 * half : 48 * half + 48]
-        extra = left(t("y1qt"), rim).reshape(8, 64, 512)
+        extra = left(t("y1qt"), rims[48 * half : 48 * half + 48]).reshape(8, 64, 512)
         for k in range(8):
             z = 8 * half + k
             plane = base[z] + extra[k]
             if z < 10:
-                plane = plane + combine(BASIS[:, z], [lambda n=n: pz[n] for n in range(5)])
+                plane = plane + combine(BASIS[:, z], [lambda n=n: rz[n] for n in range(5)])
             out[z] = plane
             if z % 4 == 3:
                 chunks[z // 4].start()
@@ -592,7 +639,7 @@
         copy.wait()
 
 
-def details(f, q, qa, qb, qc, keep, t, g, pz, kept):
+def details(f, q, qa, qb, qc, keep, t, g, da, db, kept):
     for half in range(2):
         extra = left(t("y1u"), taller(q[half], 8))
         for c in range(2):
@@ -621,24 +668,23 @@
                 kept[8 * bz : 8 * bz + 8, rows, cols] = part
     for n in range(5):
         plane = combine(SPREAD[:5, n], [lambda i=i: kept[i + 3] for i in range(5)])
-        pz[n] = plane + combine(SPREAD[5:, n], [lambda i=i: kept[i + 11] for i in range(5)])
+        plane = plane + combine(SPREAD[5:, n], [lambda i=i: kept[i + 11] for i in range(5)])
+        da[n] = plane[:32, :256]
+        db[n, :, :256] = plane[:32, 256:]
+        db[n, :, 256:] = plane[32:]
     for c in range(4):
         rows = slice(16 * c, 16 * c + 16)
         out = left(t("z1i"), kept[:, rows].reshape(256, 512))
         g[:, rows] = out.reshape(16, 16, 512)
 
 
-def details_rim(g, dz, t, pz, py, pc):
-    planes = dz[...].reshape(320, 512)
-    rims = [left(t("r5i"), planes)]
+def details_rim(g, da, db, t, py, pc):
+    top = jnp.concatenate([da[...], db[:, :, :256]], axis=2)
+    planes = jnp.concatenate([top, db[:, :, 256:]], axis=1)
+    pc[...] = left(t("r5ut"), planes.reshape(320, 512))
     for half in range(2):
         part = g[8 * half : 8 * half + 8].reshape(512, 512)
-        rims.append(left(t("y1ut"), part)[:40])
-    rims.append(left(t("r5ut"), planes))
-    rims = right(jnp.concatenate(rims, axis=0), t("x1i"))
-    pz[...] = rims[:320].reshape(5, 64, 512)
-    py[...] = rims[320:400].reshape(2, 40, 512)
-    pc[...] = rims[400:]
+        py[half] = left(t("y1ut"), part)[:40]
 
 
 def moved(value, by_z, by_y):
@@ -664,10 +710,11 @@
     index = lax.rem(lax.axis_index("gz"), MEMBERS).astype(jnp.int32).reshape(1)
     piece, half = (64, 384), (40, 512)
 
-    q, qa, qb, qc, held, deep = x_rims(vorticity)
-    held, q, qa, qc = lax.optimization_barrier((held, q, qa, qc))
+    q, qa, qb, qc = x_rims(vorticity)
+    vorticity, q, qa, qb, qc = lax.optimization_barrier((vorticity, q, qa, qb, qc))
     q, qa, qc = moved(q, 0, -1), moved(qa, -1, 0), moved(qc, -1, -1)
-    (f,) = call(x_split, 0.5, [(16, 64, 512)], held, shelves=[["x1f"]])
+    qb = moved(qb, -1, 0)
+    f, deep = x_split(vorticity)
     own, m1, m2, m3 = call(
         deep_split,
         3.0,
@@ -680,8 +727,21 @@
         table=deep,
         scratch=[(16, 32, 256), (8, 32, 256)],
     )
-    late, m1, m2, m3 = lax.optimization_barrier((index, m1, m2, m3))
+    f, late, m1, m2, m3 = lax.optimization_barrier((f, index, m1, m2, m3))
     m1, m2, m3 = moved(m1, 0, -1), moved(m2, 0, -2), moved(m3, 0, -3)
+    g, da, db = call(
+        details,
+        0.5,
+        [(16, 64, 512), (5, 32, 256), (5, 32, 768)],
+        f,
+        q,
+        qa,
+        qb,
+        qc,
+        keep_one,
+        shelves=[["y1f", "z1f", "z1i", "z1u"], ["y1u", "r5u"]],
+        scratch=[(16, 64, 512)],
+    )
     k0, k2, near = call(
         mask_pack,
         0.1,
@@ -694,7 +754,7 @@
         scratch=[(4, 176, 128)],
     )
     near = across(near, 1)
-    own, near = lax.optimization_barrier((own, near))
+    own, g, near = lax.optimization_barrier((own, g, near))
     away = jnp.stack([k2, near[1]])
 
     pieces = call(
@@ -719,10 +779,9 @@
         shelves=[["z2", "z34"], ["z2q"]],
         scratch=[(256, 384)],
     )
-    away, qb, n1, n2, n3 = lax.optimization_barrier((away, qb, n1, n2, n3))
+    away, n1, n2, n3 = lax.optimization_barrier((away, n1, n2, n3))
     n1, n2, n3 = moved(n1, -4, 0), moved(n2, -8, 0), moved(n3, -12, 0)
     away = across(away, 2)
-    qb = moved(qb, -1, 0)
 
     c2, c34, s1, s2, s3 = call(
         z_mask,
@@ -740,22 +799,12 @@
         shelves=[["z2u"], ["z34p", "z34pt", "z2ut"]],
         scratch=[(4, 176, 128), (256, 256)],
     )
-    f, s1, s2, s3 = lax.optimization_barrier((f, s1, s2, s3))
+    g, s1, s2, s3 = lax.optimization_barrier((g, s1, s2, s3))
     s1, s2, s3 = moved(s1, 4, 0), moved(s2, 8, 0), moved(s3, 12, 0)
-    g, dz = call(
-        details,
-        0.5,
-        [(16, 64, 512), (5, 64, 512)],
-        f,
-        q,
-        qa,
-        qb,
-        qc,
-        keep_one,
-        shelves=[["y1f", "z1f", "z1i", "z1u"], ["y1u", "r5u"]],
-        scratch=[(16, 64, 512)],
-    )
-    c2, g = lax.optimization_barrier((c2, g))
+    dy, dc = call(
+        details_rim, 0.3, [(2, 40, 512), half], g, da, db, shelves=[["y1ut"], ["r5ut"]]
+    )
+    c2, dy = lax.optimization_barrier((c2, dy))
     pieces = call(
         z_join,
         0.8,
@@ -778,43 +827,37 @@
         index=index,
         shelves=[["y2ut"], ["y34pt"]],
     )
-    g, m1, m2, m3 = lax.optimization_barrier((g, m1, m2, m3))
+    db, m1, m2, m3 = lax.optimization_barrier((db, m1, m2, m3))
     m1, m2, m3 = moved(m1, 0, 1), moved(m2, 0, 2), moved(m3, 0, 3)
-    dz, dy, dc = call(
-        details_rim,
-        0.5,
-        [(5, 64, 512), (2, 40, 512), half],
-        g,
-        dz,
-        shelves=[["x1i"], ["r5i"], ["y1ut"], ["r5ut"]],
-    )
-    low, pz, py, pc = call(
+    pb = moved(db, 1, 0)
+    low, pa, py, pc = call(
         deep_join,
         2.5,
-        [(16, 32, 256), (5, 64, 512), (2, 40, 512), half],
+        [(16, 32, 256), (5, 32, 256), (2, 40, 512), half],
         w,
         m1,
         m2,
         m3,
-        dz,
+        da,
         dy,
         dc,
-        shelves=[["y34t"], ["xmi", "y2t"], ["x1l", "y2qt"], ["y1ult", "r5ult"], ["r5il"]],
+        shelves=[["y34t"], ["xmi", "y2t"], ["y2qt", "y1ult", "r5ult"]],
         scratch=[(8, 32, 256)],
     )
-    pz, py, pc = moved(pz, 1, 0), moved(py, 0, 1), moved(pc, 1, 1)
+    pa, py, pc = moved(pa, 1, 0), moved(py, 0, 1), moved(pc, 1, 1)
     (base,) = call(
-        own_join, 0.5, [(16, 64, 512)], g, low, shelves=[["x1i"], ["y1i"]]
+        own_join, 0.5, [(16, 64, 512)], g, low, pb, shelves=[["x1i"], ["y1i"]]
     )
     (out,) = call(
         finish,
         2.0,
         [(16, 64, 512)],
         base,
-        pz,
+        pa,
         py,
         pc,
-        shelves=[["y1qt", "r5z"]],
+        shelves=[["x1i"], ["y1qt", "r5z"], ["r5il"]],
+        scratch=[(5, 64, 512)],
         streamed=True,
     )
     return out

time: 109 us -> 109 us (level)
  starting transfers between devices: 47.8 us -> 51 us
  local copies, waits for them, and re-layouts: 2.4 us -> 0.09 us
    ppermute x19 -> x20, starting transfers between devices: 32.2 us -> 36.6 us  [moved(): return lax.ppermute(value, ('gz', 'gy'), pairs)]
    pallas_call x1 -> x2, Pallas kernels: 4.64 us -> 7.53 us  [from_far(): pl.pallas_call(kernel, name=name, out_shape=outs, in_specs=[far] * len(op...]
    ppermute x6, starting transfers between devices: 10.6 us -> 8.16 us  [exchanged(): out.append(lax.ppermute(pieces[s], 'gz', pairs))]
    unnamed x42 -> x30, local copies, waits for them, and re-layouts: 2.4 us -> 0.09 us
    pallas_call x13 -> x12, Pallas kernels: 20.7 us -> 18.6 us  [call(): pl.pallas_call(body, name=kernel.__name__, out_shape=[jax.ShapeDtypeStruc...]
    ppermute x2, starting transfers between devices: 5.01 us -> 6.25 us  [across(): return lax.ppermute(value, 'gz', [(z, z ^ flip) for z in range(GZ)])]
    ppermute x19 -> x20, waiting for transfers between devices: 21.1 us -> 22.2 us  [moved(): return lax.ppermute(value, ('gz', 'gy'), pairs)]
  transfers between devices with their start and end apart: 27 -> 28, of which waited for: 12 -> 11; matrix products, arithmetic and copies ran while one was open for 0% -> 0% of each run, Pallas kernels for 11% -> 15%
where the time goes in v2:
time: 109 us
  starting transfers between devices  51 us (47%)
  waiting for transfers between devices  31.7 us (29%)
  Pallas kernels  26.1 us (24%)
    ppermute x20, starting transfers between devices, moved(): return lax.ppermute(value, ('gz', 'gy'), pairs)  36.6 us
    ppermute x20, waiting for transfers between devices, moved(): return lax.ppermute(value, ('gz', 'gy'), pairs)  22.2 us
    pallas_call x12, Pallas kernels, call(): pl.pallas_call(body, name=kernel.__name__, out_shape=[jax.ShapeDtypeStruc...  18.6 us
    ppermute x6, waiting for transfers between devices, exchanged(): out.append(lax.ppermute(pieces[s], 'gz', pairs))  9.48 us
    ppermute x6, starting transfers between devices, exchanged(): out.append(lax.ppermute(pieces[s], 'gz', pairs))  8.16 us
    pallas_call x2, Pallas kernels, from_far(): pl.pallas_call(kernel, name=name, out_shape=outs, in_specs=[far] * len(op...  7.53 us
    ppermute x2, starting transfers between devices, across(): return lax.ppermute(value, 'gz', [(z, z ^ flip) for z in range(GZ)])  6.25 us
  transfers between devices with their start and end apart: 28, of which 11 were waited for; matrix products, arithmetic and copies ran while one was open for 0% of the time, Pallas kernels for 15%

profile of v2, /device:TPU:1, one launch (start us, length us, event | category | flops | bytes accessed | tf_op | source)
XLA Modules:
  0.0 109.4 jit_solution(8642432823335651252)
XLA Ops:
  0.0 3.8 %x_rims.1 = (f32[2,40,512]{2,1,0:T(8,128)S(1)}, f32[5,32,256]{2,1,0:T(8,128)S(1)}, f32[5,32,768]{2,1,0:T(8,128)S(1)}, f32[40,512]{1,0:T(8,128)S(1)}) custom-call(f32[16,64,512]{2,1,0:T(8,128)} %v.2, bf16[2,960,512]{2,1,0:T(8,128)(2,1)} %constant.37.clone.small), custom_call_target="tpu_custom_call" | custom-call | flops 3300000000 | bytes 10800000 | tf_op jit(solution)/shard_map/x_rims/pallas_call | solution.py:341
  3.8 6.1 %collective-permute-start = (f32[2,40,512]{2,1,0:T(8,128)S(1)}, f32[2,40,512]{2,1,0:T(8,128)S(1)}, u32[]{:S(2)}, u32[]{:S(2)}) collective-permute-start(f32[2,40,512]{2,1,0:T(8,128)S(1)} %get-tuple-element.82), channel_id=1, source_target_pairs={{0,7},{1,0},{2,1},{3,2},{4,3},{5,4},{6,5},{7,6},{8,15},{9,8},{10,9... | collective-permute-start | bytes 491528 | tf_op jit(solution)/shard_map/ppermute | solution.py:694
  10.8 6.7 %collective-permute-start.2 = (f32[40,512]{1,0:T(8,128)S(1)}, f32[40,512]{1,0:T(8,128)S(1)}, u32[]{:S(2)}, u32[]{:S(2)}) collective-permute-start(f32[40,512]{1,0:T(8,128)S(1)} %get-tuple-element.84), channel_id=1, source_target_pairs={{0,255},{1,248},{2,249},{3,250},{4,251},{5,252},{6,253},{7,254},{8... | collective-permute-start | bytes 245768 | tf_op jit(solution)/shard_map/ppermute | solution.py:694
  17.5 3.8 %x_split.1 = (f32[16,64,512]{2,1,0:T(8,128)S(1)}, bf16[2,1360,512]{2,1,0:T(8,128)(2,1)S(1)}) custom-call(f32[16,64,512]{2,1,0:T(8,128)} %v.2, bf16[2,512,512]{2,1,0:T(8,128)(2,1)} %constant.38.clone.small, bf16[2,1360,512]{2,1,0:T(8,128)(2,1)} %constant.39.clone.large), custom_call_target="tpu_custom_call" | custom-call | flops 550000000 | bytes 1800000 | tf_op jit(solution)/shard_map/x_split/pallas_call | solution.py:341
  21.9 2.0 %deep_split.1 = (f32[256,384]{1,0:T(8,128)S(1)}, f32[384,128]{1,0:T(8,128)S(1)}, f32[64,128]{1,0:T(8,128)S(1)}, f32[16,128]{1,0:T(8,128)S(1)}) custom-call(f32[16,64,512]{2,1,0:T(8,128)S(1)} %get-tuple-element.90.refs_0_, f32[2,40,512]{2,1,0:T(8,128)S(1)} %collective-permute-done.refs_1_, f32[5,32,256]{2,1,0:T(8,128)S(1)} %collective-permute-done.1.refs_2_, ...), custom_call_target="tpu_custom_call" | custom-call | flops 3300000000 | bytes 10800000 | tf_op jit(solution)/shard_map/deep_split/pallas_call | solution.py:313
  23.9 1.8 %collective-permute-start.5 = (f32[384,128]{1,0:T(8,128)S(1)}, f32[384,128]{1,0:T(8,128)S(1)}, u32[]{:S(2)}, u32[]{:S(2)}) collective-permute-start(f32[384,128]{1,0:T(8,128)S(1)} %get-tuple-element.97), channel_id=1, source_target_pairs={{0,7},{1,0},{2,1},{3,2},{4,3},{5,4},{6,5},{7,6},{8,15},{9,8},{10,9... | collective-permute-start | bytes 589832 | tf_op jit(solution)/shard_map/ppermute | solution.py:694
  25.8 4.9 %collective-permute-start.4 = (f32[2,176,128]{2,1,0:T(8,128)S(1)}, f32[2,176,128]{2,1,0:T(8,128)S(1)}, u32[]{:S(2)}, u32[]{:S(2)}) collective-permute-start(f32[2,176,128]{2,1,0:T(8,128)S(1)} %get-tuple-element.94), channel_id=1, source_target_pairs={{0,8},{8,0},{16,24},{24,16},{32,40},{40,32},{48,56},{56,48},{64,72... | collective-permute-start | bytes 540680 | tf_op jit(solution)/shard_map/ppermute | solution.py:698
  30.7 4.6 %details.1 = (f32[16,64,512]{2,1,0:T(8,128)S(1)}, f32[5,32,256]{2,1,0:T(8,128)S(1)}, f32[5,32,768]{2,1,0:T(8,128)S(1)}) custom-call(f32[16,64,512]{2,1,0:T(8,128)S(1)} %get-tuple-element.90.refs_0_, f32[2,40,512]{2,1,0:T(8,128)S(1)} %collective-permute-done.refs_1_, f32[5,32,256]{2,1,0:T(8,128)S(1)} %collective-permute-done.1.refs_2_, ...), custom_call_target="tpu_custom_call" | custom-call | flops 550000000 | bytes 1800000 | tf_op jit(solution)/shard_map/details/pallas_call | solution.py:313
  36.0 1.6 %collective-permute-start.10 = (f32[64,384]{1,0:T(8,128)S(1)}, f32[64,384]{1,0:T(8,128)S(1)}, u32[]{:S(2)}, u32[]{:S(2)}) collective-permute-start(f32[64,384]{1,0:T(8,128)S(1)} %get-tuple-element.103), channel_id=1, source_target_pairs={{0,24},{8,0},{16,8},{24,16},{32,56},{40,32},{48,40},{56,48},{64,88... | collective-permute-start | bytes 294920 | tf_op jit(solution)/shard_map/ppermute | solution.py:705
  37.8 1.2 %collective-permute-start.9 = (f32[64,384]{1,0:T(8,128)S(1)}, f32[64,384]{1,0:T(8,128)S(1)}, u32[]{:S(2)}, u32[]{:S(2)}) collective-permute-start(f32[64,384]{1,0:T(8,128)S(1)} %get-tuple-element.102), channel_id=1, source_target_pairs={{0,16},{8,24},{16,0},{24,8},{32,48},{40,56},{48,32},{56,40},{64,80... | collective-permute-start | bytes 294920 | tf_op jit(solution)/shard_map/ppermute | solution.py:705
  39.0 1.5 %collective-permute-done.10.refs_3_ = f32[64,384]{1,0:T(8,128)S(1)} collective-permute-done((f32[64,384]{1,0:T(8,128)S(1)}, f32[64,384]{1,0:T(8,128)S(1)}, u32[]{:S(2)}, u32[]{:S(2)}) %collective-permute-start.10) | collective-permute-done | bytes 98336 | tf_op jit(solution)/shard_map/ppermute | solution.py:705
  40.6 2.8 %collective-permute-done.9.refs_2_ = f32[64,384]{1,0:T(8,128)S(1)} collective-permute-done((f32[64,384]{1,0:T(8,128)S(1)}, f32[64,384]{1,0:T(8,128)S(1)}, u32[]{:S(2)}, u32[]{:S(2)}) %collective-permute-start.9) | collective-permute-done | bytes 98336 | tf_op jit(solution)/shard_map/ppermute | solution.py:705
  43.8 1.4 %collective-permute-start.14 = (f32[2,176,128]{2,1,0:T(8,128)S(1)}, f32[2,176,128]{2,1,0:T(8,128)S(1)}, u32[]{:S(2)}, u32[]{:S(2)}) collective-permute-start(f32[2,176,128]{2,1,0:T(8,128)S(1)} %pad_maximum_fusion), channel_id=1, source_target_pairs={{0,16},{8,24},{16,0},{24,8},{32,48},{40,56},{48,32},{56,40},{64,80... | collective-permute-start | bytes 540680 | tf_op jit(solution)/shard_map/ppermute | solution.py:698
  45.2 5.6 %collective-permute-start.11 = (f32[208,128]{1,0:T(8,128)S(1)}, f32[208,128]{1,0:T(8,128)S(1)}, u32[]{:S(2)}, u32[]{:S(2)}) collective-permute-start(f32[208,128]{1,0:T(8,128)S(1)} %get-tuple-element.111), channel_id=1, source_target_pairs={{0,224},{1,225},{2,226},{3,227},{4,228},{5,229},{6,230},{7,231},{8... | collective-permute-start | bytes 319496 | tf_op jit(solution)/shard_map/ppermute | solution.py:694
  50.8 1.1 %collective-permute-start.12 = (f32[16,128]{1,0:T(8,128)S(1)}, f32[16,128]{1,0:T(8,128)S(1)}, u32[]{:S(2)}, u32[]{:S(2)}) collective-permute-start(f32[16,128]{1,0:T(8,128)S(1)} %get-tuple-element.112), channel_id=1, source_target_pairs={{0,192},{1,193},{2,194},{3,195},{4,196},{5,197},{6,198},{7,199},{8... | collective-permute-start | bytes 24584 | tf_op jit(solution)/shard_map/ppermute | solution.py:694
  52.4 3.8 %collective-permute-done.13.refs_4_ = f32[8,128]{1,0:T(8,128)S(1)} collective-permute-done((f32[8,128]{1,0:T(8,128)S(1)}, f32[8,128]{1,0:T(8,128)S(1)}, u32[]{:S(2)}, u32[]{:S(2)}) %collective-permute-start.13) | collective-permute-done | bytes 4128 | tf_op jit(solution)/shard_map/ppermute | solution.py:694
  56.8 2.0 %collective-permute-start.15 = (f32[208,128]{1,0:T(8,128)S(1)}, f32[208,128]{1,0:T(8,128)S(1)}, u32[]{:S(2)}, u32[]{:S(2)}) collective-permute-start(f32[208,128]{1,0:T(8,128)S(1)} %get-tuple-element.126), channel_id=1, source_target_pairs={{0,32},{1,33},{2,34},{3,35},{4,36},{5,37},{6,38},{7,39},{8,40},{9,... | collective-permute-start | bytes 319496 | tf_op jit(solution)/shard_map/ppermute | solution.py:694
  59.4 1.5 %collective-permute-start.17 = (f32[8,128]{1,0:T(8,128)S(1)}, f32[8,128]{1,0:T(8,128)S(1)}, u32[]{:S(2)}, u32[]{:S(2)}) collective-permute-start(f32[8,128]{1,0:T(8,128)S(1)} %get-tuple-element.128), channel_id=1, source_target_pairs={{0,96},{1,97},{2,98},{3,99},{4,100},{5,101},{6,102},{7,103},{8,104... | collective-permute-start | bytes 12296 | tf_op jit(solution)/shard_map/ppermute | solution.py:694
  61.8 3.2 %collective-permute-done.17.refs_4_ = f32[8,128]{1,0:T(8,128)S(1)} collective-permute-done((f32[8,128]{1,0:T(8,128)S(1)}, f32[8,128]{1,0:T(8,128)S(1)}, u32[]{:S(2)}, u32[]{:S(2)}) %collective-permute-start.17) | collective-permute-done | bytes 4128 | tf_op jit(solution)/shard_map/ppermute | solution.py:694
  65.6 3.9 %collective-permute-start.18 = (f32[64,384]{1,0:T(8,128)S(1)}, f32[64,384]{1,0:T(8,128)S(1)}, u32[]{:S(2)}, u32[]{:S(2)}) collective-permute-start(f32[64,384]{1,0:T(8,128)S(1)} %get-tuple-element.130), channel_id=1, source_target_pairs={{0,8},{8,16},{16,24},{24,0},{32,40},{40,48},{48,56},{56,32},{64,72... | collective-permute-start | bytes 294920 | tf_op jit(solution)/shard_map/ppermute | solution.py:705
  69.4 1.3 %collective-permute-start.19 = (f32[64,384]{1,0:T(8,128)S(1)}, f32[64,384]{1,0:T(8,128)S(1)}, u32[]{:S(2)}, u32[]{:S(2)}) collective-permute-start(f32[64,384]{1,0:T(8,128)S(1)} %get-tuple-element.131), channel_id=1, source_target_pairs={{0,16},{8,24},{16,0},{24,8},{32,48},{40,56},{48,32},{56,40},{64,80... | collective-permute-start | bytes 294920 | tf_op jit(solution)/shard_map/ppermute | solution.py:705
  71.4 3.8 %collective-permute-done.19.refs_2_ = f32[64,384]{1,0:T(8,128)S(1)} collective-permute-done((f32[64,384]{1,0:T(8,128)S(1)}, f32[64,384]{1,0:T(8,128)S(1)}, u32[]{:S(2)}, u32[]{:S(2)}) %collective-permute-start.19) | collective-permute-done | bytes 98336 | tf_op jit(solution)/shard_map/ppermute | solution.py:705
  76.2 1.3 %collective-permute-start.21 = (f32[384,128]{1,0:T(8,128)S(1)}, f32[384,128]{1,0:T(8,128)S(1)}, u32[]{:S(2)}, u32[]{:S(2)}) collective-permute-start(f32[384,128]{1,0:T(8,128)S(1)} %get-tuple-element.137), channel_id=1, source_target_pairs={{0,1},{1,2},{2,3},{3,4},{4,5},{5,6},{6,7},{7,0},{8,9},{9,10},{10,1... | collective-permute-start | bytes 589832 | tf_op jit(solution)/shard_map/ppermute | solution.py:694
  77.5 1.9 %collective-permute-start.22 = (f32[64,128]{1,0:T(8,128)S(1)}, f32[64,128]{1,0:T(8,128)S(1)}, u32[]{:S(2)}, u32[]{:S(2)}) collective-permute-start(f32[64,128]{1,0:T(8,128)S(1)} %get-tuple-element.138), channel_id=1, source_target_pairs={{0,2},{1,3},{2,4},{3,5},{4,6},{5,7},{6,0},{7,1},{8,10},{9,11},{10,... | collective-permute-start | bytes 98312 | tf_op jit(solution)/shard_map/ppermute | solution.py:694
  79.4 1.9 %collective-permute-start.23 = (f32[16,128]{1,0:T(8,128)S(1)}, f32[16,128]{1,0:T(8,128)S(1)}, u32[]{:S(2)}, u32[]{:S(2)}) collective-permute-start(f32[16,128]{1,0:T(8,128)S(1)} %get-tuple-element.139), channel_id=1, source_target_pairs={{0,3},{1,4},{2,5},{3,6},{4,7},{5,0},{6,1},{7,2},{8,11},{9,12},{10,... | collective-permute-start | bytes 24584 | tf_op jit(solution)/shard_map/ppermute | solution.py:694
  81.2 9.8 %collective-permute-done.23.refs_3_ = f32[16,128]{1,0:T(8,128)S(1)} collective-permute-done((f32[16,128]{1,0:T(8,128)S(1)}, f32[16,128]{1,0:T(8,128)S(1)}, u32[]{:S(2)}, u32[]{:S(2)}) %collective-permute-start.23) | collective-permute-done | bytes 8224 | tf_op jit(solution)/shard_map/ppermute | solution.py:694
  91.1 1.9 %deep_join.1 = (f32[16,32,256]{2,1,0:T(8,128)S(1)}, f32[5,32,256]{2,1,0:T(8,128)S(1)}, f32[2,40,512]{2,1,0:T(8,128)S(1)}, f32[40,512]{1,0:T(8,128)S(1)}) custom-call(f32[256,384]{1,0:T(8,128)S(1)} %get-tuple-element.133.refs_0_, f32[384,128]{1,0:T(8,128)S(1)} %collective-permute-done.21.refs_1_, f32[64,128]{1,0:T(8,128)S(1)} %collective-permute-done.22.refs_2_, ...), custom_call_target="tpu_custom_call" | custom-call | flops 2750000128 | bytes 9000000 | tf_op jit(solution)/shard_map/deep_join/pallas_call | solution.py:313
  93.0 1.7 %collective-permute-start.25 = (f32[5,32,256]{2,1,0:T(8,128)S(1)}, f32[5,32,256]{2,1,0:T(8,128)S(1)}, u32[]{:S(2)}, u32[]{:S(2)}) collective-permute-start(f32[5,32,256]{2,1,0:T(8,128)S(1)} %get-tuple-element.144), channel_id=1, source_target_pairs={{0,8},{1,9},{2,10},{3,11},{4,12},{5,13},{6,14},{7,15},{8,16},{9,17... | collective-permute-start | bytes 491528 | tf_op jit(solution)/shard_map/ppermute | solution.py:694
  95.1 2.6 %collective-permute-start.27 = (f32[40,512]{1,0:T(8,128)S(1)}, f32[40,512]{1,0:T(8,128)S(1)}, u32[]{:S(2)}, u32[]{:S(2)}) collective-permute-start(f32[40,512]{1,0:T(8,128)S(1)} %get-tuple-element.146), channel_id=1, source_target_pairs={{0,9},{1,10},{2,11},{3,12},{4,13},{5,14},{6,15},{7,8},{8,17},{9,18... | collective-permute-start | bytes 245768 | tf_op jit(solution)/shard_map/ppermute | solution.py:694
  97.7 3.2 %own_join.1.refs_0_ = f32[16,64,512]{2,1,0:T(8,128)S(1)} custom-call(f32[16,64,512]{2,1,0:T(8,128)S(1)} %get-tuple-element.119.refs_0_, f32[16,32,256]{2,1,0:T(8,128)S(1)} %get-tuple-element.142.refs_1_, f32[5,32,768]{2,1,0:T(8,128)S(1)} %collective-permute-done.24.refs_2_, bf16[2,768,512]{2,1,0:T(8,128)(2,1)S(1)} %copy-done.2), custom_call_target="tpu_custom_call" | custom-call | flops 550000000 | bytes 1800000 | tf_op jit(solution)/shard_map/own_join/pallas_call | solution.py:313
  100.9 4.6 %collective-permute-done.27.refs_3_ = f32[40,512]{1,0:T(8,128)S(1)} collective-permute-done((f32[40,512]{1,0:T(8,128)S(1)}, f32[40,512]{1,0:T(8,128)S(1)}, u32[]{:S(2)}, u32[]{:S(2)}) %collective-permute-start.27) | collective-permute-done | bytes 81952 | tf_op jit(solution)/shard_map/ppermute | solution.py:694
  105.5 3.7 %finish.1 = f32[16,64,512]{2,1,0:T(8,128)} custom-call(f32[16,64,512]{2,1,0:T(8,128)S(1)} %own_join.1.refs_0_, f32[5,32,256]{2,1,0:T(8,128)S(1)} %collective-permute-done.25.refs_1_, f32[2,40,512]{2,1,0:T(8,128)S(1)} %collective-permute-done.26.refs_2_, f32[40,512]{1,0:T(8,128)S(1)} %collective-permute-done.27.refs_3_, bf16[2,1344,512]{2,1,0:T(8,128)(2,1)S(1)} %copy-done.9), custom_call_target="tpu_custom_call" | custom-call | flops 2200000000 | bytes 7200000 | tf_op jit(solution)/shard_map/finish/pallas_call | solution.py:313
  (70 shorter events, 8.2 us)
Async XLA Ops:
  3.8 18.0 %collective-permute-start = (f32[2,40,512]{2,1,0:T(8,128)S(1)}, f32[2,40,512]{2,1,0:T(8,128)S(1)}, u32[]{:S(2)}, u32[]{:S(2)}) collective-permute-start(f32[2,40,512]{2,1,0:T(8,128)S(1)} %get-tuple-element.82), channel_id=1, source_target_pairs={{0,7},{1,0},{2,1},{3,2},{4,3},{5,4},{6,5},{7,6},{8,15},{9,8},{10,9... | collective-permute-start | bytes 491528 | tf_op jit(solution)/shard_map/ppermute | solution.py:694
  9.9 11.9 %collective-permute-start.1 = (f32[5,32,256]{2,1,0:T(8,128)S(1)}, f32[5,32,256]{2,1,0:T(8,128)S(1)}, u32[]{:S(2)}, u32[]{:S(2)}) collective-permute-start(f32[5,32,256]{2,1,0:T(8,128)S(1)} %get-tuple-element.83), channel_id=1, source_target_pairs={{0,248},{1,249},{2,250},{3,251},{4,252},{5,253},{6,254},{7,255},{8... | collective-permute-start | bytes 491528 | tf_op jit(solution)/shard_map/ppermute | solution.py:694
  10.8 11.0 %collective-permute-start.2 = (f32[40,512]{1,0:T(8,128)S(1)}, f32[40,512]{1,0:T(8,128)S(1)}, u32[]{:S(2)}, u32[]{:S(2)}) collective-permute-start(f32[40,512]{1,0:T(8,128)S(1)} %get-tuple-element.84), channel_id=1, source_target_pairs={{0,255},{1,248},{2,249},{3,250},{4,251},{5,252},{6,253},{7,254},{8... | collective-permute-start | bytes 245768 | tf_op jit(solution)/shard_map/ppermute | solution.py:694
  17.5 13.2 %collective-permute-start.3 = (f32[5,32,768]{2,1,0:T(8,128)S(1)}, f32[5,32,768]{2,1,0:T(8,128)S(1)}, u32[]{:S(2)}, u32[]{:S(2)}) collective-permute-start(f32[5,32,768]{2,1,0:T(8,128)S(1)} %get-tuple-element.91), channel_id=1, source_target_pairs={{0,248},{1,249},{2,250},{3,251},{4,252},{5,253},{6,254},{7,255},{8... | collective-permute-start | bytes 1474568 | tf_op jit(solution)/shard_map/ppermute | solution.py:694
  23.9 11.7 %collective-permute-start.5 = (f32[384,128]{1,0:T(8,128)S(1)}, f32[384,128]{1,0:T(8,128)S(1)}, u32[]{:S(2)}, u32[]{:S(2)}) collective-permute-start(f32[384,128]{1,0:T(8,128)S(1)} %get-tuple-element.97), channel_id=1, source_target_pairs={{0,7},{1,0},{2,1},{3,2},{4,3},{5,4},{6,5},{7,6},{8,15},{9,8},{10,9... | collective-permute-start | bytes 589832 | tf_op jit(solution)/shard_map/ppermute | solution.py:694
  25.8 9.6 %collective-permute-start.4 = (f32[2,176,128]{2,1,0:T(8,128)S(1)}, f32[2,176,128]{2,1,0:T(8,128)S(1)}, u32[]{:S(2)}, u32[]{:S(2)}) collective-permute-start(f32[2,176,128]{2,1,0:T(8,128)S(1)} %get-tuple-element.94), channel_id=1, source_target_pairs={{0,8},{8,0},{16,24},{24,16},{32,40},{40,32},{48,56},{56,48},{64,72... | collective-permute-start | bytes 540680 | tf_op jit(solution)/shard_map/ppermute | solution.py:698
  30.7 4.9 %collective-permute-start.6 = (f32[64,128]{1,0:T(8,128)S(1)}, f32[64,128]{1,0:T(8,128)S(1)}, u32[]{:S(2)}, u32[]{:S(2)}) collective-permute-start(f32[64,128]{1,0:T(8,128)S(1)} %get-tuple-element.98), channel_id=1, source_target_pairs={{0,6},{1,7},{2,0},{3,1},{4,2},{5,3},{6,4},{7,5},{8,14},{9,15},{10,... | collective-permute-start | bytes 98312 | tf_op jit(solution)/shard_map/ppermute | solution.py:694
  30.7 4.9 %collective-permute-start.7 = (f32[16,128]{1,0:T(8,128)S(1)}, f32[16,128]{1,0:T(8,128)S(1)}, u32[]{:S(2)}, u32[]{:S(2)}) collective-permute-start(f32[16,128]{1,0:T(8,128)S(1)} %get-tuple-element.99), channel_id=1, source_target_pairs={{0,5},{1,6},{2,7},{3,0},{4,1},{5,2},{6,3},{7,4},{8,13},{9,14},{10,... | collective-permute-start | bytes 24584 | tf_op jit(solution)/shard_map/ppermute | solution.py:694
  35.4 20.7 %copy-start.11 = (bf16[2,384,512]{2,1,0:T(8,128)(2,1)S(1)}, bf16[2,384,512]{2,1,0:T(8,128)(2,1)}, u32[]{:S(2)}) copy-start(bf16[2,384,512]{2,1,0:T(8,128)(2,1)} %constant.43.clone.refs_9_) | copy-start | bytes 2359300
  36.0 4.6 %collective-permute-start.10 = (f32[64,384]{1,0:T(8,128)S(1)}, f32[64,384]{1,0:T(8,128)S(1)}, u32[]{:S(2)}, u32[]{:S(2)}) collective-permute-start(f32[64,384]{1,0:T(8,128)S(1)} %get-tuple-element.103), channel_id=1, source_target_pairs={{0,24},{8,0},{16,8},{24,16},{32,56},{40,32},{48,40},{56,48},{64,88... | collective-permute-start | bytes 294920 | tf_op jit(solution)/shard_map/ppermute | solution.py:705
  37.6 3.0 %collective-permute-start.8 = (f32[64,384]{1,0:T(8,128)S(1)}, f32[64,384]{1,0:T(8,128)S(1)}, u32[]{:S(2)}, u32[]{:S(2)}) collective-permute-start(f32[64,384]{1,0:T(8,128)S(1)} %get-tuple-element.101), channel_id=1, source_target_pairs={{0,8},{8,16},{16,24},{24,0},{32,40},{40,48},{48,56},{56,32},{64,72... | collective-permute-start | bytes 294920 | tf_op jit(solution)/shard_map/ppermute | solution.py:705
  37.8 5.5 %collective-permute-start.9 = (f32[64,384]{1,0:T(8,128)S(1)}, f32[64,384]{1,0:T(8,128)S(1)}, u32[]{:S(2)}, u32[]{:S(2)}) collective-permute-start(f32[64,384]{1,0:T(8,128)S(1)} %get-tuple-element.102), channel_id=1, source_target_pairs={{0,16},{8,24},{16,0},{24,8},{32,48},{40,56},{48,32},{56,40},{64,80... | collective-permute-start | bytes 294920 | tf_op jit(solution)/shard_map/ppermute | solution.py:705
  43.3 17.6 %copy-start.3 = (bf16[2,96,512]{2,1,0:T(8,128)(2,1)S(1)}, bf16[2,96,512]{2,1,0:T(8,128)(2,1)}, u32[]{:S(2)}) copy-start(bf16[2,96,512]{2,1,0:T(8,128)(2,1)} %constant.44.clone.refs_3_) | copy-start | bytes 589828
  43.8 12.3 %collective-permute-start.14 = (f32[2,176,128]{2,1,0:T(8,128)S(1)}, f32[2,176,128]{2,1,0:T(8,128)S(1)}, u32[]{:S(2)}, u32[]{:S(2)}) collective-permute-start(f32[2,176,128]{2,1,0:T(8,128)S(1)} %pad_maximum_fusion), channel_id=1, source_target_pairs={{0,16},{8,24},{16,0},{24,8},{32,48},{40,56},{48,32},{56,40},{64,80... | collective-permute-start | bytes 540680 | tf_op jit(solution)/shard_map/ppermute | solution.py:698
  45.2 11.0 %collective-permute-start.11 = (f32[208,128]{1,0:T(8,128)S(1)}, f32[208,128]{1,0:T(8,128)S(1)}, u32[]{:S(2)}, u32[]{:S(2)}) collective-permute-start(f32[208,128]{1,0:T(8,128)S(1)} %get-tuple-element.111), channel_id=1, source_target_pairs={{0,224},{1,225},{2,226},{3,227},{4,228},{5,229},{6,230},{7,231},{8... | collective-permute-start | bytes 319496 | tf_op jit(solution)/shard_map/ppermute | solution.py:694
  50.8 5.4 %collective-permute-start.12 = (f32[16,128]{1,0:T(8,128)S(1)}, f32[16,128]{1,0:T(8,128)S(1)}, u32[]{:S(2)}, u32[]{:S(2)}) collective-permute-start(f32[16,128]{1,0:T(8,128)S(1)} %get-tuple-element.112), channel_id=1, source_target_pairs={{0,192},{1,193},{2,194},{3,195},{4,196},{5,197},{6,198},{7,199},{8... | collective-permute-start | bytes 24584 | tf_op jit(solution)/shard_map/ppermute | solution.py:694
  51.9 4.3 %collective-permute-start.13 = (f32[8,128]{1,0:T(8,128)S(1)}, f32[8,128]{1,0:T(8,128)S(1)}, u32[]{:S(2)}, u32[]{:S(2)}) collective-permute-start(f32[8,128]{1,0:T(8,128)S(1)} %get-tuple-element.113), channel_id=1, source_target_pairs={{0,160},{1,161},{2,162},{3,163},{4,164},{5,165},{6,166},{7,167},{8... | collective-permute-start | bytes 12296 | tf_op jit(solution)/shard_map/ppermute | solution.py:694
  56.8 8.2 %collective-permute-start.15 = (f32[208,128]{1,0:T(8,128)S(1)}, f32[208,128]{1,0:T(8,128)S(1)}, u32[]{:S(2)}, u32[]{:S(2)}) collective-permute-start(f32[208,128]{1,0:T(8,128)S(1)} %get-tuple-element.126), channel_id=1, source_target_pairs={{0,32},{1,33},{2,34},{3,35},{4,36},{5,37},{6,38},{7,39},{8,40},{9,... | collective-permute-start | bytes 319496 | tf_op jit(solution)/shard_map/ppermute | solution.py:694
  58.8 6.2 %collective-permute-start.16 = (f32[16,128]{1,0:T(8,128)S(1)}, f32[16,128]{1,0:T(8,128)S(1)}, u32[]{:S(2)}, u32[]{:S(2)}) collective-permute-start(f32[16,128]{1,0:T(8,128)S(1)} %get-tuple-element.127), channel_id=1, source_target_pairs={{0,64},{1,65},{2,66},{3,67},{4,68},{5,69},{6,70},{7,71},{8,72},{9,... | collective-permute-start | bytes 24584 | tf_op jit(solution)/shard_map/ppermute | solution.py:694
  59.4 5.6 %collective-permute-start.17 = (f32[8,128]{1,0:T(8,128)S(1)}, f32[8,128]{1,0:T(8,128)S(1)}, u32[]{:S(2)}, u32[]{:S(2)}) collective-permute-start(f32[8,128]{1,0:T(8,128)S(1)} %get-tuple-element.128), channel_id=1, source_target_pairs={{0,96},{1,97},{2,98},{3,99},{4,100},{5,101},{6,102},{7,103},{8,104... | collective-permute-start | bytes 12296 | tf_op jit(solution)/shard_map/ppermute | solution.py:694
  61.8 14.1 %copy-start.14 = (bf16[2,144,256]{2,1,0:T(8,128)(2,1)S(1)}, bf16[2,144,256]{2,1,0:T(8,128)(2,1)}, u32[]{:S(2)}) copy-start(bf16[2,144,256]{2,1,0:T(8,128)(2,1)} %constant.46.clone.refs_5_) | copy-start | bytes 442372
  65.0 26.1 %copy-start.8 = (bf16[2,1280,640]{2,1,0:T(8,128)(2,1)S(1)}, bf16[2,1280,640]{2,1,0:T(8,128)(2,1)}, u32[]{:S(2)}) copy-start(bf16[2,1280,640]{2,1,0:T(8,128)(2,1)} %constant.47.clone.refs_7_) | copy-start | bytes 9830404
  65.6 5.8 %collective-permute-start.18 = (f32[64,384]{1,0:T(8,128)S(1)}, f32[64,384]{1,0:T(8,128)S(1)}, u32[]{:S(2)}, u32[]{:S(2)}) collective-permute-start(f32[64,384]{1,0:T(8,128)S(1)} %get-tuple-element.130), channel_id=1, source_target_pairs={{0,8},{8,16},{16,24},{24,0},{32,40},{40,48},{48,56},{56,32},{64,72... | collective-permute-start | bytes 294920 | tf_op jit(solution)/shard_map/ppermute | solution.py:705
  69.4 5.8 %collective-permute-start.19 = (f32[64,384]{1,0:T(8,128)S(1)}, f32[64,384]{1,0:T(8,128)S(1)}, u32[]{:S(2)}, u32[]{:S(2)}) collective-permute-start(f32[64,384]{1,0:T(8,128)S(1)} %get-tuple-element.131), channel_id=1, source_target_pairs={{0,16},{8,24},{16,0},{24,8},{32,48},{40,56},{48,32},{56,40},{64,80... | collective-permute-start | bytes 294920 | tf_op jit(solution)/shard_map/ppermute | solution.py:705
  70.7 5.2 %collective-permute-start.20 = (f32[64,384]{1,0:T(8,128)S(1)}, f32[64,384]{1,0:T(8,128)S(1)}, u32[]{:S(2)}, u32[]{:S(2)}) collective-permute-start(f32[64,384]{1,0:T(8,128)S(1)} %get-tuple-element.132), channel_id=1, source_target_pairs={{0,24},{8,0},{16,8},{24,16},{32,56},{40,32},{48,40},{56,48},{64,88... | collective-permute-start | bytes 294920 | tf_op jit(solution)/shard_map/ppermute | solution.py:705
  76.2 14.9 %collective-permute-start.21 = (f32[384,128]{1,0:T(8,128)S(1)}, f32[384,128]{1,0:T(8,128)S(1)}, u32[]{:S(2)}, u32[]{:S(2)}) collective-permute-start(f32[384,128]{1,0:T(8,128)S(1)} %get-tuple-element.137), channel_id=1, source_target_pairs={{0,1},{1,2},{2,3},{3,4},{4,5},{5,6},{6,7},{7,0},{8,9},{9,10},{10,1... | collective-permute-start | bytes 589832 | tf_op jit(solution)/shard_map/ppermute | solution.py:694
  77.4 20.3 %collective-permute-start.24 = (f32[5,32,768]{2,1,0:T(8,128)S(1)}, f32[5,32,768]{2,1,0:T(8,128)S(1)}, u32[]{:S(2)}, u32[]{:S(2)}) collective-permute-start(f32[5,32,768]{2,1,0:T(8,128)S(1)} %get-tuple-element.143.refs_2_), channel_id=1, source_target_pairs={{0,8},{1,9},{2,10},{3,11},{4,12},{5,13},{6,14},{7,15},{8,16},{9,17... | collective-permute-start | bytes 1474568 | tf_op jit(solution)/shard_map/ppermute | solution.py:694
  77.5 13.6 %collective-permute-start.22 = (f32[64,128]{1,0:T(8,128)S(1)}, f32[64,128]{1,0:T(8,128)S(1)}, u32[]{:S(2)}, u32[]{:S(2)}) collective-permute-start(f32[64,128]{1,0:T(8,128)S(1)} %get-tuple-element.138), channel_id=1, source_target_pairs={{0,2},{1,3},{2,4},{3,5},{4,6},{5,7},{6,0},{7,1},{8,10},{9,11},{10,... | collective-permute-start | bytes 98312 | tf_op jit(solution)/shard_map/ppermute | solution.py:694
  79.4 11.7 %collective-permute-start.23 = (f32[16,128]{1,0:T(8,128)S(1)}, f32[16,128]{1,0:T(8,128)S(1)}, u32[]{:S(2)}, u32[]{:S(2)}) collective-permute-start(f32[16,128]{1,0:T(8,128)S(1)} %get-tuple-element.139), channel_id=1, source_target_pairs={{0,3},{1,4},{2,5},{3,6},{4,7},{5,0},{6,1},{7,2},{8,11},{9,12},{10,... | collective-permute-start | bytes 24584 | tf_op jit(solution)/shard_map/ppermute | solution.py:694
  93.0 12.6 %collective-permute-start.25 = (f32[5,32,256]{2,1,0:T(8,128)S(1)}, f32[5,32,256]{2,1,0:T(8,128)S(1)}, u32[]{:S(2)}, u32[]{:S(2)}) collective-permute-start(f32[5,32,256]{2,1,0:T(8,128)S(1)} %get-tuple-element.144), channel_id=1, source_target_pairs={{0,8},{1,9},{2,10},{3,11},{4,12},{5,13},{6,14},{7,15},{8,16},{9,17... | collective-permute-start | bytes 491528 | tf_op jit(solution)/shard_map/ppermute | solution.py:694
  94.6 10.9 %collective-permute-start.26 = (f32[2,40,512]{2,1,0:T(8,128)S(1)}, f32[2,40,512]{2,1,0:T(8,128)S(1)}, u32[]{:S(2)}, u32[]{:S(2)}) collective-permute-start(f32[2,40,512]{2,1,0:T(8,128)S(1)} %get-tuple-element.145), channel_id=1, source_target_pairs={{0,1},{1,2},{2,3},{3,4},{4,5},{5,6},{6,7},{7,0},{8,9},{9,10},{10,1... | collective-permute-start | bytes 491528 | tf_op jit(solution)/shard_map/ppermute | solution.py:694
  95.1 10.4 %collective-permute-start.27 = (f32[40,512]{1,0:T(8,128)S(1)}, f32[40,512]{1,0:T(8,128)S(1)}, u32[]{:S(2)}, u32[]{:S(2)}) collective-permute-start(f32[40,512]{1,0:T(8,128)S(1)} %get-tuple-element.146), channel_id=1, source_target_pairs={{0,9},{1,10},{2,11},{3,12},{4,13},{5,14},{6,15},{7,8},{8,17},{9,18... | collective-permute-start | bytes 245768 | tf_op jit(solution)/shard_map/ppermute | solution.py:694
  (11 other events, 73.7 us)

commit v3 on v1

--- a/solution.py
+++ b/solution.py
@@ -335,21 +335,39 @@
 DEEP = [["y34"], ["xmf"], ["y2", "y1l"], ["y1ul", "r5ul", "y2q"]]
 
 
+def from_far(kernel, name, micros, outs, operands, scratch):
+    spec, far = pl.BlockSpec(memory_space=pltpu.VMEM), pl.BlockSpec(memory_space=pltpu.HBM)
+    operands = [pltpu.with_memory_space_constraint(part, pltpu.HBM) for part in operands]
+    return pl.pallas_call(
+        kernel,
+        name=name,
+        out_shape=outs,
+        in_specs=[far] * len(operands),
+        out_specs=[spec] * len(outs),
+        scratch_shapes=scratch,
+        cost_estimate=pl.CostEstimate(
+            flops=int(micros * 1.1e9), transcendentals=0, bytes_accessed=int(micros * 3.6e6)
+        ),
+        compiler_params=pltpu.CompilerParams(vmem_limit_bytes=24 * 2**20),
+    )(*operands)
+
+
+def planes_in(v, held, sems):
+    chunks = []
+    for c in range(4):
+        rows = pl.ds(4 * c, 4)
+        chunks.append(pltpu.make_async_copy(v.at[rows], held.at[rows], sems.at[c]))
+    return chunks
+
+
 def x_rims(vorticity):
     table, places = packed([["x1f"], ["r5f"], ["y1r"]])
-    deep_table, _ = packed(DEEP)
-    operands = [vorticity, jnp.asarray(table), jnp.asarray(deep_table)]
-    operands = [pltpu.with_memory_space_constraint(part, pltpu.HBM) for part in operands]
-    outs = [(2, 40, 512), (5, 32, 256), (5, 32, 768), (40, 512), (16, 64, 512)]
-
-    def kernel(v, small, large, q, qa, qb, qc, held, deep, small_held, b, sems):
-        chunks = []
-        for c in range(4):
-            rows = pl.ds(4 * c, 4)
-            chunks.append(pltpu.make_async_copy(v.at[rows], held.at[rows], sems.at[c]))
+    outs = [(2, 40, 512), (5, 32, 256), (5, 32, 768), (40, 512)]
+
+    def kernel(v, small, q, qa, qb, qc, held, small_held, b, sems):
+        chunks = planes_in(v, held, sems)
         small_copy = pltpu.make_async_copy(small, small_held, sems.at[4])
-        deep_copy = pltpu.make_async_copy(large, deep, sems.at[5])
-        for copy in chunks[:3] + [small_copy, chunks[3], deep_copy]:
+        for copy in chunks[:3] + [small_copy, chunks[3]]:
             copy.start()
         for copy in chunks[:3]:
             copy.wait()
@@ -366,31 +384,55 @@
         qa[...] = rim[:160, :256].reshape(5, 32, 256)
         qb[:, :, :256] = rim[:160, 256:].reshape(5, 32, 256)
         qb[:, :, 256:] = rim[200:360].reshape(5, 32, 512)
-        deep_copy.wait()
-
-    spec, far = pl.BlockSpec(memory_space=pltpu.VMEM), pl.BlockSpec(memory_space=pltpu.HBM)
-    shapes = [jax.ShapeDtypeStruct(shape, F32) for shape in outs]
-    shapes.append(jax.ShapeDtypeStruct(deep_table.shape, BF16))
-    return pl.pallas_call(
+
+    return from_far(
         kernel,
-        name="x_rims",
-        out_shape=shapes,
-        in_specs=[far] * 3,
-        out_specs=[spec] * 6,
-        scratch_shapes=[
+        "x_rims",
+        3.0,
+        [jax.ShapeDtypeStruct(shape, F32) for shape in outs],
+        [vorticity, jnp.asarray(table)],
+        [
+            pltpu.VMEM(vorticity.shape, F32),
             pltpu.VMEM(table.shape, BF16),
             pltpu.VMEM((5, 64, 512), F32),
+            pltpu.SemaphoreType.DMA((5,)),
+        ],
+    )
+
+
+def x_split(vorticity):
+    table, places = packed([["x1f"]])
+    deep_table, _ = packed(DEEP)
+
+    def kernel(v, small, large, f, deep, held, small_held, sems):
+        chunks = planes_in(v, held, sems)
+        small_copy = pltpu.make_async_copy(small, small_held, sems.at[4])
+        deep_copy = pltpu.make_async_copy(large, deep, sems.at[5])
+        for copy in [small_copy] + chunks + [deep_copy]:
+            copy.start()
+        small_copy.wait()
+        t = Tables(small_held, places)
+        for c in range(4):
+            chunks[c].wait()
+            part = held[4 * c : 4 * c + 4].reshape(256, 512)
+            f[4 * c : 4 * c + 4] = right(part, t("x1f")).reshape(4, 64, 512)
+        deep_copy.wait()
+
+    return from_far(
+        kernel,
+        "x_split",
+        0.5,
+        [
+            jax.ShapeDtypeStruct(vorticity.shape, F32),
+            jax.ShapeDtypeStruct(deep_table.shape, BF16),
+        ],
+        [vorticity, jnp.asarray(table), jnp.asarray(deep_table)],
+        [
+            pltpu.VMEM(vorticity.shape, F32),
+            pltpu.VMEM(table.shape, BF16),
             pltpu.SemaphoreType.DMA((6,)),
         ],
-        cost_estimate=pl.CostEstimate(flops=3 * 10**9, transcendentals=0, bytes_accessed=10**7),
-        compiler_params=pltpu.CompilerParams(vmem_limit_bytes=24 * 2**20),
-    )(*operands)
-
-
-def x_split(v, t, f):
-    for c in range(4):
-        part = v[4 * c : 4 * c + 4].reshape(256, 512)
-        f[4 * c : 4 * c + 4] = right(part, t("x1f")).reshape(4, 64, 512)
+    )
 
 
 def deep_split(f, q, qa, qc, t, own, m1, m2, m3, g, low):
@@ -664,10 +706,10 @@
     index = lax.rem(lax.axis_index("gz"), MEMBERS).astype(jnp.int32).reshape(1)
     piece, half = (64, 384), (40, 512)
 
-    q, qa, qb, qc, held, deep = x_rims(vorticity)
-    held, q, qa, qc = lax.optimization_barrier((held, q, qa, qc))
+    q, qa, qb, qc = x_rims(vorticity)
+    vorticity, q, qa, qc = lax.optimization_barrier((vorticity, q, qa, qc))
     q, qa, qc = moved(q, 0, -1), moved(qa, -1, 0), moved(qc, -1, -1)
-    (f,) = call(x_split, 0.5, [(16, 64, 512)], held, shelves=[["x1f"]])
+    f, deep = x_split(vorticity)
     own, m1, m2, m3 = call(
         deep_split,
         3.0,

time: 109 us -> 105 us (0.963)
  local copies, waits for them, and re-layouts: 2.4 us -> 0.1 us
  starting transfers between devices: 47.8 us -> 45.7 us
  Pallas kernels: 25.3 us -> 26.4 us
    pallas_call x1 -> x2, Pallas kernels: 4.64 us -> 7.52 us  [from_far(): pl.pallas_call(kernel, name=name, out_shape=outs, in_specs=[far] * len(op...]
    unnamed x42 -> x32, local copies, waits for them, and re-layouts: 2.4 us -> 0.09 us
    ppermute x2, starting transfers between devices: 5.01 us -> 2.84 us  [across(): return lax.ppermute(value, 'gz', [(z, z ^ flip) for z in range(GZ)])]
    pallas_call x13 -> x12, Pallas kernels: 20.7 us -> 18.9 us  [call(): pl.pallas_call(body, name=kernel.__name__, out_shape=[jax.ShapeDtypeStruc...]
  transfers between devices with their start and end apart: 27 -> 27, of which waited for: 12 -> 12; matrix products, arithmetic and copies ran while one was open for 0% -> 0% of each run, Pallas kernels for 11% -> 14%
where the time goes in v3:
time: 105 us
  starting transfers between devices  45.7 us (44%)
  waiting for transfers between devices  32.4 us (31%)
  Pallas kernels  26.4 us (25%)
    ppermute x19, starting transfers between devices, moved(): return lax.ppermute(value, ('gz', 'gy'), pairs)  32.3 us
    ppermute x19, waiting for transfers between devices, moved(): return lax.ppermute(value, ('gz', 'gy'), pairs)  21.1 us
    pallas_call x12, Pallas kernels, call(): pl.pallas_call(body, name=kernel.__name__, out_shape=[jax.ShapeDtypeStruc...  18.9 us
    ppermute x6, starting transfers between devices, exchanged(): out.append(lax.ppermute(pieces[s], 'gz', pairs))  10.6 us
    ppermute x6, waiting for transfers between devices, exchanged(): out.append(lax.ppermute(pieces[s], 'gz', pairs))  10.3 us
    pallas_call x2, Pallas kernels, from_far(): pl.pallas_call(kernel, name=name, out_shape=outs, in_specs=[far] * len(op...  7.52 us
    ppermute x2, starting transfers between devices, across(): return lax.ppermute(value, 'gz', [(z, z ^ flip) for z in range(GZ)])  2.84 us
  transfers between devices with their start and end apart: 27, of which 12 were waited for; matrix products, arithmetic and copies ran while one was open for 0% of the time, Pallas kernels for 14%

profile of v3, /device:TPU:1, one launch (start us, length us, event | category | flops | bytes accessed | tf_op | source)
XLA Modules:
  0.0 105.2 jit_solution(6917362158645219841)
XLA Ops:
  0.0 3.8 %x_rims.1 = (f32[2,40,512]{2,1,0:T(8,128)S(1)}, f32[5,32,256]{2,1,0:T(8,128)S(1)}, f32[5,32,768]{2,1,0:T(8,128)S(1)}, f32[40,512]{1,0:T(8,128)S(1)}) custom-call(f32[16,64,512]{2,1,0:T(8,128)} %v.2, bf16[2,960,512]{2,1,0:T(8,128)(2,1)} %constant.37.clone.small), custom_call_target="tpu_custom_call" | custom-call | flops 3300000000 | bytes 10800000 | tf_op jit(solution)/shard_map/x_rims/pallas_call | solution.py:341
  3.8 6.1 %collective-permute-start = (f32[2,40,512]{2,1,0:T(8,128)S(1)}, f32[2,40,512]{2,1,0:T(8,128)S(1)}, u32[]{:S(2)}, u32[]{:S(2)}) collective-permute-start(f32[2,40,512]{2,1,0:T(8,128)S(1)} %get-tuple-element.79), channel_id=1, source_target_pairs={{0,7},{1,0},{2,1},{3,2},{4,3},{5,4},{6,5},{7,6},{8,15},{9,8},{10,9... | collective-permute-start | bytes 491528 | tf_op jit(solution)/shard_map/ppermute | solution.py:690
  10.8 6.7 %collective-permute-start.2 = (f32[40,512]{1,0:T(8,128)S(1)}, f32[40,512]{1,0:T(8,128)S(1)}, u32[]{:S(2)}, u32[]{:S(2)}) collective-permute-start(f32[40,512]{1,0:T(8,128)S(1)} %get-tuple-element.81), channel_id=1, source_target_pairs={{0,255},{1,248},{2,249},{3,250},{4,251},{5,252},{6,253},{7,254},{8... | collective-permute-start | bytes 245768 | tf_op jit(solution)/shard_map/ppermute | solution.py:690
  17.5 3.8 %x_split.1 = (f32[16,64,512]{2,1,0:T(8,128)S(1)}, bf16[2,1360,512]{2,1,0:T(8,128)(2,1)S(1)}) custom-call(f32[16,64,512]{2,1,0:T(8,128)} %v.2, bf16[2,512,512]{2,1,0:T(8,128)(2,1)} %constant.38.clone.small, bf16[2,1360,512]{2,1,0:T(8,128)(2,1)} %constant.39.clone.large), custom_call_target="tpu_custom_call" | custom-call | flops 550000000 | bytes 1800000 | tf_op jit(solution)/shard_map/x_split/pallas_call | solution.py:341
  21.3 2.0 %deep_split.1 = (f32[256,384]{1,0:T(8,128)S(1)}, f32[384,128]{1,0:T(8,128)S(1)}, f32[64,128]{1,0:T(8,128)S(1)}, f32[16,128]{1,0:T(8,128)S(1)}) custom-call(f32[16,64,512]{2,1,0:T(8,128)S(1)} %get-tuple-element.114.refs_0_, f32[2,40,512]{2,1,0:T(8,128)S(1)} %collective-permute-done.refs_1_, f32[5,32,256]{2,1,0:T(8,128)S(1)} %collective-permute-done.1.refs_2_, ...), custom_call_target="tpu_custom_call" | custom-call | flops 3300000000 | bytes 10800000 | tf_op jit(solution)/shard_map/deep_split/pallas_call | solution.py:313
  23.4 1.5 %collective-permute-start.4 = (f32[384,128]{1,0:T(8,128)S(1)}, f32[384,128]{1,0:T(8,128)S(1)}, u32[]{:S(2)}, u32[]{:S(2)}) collective-permute-start(f32[384,128]{1,0:T(8,128)S(1)} %get-tuple-element.90), channel_id=1, source_target_pairs={{0,7},{1,0},{2,1},{3,2},{4,3},{5,4},{6,5},{7,6},{8,15},{9,8},{10,9... | collective-permute-start | bytes 589832 | tf_op jit(solution)/shard_map/ppermute | solution.py:690
  25.0 2.7 %collective-permute-start.3 = (f32[2,176,128]{2,1,0:T(8,128)S(1)}, f32[2,176,128]{2,1,0:T(8,128)S(1)}, u32[]{:S(2)}, u32[]{:S(2)}) collective-permute-start(f32[2,176,128]{2,1,0:T(8,128)S(1)} %get-tuple-element.88), channel_id=1, source_target_pairs={{0,8},{8,0},{16,24},{24,16},{32,40},{40,32},{48,56},{56,48},{64,72... | collective-permute-start | bytes 540680 | tf_op jit(solution)/shard_map/ppermute | solution.py:694
  27.8 1.0 collective-permute-done.3.refs_6_
  28.8 3.8 %collective-permute-done.6.refs_3_ = f32[16,128]{1,0:T(8,128)S(1)} collective-permute-done((f32[16,128]{1,0:T(8,128)S(1)}, f32[16,128]{1,0:T(8,128)S(1)}, u32[]{:S(2)}, u32[]{:S(2)}) %collective-permute-start.6) | collective-permute-done | bytes 8224 | tf_op jit(solution)/shard_map/ppermute | solution.py:690
  33.1 2.7 %collective-permute-start.8 = (f32[64,384]{1,0:T(8,128)S(1)}, f32[64,384]{1,0:T(8,128)S(1)}, u32[]{:S(2)}, u32[]{:S(2)}) collective-permute-start(f32[64,384]{1,0:T(8,128)S(1)} %get-tuple-element.95), channel_id=1, source_target_pairs={{0,16},{8,24},{16,0},{24,8},{32,48},{40,56},{48,32},{56,40},{64,80... | collective-permute-start | bytes 294920 | tf_op jit(solution)/shard_map/ppermute | solution.py:701
  35.8 4.5 %collective-permute-done.8.refs_2_ = f32[64,384]{1,0:T(8,128)S(1)} collective-permute-done((f32[64,384]{1,0:T(8,128)S(1)}, f32[64,384]{1,0:T(8,128)S(1)}, u32[]{:S(2)}, u32[]{:S(2)}) %collective-permute-start.8) | collective-permute-done | bytes 98336 | tf_op jit(solution)/shard_map/ppermute | solution.py:701
  41.6 3.3 %collective-permute-start.10 = (f32[208,128]{1,0:T(8,128)S(1)}, f32[208,128]{1,0:T(8,128)S(1)}, u32[]{:S(2)}, u32[]{:S(2)}) collective-permute-start(f32[208,128]{1,0:T(8,128)S(1)} %get-tuple-element.105), channel_id=1, source_target_pairs={{0,224},{1,225},{2,226},{3,227},{4,228},{5,229},{6,230},{7,231},{8... | collective-permute-start | bytes 319496 | tf_op jit(solution)/shard_map/ppermute | solution.py:690
  45.0 1.1 %collective-permute-start.11 = (f32[16,128]{1,0:T(8,128)S(1)}, f32[16,128]{1,0:T(8,128)S(1)}, u32[]{:S(2)}, u32[]{:S(2)}) collective-permute-start(f32[16,128]{1,0:T(8,128)S(1)} %get-tuple-element.106), channel_id=1, source_target_pairs={{0,192},{1,193},{2,194},{3,195},{4,196},{5,197},{6,198},{7,199},{8... | collective-permute-start | bytes 24584 | tf_op jit(solution)/shard_map/ppermute | solution.py:690
  46.5 3.9 %collective-permute-done.12.refs_4_ = f32[8,128]{1,0:T(8,128)S(1)} collective-permute-done((f32[8,128]{1,0:T(8,128)S(1)}, f32[8,128]{1,0:T(8,128)S(1)}, u32[]{:S(2)}, u32[]{:S(2)}) %collective-permute-start.12) | collective-permute-done | bytes 4128 | tf_op jit(solution)/shard_map/ppermute | solution.py:690
  51.1 2.0 %collective-permute-start.15 = (f32[208,128]{1,0:T(8,128)S(1)}, f32[208,128]{1,0:T(8,128)S(1)}, u32[]{:S(2)}, u32[]{:S(2)}) collective-permute-start(f32[208,128]{1,0:T(8,128)S(1)} %get-tuple-element.120), channel_id=1, source_target_pairs={{0,32},{1,33},{2,34},{3,35},{4,36},{5,37},{6,38},{7,39},{8,40},{9,... | collective-permute-start | bytes 319496 | tf_op jit(solution)/shard_map/ppermute | solution.py:690
  53.7 1.6 %collective-permute-start.17 = (f32[8,128]{1,0:T(8,128)S(1)}, f32[8,128]{1,0:T(8,128)S(1)}, u32[]{:S(2)}, u32[]{:S(2)}) collective-permute-start(f32[8,128]{1,0:T(8,128)S(1)} %get-tuple-element.122), channel_id=1, source_target_pairs={{0,96},{1,97},{2,98},{3,99},{4,100},{5,101},{6,102},{7,103},{8,104... | collective-permute-start | bytes 12296 | tf_op jit(solution)/shard_map/ppermute | solution.py:690
  55.3 4.6 %details.1 = (f32[16,64,512]{2,1,0:T(8,128)S(1)}, f32[5,64,512]{2,1,0:T(8,128)S(1)}) custom-call(f32[16,64,512]{2,1,0:T(8,128)S(1)} %get-tuple-element.114.refs_0_, f32[2,40,512]{2,1,0:T(8,128)S(1)} %collective-permute-done.refs_1_, f32[5,32,256]{2,1,0:T(8,128)S(1)} %collective-permute-done.1.refs_2_, f32[5,32,768]{2,1,0:T(8,128)S(1)} %collective-permute-done.14.refs_3_, ...), custom_call_target="tpu_custom_call" | custom-call | flops 550000000 | bytes 1800000 | tf_op jit(solution)/shard_map/details/pallas_call | solution.py:313
  60.6 6.1 %collective-permute-start.18 = (f32[64,384]{1,0:T(8,128)S(1)}, f32[64,384]{1,0:T(8,128)S(1)}, u32[]{:S(2)}, u32[]{:S(2)}) collective-permute-start(f32[64,384]{1,0:T(8,128)S(1)} %get-tuple-element.124), channel_id=1, source_target_pairs={{0,8},{8,16},{16,24},{24,0},{32,40},{40,48},{48,56},{56,32},{64,72... | collective-permute-start | bytes 294920 | tf_op jit(solution)/shard_map/ppermute | solution.py:701
  66.7 1.8 %collective-permute-start.19 = (f32[64,384]{1,0:T(8,128)S(1)}, f32[64,384]{1,0:T(8,128)S(1)}, u32[]{:S(2)}, u32[]{:S(2)}) collective-permute-start(f32[64,384]{1,0:T(8,128)S(1)} %get-tuple-element.125), channel_id=1, source_target_pairs={{0,16},{8,24},{16,0},{24,8},{32,48},{40,56},{48,32},{56,40},{64,80... | collective-permute-start | bytes 294920 | tf_op jit(solution)/shard_map/ppermute | solution.py:701
  68.6 4.3 %collective-permute-done.19.refs_2_ = f32[64,384]{1,0:T(8,128)S(1)} collective-permute-done((f32[64,384]{1,0:T(8,128)S(1)}, f32[64,384]{1,0:T(8,128)S(1)}, u32[]{:S(2)}, u32[]{:S(2)}) %collective-permute-start.19) | collective-permute-done | bytes 98336 | tf_op jit(solution)/shard_map/ppermute | solution.py:701
  73.9 2.3 %collective-permute-start.21 = (f32[384,128]{1,0:T(8,128)S(1)}, f32[384,128]{1,0:T(8,128)S(1)}, u32[]{:S(2)}, u32[]{:S(2)}) collective-permute-start(f32[384,128]{1,0:T(8,128)S(1)} %get-tuple-element.132), channel_id=1, source_target_pairs={{0,1},{1,2},{2,3},{3,4},{4,5},{5,6},{6,7},{7,0},{8,9},{9,10},{10,1... | collective-permute-start | bytes 589832 | tf_op jit(solution)/shard_map/ppermute | solution.py:690
  76.2 2.1 %collective-permute-start.23 = (f32[16,128]{1,0:T(8,128)S(1)}, f32[16,128]{1,0:T(8,128)S(1)}, u32[]{:S(2)}, u32[]{:S(2)}) collective-permute-start(f32[16,128]{1,0:T(8,128)S(1)} %get-tuple-element.134), channel_id=1, source_target_pairs={{0,3},{1,4},{2,5},{3,6},{4,7},{5,0},{6,1},{7,2},{8,11},{9,12},{10,... | collective-permute-start | bytes 24584 | tf_op jit(solution)/shard_map/ppermute | solution.py:690
  78.3 2.1 %details_rim.1 = (f32[5,64,512]{2,1,0:T(8,128)S(1)}, f32[2,40,512]{2,1,0:T(8,128)S(1)}, f32[40,512]{1,0:T(8,128)S(1)}) custom-call(f32[16,64,512]{2,1,0:T(8,128)S(1)} %get-tuple-element.130.refs_0_, f32[5,64,512]{2,1,0:T(8,128)S(1)} %get-tuple-element.135.refs_1_, bf16[2,928,512]{2,1,0:T(8,128)(2,1)S(1)} %copy-done.1), custom_call_target="tpu_custom_call" | custom-call | flops 550000000 | bytes 1800000 | tf_op jit(solution)/shard_map/details_rim/pallas_call | solution.py:313
  80.5 3.2 %collective-permute-done.23.refs_3_ = f32[16,128]{1,0:T(8,128)S(1)} collective-permute-done((f32[16,128]{1,0:T(8,128)S(1)}, f32[16,128]{1,0:T(8,128)S(1)}, u32[]{:S(2)}, u32[]{:S(2)}) %collective-permute-start.23) | collective-permute-done | bytes 8224 | tf_op jit(solution)/shard_map/ppermute | solution.py:690
  83.7 1.4 %collective-permute-done.22.refs_2_ = f32[64,128]{1,0:T(8,128)S(1)} collective-permute-done((f32[64,128]{1,0:T(8,128)S(1)}, f32[64,128]{1,0:T(8,128)S(1)}, u32[]{:S(2)}, u32[]{:S(2)}) %collective-permute-start.22) | collective-permute-done | bytes 32800 | tf_op jit(solution)/shard_map/ppermute | solution.py:690
  85.0 2.4 %deep_join.1 = (f32[16,32,256]{2,1,0:T(8,128)S(1)}, f32[5,64,512]{2,1,0:T(8,128)S(1)}, f32[2,40,512]{2,1,0:T(8,128)S(1)}, f32[40,512]{1,0:T(8,128)S(1)}) custom-call(f32[256,384]{1,0:T(8,128)S(1)} %get-tuple-element.131.refs_0_, f32[384,128]{1,0:T(8,128)S(1)} %collective-permute-done.21.refs_1_, f32[64,128]{1,0:T(8,128)S(1)} %collective-permute-done.22.refs_2_, ...), custom_call_target="tpu_custom_call" | custom-call | flops 2750000128 | bytes 9000000 | tf_op jit(solution)/shard_map/deep_join/pallas_call | solution.py:313
  87.6 1.4 %collective-permute-start.25 = (f32[2,40,512]{2,1,0:T(8,128)S(1)}, f32[2,40,512]{2,1,0:T(8,128)S(1)}, u32[]{:S(2)}, u32[]{:S(2)}) collective-permute-start(f32[2,40,512]{2,1,0:T(8,128)S(1)} %get-tuple-element.141), channel_id=1, source_target_pairs={{0,1},{1,2},{2,3},{3,4},{4,5},{5,6},{6,7},{7,0},{8,9},{9,10},{10,1... | collective-permute-start | bytes 491528 | tf_op jit(solution)/shard_map/ppermute | solution.py:690
  89.0 1.9 %collective-permute-start.26 = (f32[40,512]{1,0:T(8,128)S(1)}, f32[40,512]{1,0:T(8,128)S(1)}, u32[]{:S(2)}, u32[]{:S(2)}) collective-permute-start(f32[40,512]{1,0:T(8,128)S(1)} %get-tuple-element.142), channel_id=1, source_target_pairs={{0,9},{1,10},{2,11},{3,12},{4,13},{5,14},{6,15},{7,8},{8,17},{9,18... | collective-permute-start | bytes 245768 | tf_op jit(solution)/shard_map/ppermute | solution.py:690
  90.9 3.0 %own_join.1.refs_0_ = f32[16,64,512]{2,1,0:T(8,128)S(1)} custom-call(f32[16,64,512]{2,1,0:T(8,128)S(1)} %get-tuple-element.130.refs_0_, f32[16,32,256]{2,1,0:T(8,128)S(1)} %get-tuple-element.139.refs_1_, bf16[2,768,512]{2,1,0:T(8,128)(2,1)S(1)} %copy-done.3), custom_call_target="tpu_custom_call" | custom-call | flops 550000000 | bytes 1800000 | tf_op jit(solution)/shard_map/own_join/pallas_call | solution.py:313
  93.9 6.3 %collective-permute-done.26.refs_3_ = f32[40,512]{1,0:T(8,128)S(1)} collective-permute-done((f32[40,512]{1,0:T(8,128)S(1)}, f32[40,512]{1,0:T(8,128)S(1)}, u32[]{:S(2)}, u32[]{:S(2)}) %collective-permute-start.26) | collective-permute-done | bytes 81952 | tf_op jit(solution)/shard_map/ppermute | solution.py:690
  100.2 2.5 %collective-permute-done.25.refs_2_ = f32[2,40,512]{2,1,0:T(8,128)S(1)} collective-permute-done((f32[2,40,512]{2,1,0:T(8,128)S(1)}, f32[2,40,512]{2,1,0:T(8,128)S(1)}, u32[]{:S(2)}, u32[]{:S(2)}) %collective-permute-start.25) | collective-permute-done | bytes 163872 | tf_op jit(solution)/shard_map/ppermute | solution.py:690
  102.6 2.4 %finish.1 = f32[16,64,512]{2,1,0:T(8,128)} custom-call(f32[16,64,512]{2,1,0:T(8,128)S(1)} %own_join.1.refs_0_, f32[5,64,512]{2,1,0:T(8,128)S(1)} %collective-permute-done.24.refs_1_, f32[2,40,512]{2,1,0:T(8,128)S(1)} %collective-permute-done.25.refs_2_, f32[40,512]{1,0:T(8,128)S(1)} %collective-permute-done.26.refs_3_, bf16[2,512,256]{2,1,0:T(8,128)(2,1)S(1)} %copy-done.11), custom_call_target="tpu_custom_call" | custom-call | flops 2200000000 | bytes 7200000 | tf_op jit(solution)/shard_map/finish/pallas_call | solution.py:313
  (71 shorter events, 6.3 us)
Async XLA Ops:
  3.8 17.5 %collective-permute-start = (f32[2,40,512]{2,1,0:T(8,128)S(1)}, f32[2,40,512]{2,1,0:T(8,128)S(1)}, u32[]{:S(2)}, u32[]{:S(2)}) collective-permute-start(f32[2,40,512]{2,1,0:T(8,128)S(1)} %get-tuple-element.79), channel_id=1, source_target_pairs={{0,7},{1,0},{2,1},{3,2},{4,3},{5,4},{6,5},{7,6},{8,15},{9,8},{10,9... | collective-permute-start | bytes 491528 | tf_op jit(solution)/shard_map/ppermute | solution.py:690
  9.9 11.4 %collective-permute-start.1 = (f32[5,32,256]{2,1,0:T(8,128)S(1)}, f32[5,32,256]{2,1,0:T(8,128)S(1)}, u32[]{:S(2)}, u32[]{:S(2)}) collective-permute-start(f32[5,32,256]{2,1,0:T(8,128)S(1)} %get-tuple-element.80), channel_id=1, source_target_pairs={{0,248},{1,249},{2,250},{3,251},{4,252},{5,253},{6,254},{7,255},{8... | collective-permute-start | bytes 491528 | tf_op jit(solution)/shard_map/ppermute | solution.py:690
  10.8 10.4 %collective-permute-start.2 = (f32[40,512]{1,0:T(8,128)S(1)}, f32[40,512]{1,0:T(8,128)S(1)}, u32[]{:S(2)}, u32[]{:S(2)}) collective-permute-start(f32[40,512]{1,0:T(8,128)S(1)} %get-tuple-element.81), channel_id=1, source_target_pairs={{0,255},{1,248},{2,249},{3,250},{4,251},{5,252},{6,253},{7,254},{8... | collective-permute-start | bytes 245768 | tf_op jit(solution)/shard_map/ppermute | solution.py:690
  23.4 17.6 %copy-start.10 = (bf16[2,336,512]{2,1,0:T(8,128)(2,1)S(1)}, bf16[2,336,512]{2,1,0:T(8,128)(2,1)}, u32[]{:S(2)}) copy-start(bf16[2,336,512]{2,1,0:T(8,128)(2,1)} %constant.41.clone.refs_5_) | copy-start | bytes 2064388
  23.4 9.3 %collective-permute-start.4 = (f32[384,128]{1,0:T(8,128)S(1)}, f32[384,128]{1,0:T(8,128)S(1)}, u32[]{:S(2)}, u32[]{:S(2)}) collective-permute-start(f32[384,128]{1,0:T(8,128)S(1)} %get-tuple-element.90), channel_id=1, source_target_pairs={{0,7},{1,0},{2,1},{3,2},{4,3},{5,4},{6,5},{7,6},{8,15},{9,8},{10,9... | collective-permute-start | bytes 589832 | tf_op jit(solution)/shard_map/ppermute | solution.py:690
  25.0 3.8 %collective-permute-start.3 = (f32[2,176,128]{2,1,0:T(8,128)S(1)}, f32[2,176,128]{2,1,0:T(8,128)S(1)}, u32[]{:S(2)}, u32[]{:S(2)}) collective-permute-start(f32[2,176,128]{2,1,0:T(8,128)S(1)} %get-tuple-element.88), channel_id=1, source_target_pairs={{0,8},{8,0},{16,24},{24,16},{32,40},{40,32},{48,56},{56,48},{64,72... | collective-permute-start | bytes 540680 | tf_op jit(solution)/shard_map/ppermute | solution.py:694
  27.8 4.9 %collective-permute-start.5 = (f32[64,128]{1,0:T(8,128)S(1)}, f32[64,128]{1,0:T(8,128)S(1)}, u32[]{:S(2)}, u32[]{:S(2)}) collective-permute-start(f32[64,128]{1,0:T(8,128)S(1)} %get-tuple-element.91), channel_id=1, source_target_pairs={{0,6},{1,7},{2,0},{3,1},{4,2},{5,3},{6,4},{7,5},{8,14},{9,15},{10,... | collective-permute-start | bytes 98312 | tf_op jit(solution)/shard_map/ppermute | solution.py:690
  27.8 4.9 %collective-permute-start.6 = (f32[16,128]{1,0:T(8,128)S(1)}, f32[16,128]{1,0:T(8,128)S(1)}, u32[]{:S(2)}, u32[]{:S(2)}) collective-permute-start(f32[16,128]{1,0:T(8,128)S(1)} %get-tuple-element.92), channel_id=1, source_target_pairs={{0,5},{1,6},{2,7},{3,0},{4,1},{5,2},{6,3},{7,4},{8,13},{9,14},{10,... | collective-permute-start | bytes 24584 | tf_op jit(solution)/shard_map/ppermute | solution.py:690
  28.8 21.7 %copy-start.9 = (bf16[2,384,512]{2,1,0:T(8,128)(2,1)S(1)}, bf16[2,384,512]{2,1,0:T(8,128)(2,1)}, u32[]{:S(2)}) copy-start(bf16[2,384,512]{2,1,0:T(8,128)(2,1)} %constant.42.clone.refs_9_) | copy-start | bytes 2359300
  33.0 2.8 %collective-permute-start.7 = (f32[64,384]{1,0:T(8,128)S(1)}, f32[64,384]{1,0:T(8,128)S(1)}, u32[]{:S(2)}, u32[]{:S(2)}) collective-permute-start(f32[64,384]{1,0:T(8,128)S(1)} %get-tuple-element.94), channel_id=1, source_target_pairs={{0,8},{8,16},{16,24},{24,0},{32,40},{40,48},{48,56},{56,32},{64,72... | collective-permute-start | bytes 294920 | tf_op jit(solution)/shard_map/ppermute | solution.py:701
  33.1 7.2 %collective-permute-start.8 = (f32[64,384]{1,0:T(8,128)S(1)}, f32[64,384]{1,0:T(8,128)S(1)}, u32[]{:S(2)}, u32[]{:S(2)}) collective-permute-start(f32[64,384]{1,0:T(8,128)S(1)} %get-tuple-element.95), channel_id=1, source_target_pairs={{0,16},{8,24},{16,0},{24,8},{32,48},{40,56},{48,32},{56,40},{64,80... | collective-permute-start | bytes 294920 | tf_op jit(solution)/shard_map/ppermute | solution.py:701
  35.8 5.2 %collective-permute-start.9 = (f32[64,384]{1,0:T(8,128)S(1)}, f32[64,384]{1,0:T(8,128)S(1)}, u32[]{:S(2)}, u32[]{:S(2)}) collective-permute-start(f32[64,384]{1,0:T(8,128)S(1)} %get-tuple-element.96), channel_id=1, source_target_pairs={{0,24},{8,0},{16,8},{24,16},{32,56},{40,32},{48,40},{56,48},{64,88... | collective-permute-start | bytes 294920 | tf_op jit(solution)/shard_map/ppermute | solution.py:701
  41.4 13.8 %collective-permute-start.14 = (f32[5,32,768]{2,1,0:T(8,128)S(1)}, f32[5,32,768]{2,1,0:T(8,128)S(1)}, u32[]{:S(2)}, u32[]{:S(2)}) collective-permute-start(f32[5,32,768]{2,1,0:T(8,128)S(1)} %get-tuple-element.115), channel_id=1, source_target_pairs={{0,248},{1,249},{2,250},{3,251},{4,252},{5,253},{6,254},{7,255},{8... | collective-permute-start | bytes 1474568 | tf_op jit(solution)/shard_map/ppermute | solution.py:690
  41.5 8.9 %collective-permute-start.13 = (f32[2,176,128]{2,1,0:T(8,128)S(1)}, f32[2,176,128]{2,1,0:T(8,128)S(1)}, u32[]{:S(2)}, u32[]{:S(2)}) collective-permute-start(f32[2,176,128]{2,1,0:T(8,128)S(1)} %pad_maximum_fusion), channel_id=1, source_target_pairs={{0,16},{8,24},{16,0},{24,8},{32,48},{40,56},{48,32},{56,40},{64,80... | collective-permute-start | bytes 540680 | tf_op jit(solution)/shard_map/ppermute | solution.py:694
  41.6 8.8 %collective-permute-start.10 = (f32[208,128]{1,0:T(8,128)S(1)}, f32[208,128]{1,0:T(8,128)S(1)}, u32[]{:S(2)}, u32[]{:S(2)}) collective-permute-start(f32[208,128]{1,0:T(8,128)S(1)} %get-tuple-element.105), channel_id=1, source_target_pairs={{0,224},{1,225},{2,226},{3,227},{4,228},{5,229},{6,230},{7,231},{8... | collective-permute-start | bytes 319496 | tf_op jit(solution)/shard_map/ppermute | solution.py:690
  45.0 5.5 %collective-permute-start.11 = (f32[16,128]{1,0:T(8,128)S(1)}, f32[16,128]{1,0:T(8,128)S(1)}, u32[]{:S(2)}, u32[]{:S(2)}) collective-permute-start(f32[16,128]{1,0:T(8,128)S(1)} %get-tuple-element.106), channel_id=1, source_target_pairs={{0,192},{1,193},{2,194},{3,195},{4,196},{5,197},{6,198},{7,199},{8... | collective-permute-start | bytes 24584 | tf_op jit(solution)/shard_map/ppermute | solution.py:690
  46.1 4.4 %collective-permute-start.12 = (f32[8,128]{1,0:T(8,128)S(1)}, f32[8,128]{1,0:T(8,128)S(1)}, u32[]{:S(2)}, u32[]{:S(2)}) collective-permute-start(f32[8,128]{1,0:T(8,128)S(1)} %get-tuple-element.107), channel_id=1, source_target_pairs={{0,160},{1,161},{2,162},{3,163},{4,164},{5,165},{6,166},{7,167},{8... | collective-permute-start | bytes 12296 | tf_op jit(solution)/shard_map/ppermute | solution.py:690
  51.1 8.9 %collective-permute-start.15 = (f32[208,128]{1,0:T(8,128)S(1)}, f32[208,128]{1,0:T(8,128)S(1)}, u32[]{:S(2)}, u32[]{:S(2)}) collective-permute-start(f32[208,128]{1,0:T(8,128)S(1)} %get-tuple-element.120), channel_id=1, source_target_pairs={{0,32},{1,33},{2,34},{3,35},{4,36},{5,37},{6,38},{7,39},{8,40},{9,... | collective-permute-start | bytes 319496 | tf_op jit(solution)/shard_map/ppermute | solution.py:690
  53.1 6.9 %collective-permute-start.16 = (f32[16,128]{1,0:T(8,128)S(1)}, f32[16,128]{1,0:T(8,128)S(1)}, u32[]{:S(2)}, u32[]{:S(2)}) collective-permute-start(f32[16,128]{1,0:T(8,128)S(1)} %get-tuple-element.121), channel_id=1, source_target_pairs={{0,64},{1,65},{2,66},{3,67},{4,68},{5,69},{6,70},{7,71},{8,72},{9,... | collective-permute-start | bytes 24584 | tf_op jit(solution)/shard_map/ppermute | solution.py:690
  53.7 6.3 %collective-permute-start.17 = (f32[8,128]{1,0:T(8,128)S(1)}, f32[8,128]{1,0:T(8,128)S(1)}, u32[]{:S(2)}, u32[]{:S(2)}) collective-permute-start(f32[8,128]{1,0:T(8,128)S(1)} %get-tuple-element.122), channel_id=1, source_target_pairs={{0,96},{1,97},{2,98},{3,99},{4,100},{5,101},{6,102},{7,103},{8,104... | collective-permute-start | bytes 12296 | tf_op jit(solution)/shard_map/ppermute | solution.py:690
  55.3 29.7 %slice-start = ((s8[4218880]{0:T(1024)(128)(4,1)}), s8[24576]{0:T(1024)(128)(4,1)S(1)}, s32[]{:S(2)}) async-start(s8[4218880]{0:T(1024)(128)(4,1)} %bitcast.3), calls=%async_computation | async-start | bytes 49152
  60.0 18.3 %copy-start.1 = (bf16[2,928,512]{2,1,0:T(8,128)(2,1)S(1)}, bf16[2,928,512]{2,1,0:T(8,128)(2,1)}, u32[]{:S(2)}) copy-start(bf16[2,928,512]{2,1,0:T(8,128)(2,1)} %constant.46.clone.refs_2_) | copy-start | bytes 5701636
  60.0 25.0 %slice-start.1 = ((s8[4218880]{0:T(1024)(128)(4,1)}), s8[4194304]{0:T(1024)(128)(4,1)S(1)}, s32[]{:S(2)}) async-start(s8[4218880]{0:T(1024)(128)(4,1)} %bitcast.3), calls=%async_computation.1 | async-start | bytes 8388608
  60.6 8.0 %collective-permute-start.18 = (f32[64,384]{1,0:T(8,128)S(1)}, f32[64,384]{1,0:T(8,128)S(1)}, u32[]{:S(2)}, u32[]{:S(2)}) collective-permute-start(f32[64,384]{1,0:T(8,128)S(1)} %get-tuple-element.124), channel_id=1, source_target_pairs={{0,8},{8,16},{16,24},{24,0},{32,40},{40,48},{48,56},{56,32},{64,72... | collective-permute-start | bytes 294920 | tf_op jit(solution)/shard_map/ppermute | solution.py:701
  66.7 6.3 %collective-permute-start.19 = (f32[64,384]{1,0:T(8,128)S(1)}, f32[64,384]{1,0:T(8,128)S(1)}, u32[]{:S(2)}, u32[]{:S(2)}) collective-permute-start(f32[64,384]{1,0:T(8,128)S(1)} %get-tuple-element.125), channel_id=1, source_target_pairs={{0,16},{8,24},{16,0},{24,8},{32,48},{40,56},{48,32},{56,40},{64,80... | collective-permute-start | bytes 294920 | tf_op jit(solution)/shard_map/ppermute | solution.py:701
  68.4 5.2 %collective-permute-start.20 = (f32[64,384]{1,0:T(8,128)S(1)}, f32[64,384]{1,0:T(8,128)S(1)}, u32[]{:S(2)}, u32[]{:S(2)}) collective-permute-start(f32[64,384]{1,0:T(8,128)S(1)} %get-tuple-element.126), channel_id=1, source_target_pairs={{0,24},{8,0},{16,8},{24,16},{32,56},{40,32},{48,40},{56,48},{64,88... | collective-permute-start | bytes 294920 | tf_op jit(solution)/shard_map/ppermute | solution.py:701
  73.9 11.2 %collective-permute-start.21 = (f32[384,128]{1,0:T(8,128)S(1)}, f32[384,128]{1,0:T(8,128)S(1)}, u32[]{:S(2)}, u32[]{:S(2)}) collective-permute-start(f32[384,128]{1,0:T(8,128)S(1)} %get-tuple-element.132), channel_id=1, source_target_pairs={{0,1},{1,2},{2,3},{3,4},{4,5},{5,6},{6,7},{7,0},{8,9},{9,10},{10,1... | collective-permute-start | bytes 589832 | tf_op jit(solution)/shard_map/ppermute | solution.py:690
  76.2 8.8 %collective-permute-start.22 = (f32[64,128]{1,0:T(8,128)S(1)}, f32[64,128]{1,0:T(8,128)S(1)}, u32[]{:S(2)}, u32[]{:S(2)}) collective-permute-start(f32[64,128]{1,0:T(8,128)S(1)} %get-tuple-element.133), channel_id=1, source_target_pairs={{0,2},{1,3},{2,4},{3,5},{4,6},{5,7},{6,0},{7,1},{8,10},{9,11},{10,... | collective-permute-start | bytes 98312 | tf_op jit(solution)/shard_map/ppermute | solution.py:690
  76.2 7.4 %collective-permute-start.23 = (f32[16,128]{1,0:T(8,128)S(1)}, f32[16,128]{1,0:T(8,128)S(1)}, u32[]{:S(2)}, u32[]{:S(2)}) collective-permute-start(f32[16,128]{1,0:T(8,128)S(1)} %get-tuple-element.134), channel_id=1, source_target_pairs={{0,3},{1,4},{2,5},{3,6},{4,7},{5,0},{6,1},{7,2},{8,11},{9,12},{10,... | collective-permute-start | bytes 24584 | tf_op jit(solution)/shard_map/ppermute | solution.py:690
  87.5 15.2 %collective-permute-start.24 = (f32[5,64,512]{2,1,0:T(8,128)S(1)}, f32[5,64,512]{2,1,0:T(8,128)S(1)}, u32[]{:S(2)}, u32[]{:S(2)}) collective-permute-start(f32[5,64,512]{2,1,0:T(8,128)S(1)} %get-tuple-element.140), channel_id=1, source_target_pairs={{0,8},{1,9},{2,10},{3,11},{4,12},{5,13},{6,14},{7,15},{8,16},{9,17... | collective-permute-start | bytes 1966088 | tf_op jit(solution)/shard_map/ppermute | solution.py:690
  87.6 15.1 %collective-permute-start.25 = (f32[2,40,512]{2,1,0:T(8,128)S(1)}, f32[2,40,512]{2,1,0:T(8,128)S(1)}, u32[]{:S(2)}, u32[]{:S(2)}) collective-permute-start(f32[2,40,512]{2,1,0:T(8,128)S(1)} %get-tuple-element.141), channel_id=1, source_target_pairs={{0,1},{1,2},{2,3},{3,4},{4,5},{5,6},{6,7},{7,0},{8,9},{9,10},{10,1... | collective-permute-start | bytes 491528 | tf_op jit(solution)/shard_map/ppermute | solution.py:690
  89.0 11.2 %collective-permute-start.26 = (f32[40,512]{1,0:T(8,128)S(1)}, f32[40,512]{1,0:T(8,128)S(1)}, u32[]{:S(2)}, u32[]{:S(2)}) collective-permute-start(f32[40,512]{1,0:T(8,128)S(1)} %get-tuple-element.142), channel_id=1, source_target_pairs={{0,9},{1,10},{2,11},{3,12},{4,13},{5,14},{6,15},{7,8},{8,17},{9,18... | collective-permute-start | bytes 245768 | tf_op jit(solution)/shard_map/ppermute | solution.py:690
  (11 other events, 94.5 us)
